TPU v7x, 32 devices: a whole 2x2x4 slice. The times are simulated.
32 devices in a mesh: dp: 16 (over z, x, core), chan: 2 (over y).
Axes of the slice: x: 2, y: 2, z: 4, core: 2. Of those that a mesh axis runs over, the one named last changes fastest.
Arguments:
- params: float32 [2, 2, 13696, 128], P('chan', None, 'dp'), may hold values from -6 to 6, as said below
- momentum: float32 [2, 2, 13696, 128], P('chan', None, 'dp'), may hold values from -1.5 to 1.5
- ema_params: float32 [2, 2, 13696, 128], P('chan', None, 'dp'), may hold values from -0.75 to 0.75
- latents: float32 [16, 4, 1024], P('dp'), may hold values from -6 to 6
- noise_eps: float32 [16, 4, 1024], P('dp'), may hold values from -6 to 6
- timesteps: int32 [16], P('dp'), may hold values from 0 to 999
- pixel_mask: int32 [16, 1024], P('dp'), may hold values from 0 to 1
- context: bfloat16 [16, 77, 768], P('dp'), may hold values from -6 to 6
Outputs:
- new_params: float32 [2, 2, 13696, 128], P('chan', None, 'dp')
- new_momentum: float32 [2, 2, 13696, 128], P('chan', None, 'dp')
- new_ema: float32 [2, 2, 13696, 128], P('chan', None, 'dp')
- loss_sum: float32 [], replicated
- pixel_count: float32 [], replicated
Inputs may be any that keep to these rules, and one draw needn't show every extreme that they name: `params`: weights about fan_in^-0.5 (self_out 8 times, cross_out 4 times that), gains about 1, biases about 0.1.
All inputs are finite; a program needn't handle non-finite values.
Results may differ from a plain program's by a relative error of at most 0.00096.
Values may be sent and summed in bfloat16 or wider, within the bound.
A program may use at most 448 MiB of HBM per device.

v0:
```python
import math

import jax
import jax.numpy as jnp
from jax import lax
from jax.experimental import pallas as pl
from jax.experimental.pallas import tpu as pltpu
from jax.sharding import PartitionSpec as P

D = 320
W = 160
HEADS = 8
HD = 40
CTX = 768
TXT = 77
LAT = 4
SIDE = 32
N = 1024
T = 256
EPS = 1e-5
LR = 0.2
MU = 0.9
ED = 0.9
CH = "chan"
DP = "dp"
F32 = jnp.float32
BF = jnp.bfloat16
HI = lax.Precision.HIGHEST
SCALE = HD**-0.5
LOG2E = 1.0 / math.log(2.0)

R0 = 4000
FRONT = 3650
T1, T2, T3 = 3650, 5255, 11660
C2 = 2
PI = 2885
QKV = 3208
SO = 4168
CQ = 4491
CKV = 4811
CO = 6347
GI = 6670
GIB = 9230
GO = 9238
PO = 10519
OUT = 10842
OUTB = 10878
R1 = 13600
VEC0 = (36, 37, 38, 2919)
VEC1 = (0, 1, 2882, 2883, 2884, 3205, 3206, 3207, 4488, 4489, 4490, 6667, 6668, 6669, 10518, 10839, 10840, 10841)
(N2G, N2B, C2B, NTG, NTB, PIB, L1G, L1B, SOB, L2G, L2B, COB, L3G, L3B, GOB, POB, NOG, NOB) = range(18)
MPI, MQ, MK, MV, MSO, MCQ, MCO, MGV, MGG, MGO, MPO = 9, 10, 11, 12, 13, 14, 15, 16, 20, 24, 28
NMAT = 29


def kcall(body, outs, ins, scratch=()):
    vm = pl.BlockSpec(memory_space=pltpu.VMEM)
    return pl.pallas_call(
        body,
        out_shape=outs,
        in_specs=[vm] * len(ins),
        out_specs=jax.tree.map(lambda _: vm, outs),
        scratch_shapes=list(scratch),
        compiler_params=pltpu.CompilerParams(vmem_limit_bytes=60 * 2**20),
    )(*ins)


def sds(shape, dtype=F32):
    return jax.ShapeDtypeStruct(shape, dtype)


def tiles(fn, size=T, total=N):
    @pl.loop(0, total // size)
    def _(t):
        fn(pl.ds(pl.multiple_of(t * size, size), size))


def nn(a, b):
    return jnp.dot(a, b, preferred_element_type=F32)


def nt(a, b):
    return lax.dot_general(a, b, (((1,), (1,)), ((), ())), preferred_element_type=F32)


def tn(a, b):
    return lax.dot_general(a, b, (((0,), (0,)), ((), ())), preferred_element_type=F32)


def colsum(v):
    return jnp.sum(v, axis=0, keepdims=True)


def unroll_rows(a_ref, tmp, s_ref, chunks):
    q = 80

    @pl.loop(0, chunks)
    def _(c):
        src = pl.ds(pl.multiple_of(c * 5 * q, 5 * q), 5 * q)
        for b in range(2):
            tmp[b] = a_ref[b, src, :].astype(F32)
        f = [[tmp[b, pl.ds(j, q, stride=5), :] for j in range(5)] for b in range(2)]
        for i in range(4):
            row = []
            for b in range(2):
                lo = 32 * i
                first, second = f[b][i], f[b][i + 1]
                row += [first[:, lo:], second[:, : lo + 32]] if lo else [first, second[:, :32]]
            full = jnp.concatenate(row, axis=1)
            for k, (lo, hi) in enumerate(((0, 128), (128, 256), (256, 320))):
                s_ref[k, pl.ds(c * 4 * q + i, q, stride=4), : hi - lo] = full[:, lo:hi]


def get_rows(s_ref, start, count, step=1):
    ds = pl.ds(start, count) if step == 1 else pl.ds(start, count, stride=step)
    return jnp.concatenate([s_ref[0, ds, :], s_ref[1, ds, :], s_ref[2, ds, :64]], axis=1)


def unpack0_kernel(a_ref, win, w1, vec, tmp, s_ref):
    unroll_rows(a_ref, tmp, s_ref, R0 // 400)
    win[...] = get_rows(s_ref, 0, 36).astype(BF)
    for t in range(9):
        w1[t] = get_rows(s_ref, 39 + D * t, D).astype(BF)
    for i, r in enumerate(VEC0):
        vec[i : i + 1, :] = get_rows(s_ref, r, 1)


def unpack1_kernel(a_ref, mats, kv, vec, gib, wout, outb, tmp, s_ref, o_ref):
    unroll_rows(a_ref, tmp, s_ref, R1 // 400)
    for t in range(9):
        mats[t] = get_rows(s_ref, C2 + D * t, D).astype(BF)
    for m, r in ((MPI, PI), (MSO, SO), (MCQ, CQ), (MCO, CO), (MPO, PO)):
        mats[m] = get_rows(s_ref, r, D).astype(BF)
    for j in range(3):
        mats[MQ + j] = get_rows(s_ref, QKV + j, D, 3).astype(BF)
    for j in range(8):
        mats[MGV + j] = get_rows(s_ref, GI + j, D, 8).astype(BF)
    for j in range(4):
        for b in range(2):
            mats[MGO + j, b * W : (b + 1) * W, :] = get_rows(s_ref, GO + 640 * b + W * j, W).astype(BF)
    for j in range(2):
        kv[j] = get_rows(s_ref, CKV + j, CTX, 2).astype(BF)
    for i, r in enumerate(VEC1):
        vec[i : i + 1, :] = get_rows(s_ref, r, 1)
    gib[...] = get_rows(s_ref, GIB, 8)
    outb[...] = get_rows(s_ref, OUTB, 1)
    lane = lax.broadcasted_iota(jnp.int32, (W, W), 0)
    col = lax.broadcasted_iota(jnp.int32, (W, W), 1)
    pick = ((lane % 2) * 80 + lane // 2 == col).astype(BF)
    raw = get_rows(s_ref, OUT, 36).astype(BF)
    for b in range(2):
        moved = nn(raw[:, W * b : W * (b + 1)], pick)
        o_ref[0, :36, :] = moved[:, :128]
        o_ref[1, :36, :32] = moved[:, 128:]
        for ch in range(2):
            pieces = []
            for m in range(4):
                ds = pl.ds(m, 9, stride=4)
                both = jnp.concatenate([o_ref[0, ds, :], o_ref[1, ds, :32]], axis=1)
                pieces.append(both[:, 80 * ch : 80 * ch + 80])
            at = (2 * b + ch) * 9
            wout[at : at + 9, :] = jnp.concatenate(pieces, axis=1).astype(BF)


def pixel_col(n, axis):
    shape = (n, 1) if axis == 0 else (1, n)
    return lax.broadcasted_iota(jnp.int32, shape, axis)


def shift_lanes(v, tap):
    r, s = tap // 3 - 1, tap % 3 - 1
    pix = pixel_col(N, 1)
    i, j = pix // SIDE + r, pix % SIDE + s
    ok = (i >= 0) & (i < SIDE) & (j >= 0) & (j < SIDE)
    move = -(r * SIDE + s) % N
    moved = pltpu.roll(v, move, 1) if move else v
    return jnp.where(ok, moved, 0.0)


def put_shifts(ref, rows, v):
    n = v.shape[0]
    j = pixel_col(n, 0) % SIDE
    at = pl.ds(pl.multiple_of(rows.start + SIDE, SIDE), n)
    ref[0, at, :] = jnp.where(j == 0, 0.0, pltpu.roll(v, 1, 0)).astype(BF)
    ref[1, at, :] = v.astype(BF)
    ref[2, at, :] = jnp.where(j == SIDE - 1, 0.0, pltpu.roll(v, n - 1, 0)).astype(BF)


def clear_margins(ref):
    for s in range(3):
        zero = jnp.zeros((SIDE, ref.shape[2]), BF)
        ref[s, :SIDE, :] = zero
        ref[s, N + SIDE :, :] = zero


def tap_rows(ref, rows, tap):
    at = pl.ds(pl.multiple_of(rows.start + SIDE * (tap // 3), SIDE), T)
    return ref[tap % 3, at, :]


def conv_rows(ref, rows, w_ref):
    total = nn(tap_rows(ref, rows, 0), w_ref[0])
    for tap in range(1, 9):
        total += nn(tap_rows(ref, rows, tap), w_ref[tap])
    return total


def conv_back_rows(ref, rows, w_ref):
    total = nt(tap_rows(ref, rows, 8), w_ref[0])
    for tap in range(1, 9):
        total += nt(tap_rows(ref, rows, 8 - tap), w_ref[tap])
    return total


def group_mean(sums):
    a = lax.broadcasted_iota(jnp.int32, (D, D), 0) // 10
    b = lax.broadcasted_iota(jnp.int32, (D, D), 1) // 10
    pool = jnp.where(a == b, 1.0, 0.0)
    wide = jnp.broadcast_to(sums, (8, D))
    out = jnp.dot(wide, pool, precision=HI, preferred_element_type=F32)
    return out[:1] * (1.0 / (10 * N))


def group_stats(v_ref, acc, sums):
    mean = group_mean(sums)
    acc[0:1, :] = jnp.zeros((1, D), F32)

    def one(rows):
        acc[0:1, :] += colsum(jnp.square(v_ref[rows, :] - mean))

    tiles(one)
    return mean, lax.rsqrt(group_mean(acc[0:1, :]) + EPS)


def silu(v):
    return v * jax.nn.sigmoid(v)


def silu_slope(v):
    sig = jax.nn.sigmoid(v)
    return sig * (1.0 + v * (1.0 - sig))


def layer(v):
    mean = jnp.sum(v, axis=1, keepdims=True) * (1.0 / D)
    sq = jnp.sum(v * v, axis=1, keepdims=True) * (1.0 / D)
    inv = lax.rsqrt(sq - mean * mean + EPS)
    return (v - mean) * inv, inv


def layer_back(grad, normed, inv, gain):
    ghat = grad * gain
    m1 = jnp.sum(ghat, axis=1, keepdims=True) * (1.0 / D)
    m2 = jnp.sum(ghat * normed, axis=1, keepdims=True) * (1.0 / D)
    return inv * (ghat - m1 - normed * m2)


def head(v, h):
    return v[:, HD * h : HD * (h + 1)]


def front_kernel(noisy, tv, win, w1, vec0, mats, vec1, h0, h1, h2, z0, a1, a2, ntr, x1, q, k, v, stats, sh, acc):
    cols = jnp.concatenate([shift_lanes(noisy[...], t) for t in range(9)], axis=0).astype(BF)
    acc[...] = jnp.zeros_like(acc)
    clear_margins(sh)
    h = tn(cols, win[...]) + vec0[0:1, :]
    h0[...] = h
    mean, inv = group_stats(h0, acc, colsum(h))
    stats[0:1, :], stats[1:2, :] = mean, inv

    def act(src, dst, gain, bias):
        def one(rows):
            y = silu((src[rows, :] - mean) * inv * gain + bias)
            put_shifts(sh, rows, y)
            dst[rows, :] = y.astype(BF)

        tiles(one)

    act(h0, a1, vec0[1:2, :], vec0[2:3, :])
    acc[1:2, :] = jnp.zeros((1, D), F32)

    def conv1(rows):
        y = conv_rows(sh, rows, w1) + vec0[3:4, :] + tv[...]
        h1[rows, :] = y
        acc[1:2, :] += colsum(y)

    tiles(conv1)
    mean, inv = group_stats(h1, acc, acc[1:2, :])
    stats[2:3, :], stats[3:4, :] = mean, inv
    act(h1, a2, vec1[N2G : N2G + 1, :], vec1[N2B : N2B + 1, :])
    acc[1:2, :] = jnp.zeros((1, D), F32)

    def conv2(rows):
        y = h0[rows, :] + conv_rows(sh, rows, mats) + vec1[C2B : C2B + 1, :]
        h2[rows, :] = y
        acc[1:2, :] += colsum(y)

    tiles(conv2)
    mean, inv = group_stats(h2, acc, acc[1:2, :])
    stats[4:5, :], stats[5:6, :] = mean, inv

    def last(rows):
        n = ((h2[rows, :] - mean) * inv * vec1[NTG : NTG + 1, :] + vec1[NTB : NTB + 1, :]).astype(BF)
        ntr[rows, :] = n
        z = nn(n, mats[MPI]) + vec1[PIB : PIB + 1, :]
        z0[rows, :] = z
        normed, _ = layer(z)
        x = (normed * vec1[L1G : L1G + 1, :] + vec1[L1B : L1B + 1, :]).astype(BF)
        x1[rows, :] = x
        for at, dst in ((MQ, q), (MK, k), (MV, v)):
            y = nn(x, mats[at]).astype(BF)
            for hd in range(HEADS):
                dst[hd, rows, :] = head(y, hd)

    tiles(last)


def attend_kernel(q, k, v, o, lse, ot):
    @pl.loop(0, HEADS)
    def _(h):
        kk = k[h]
        vt = v[h].astype(F32).T.astype(BF)
        for t in range(N // T):
            rows = pl.ds(t * T, T)
            s = nt(kk, q[h, rows, :]) * (SCALE * LOG2E)
            top = jnp.max(s, axis=0, keepdims=True)
            e = jnp.exp2(s - top)
            total = jnp.sum(e, axis=0, keepdims=True)
            lse[h, :, rows] = top + jnp.log(total) * LOG2E
            p = (e * (1.0 / total)).astype(BF)
            ot[pl.ds(pl.multiple_of(h * HD, HD), HD), rows] = nn(vt, p)

    o[...] = ot[...].T.astype(BF)


def cross_head(qh, kh, vh):
    s = nt(kh, qh) * (SCALE * LOG2E)
    e = jnp.exp2(s - jnp.max(s, axis=0, keepdims=True))
    return e * (1.0 / jnp.sum(e, axis=0, keepdims=True))


def back_half_kernel(
    o, z0, h2, ctx, noise, mask, mats, kvw, vec, gib, wout, outb,
    z1, z2, h3, x2, x3, oc, z3b, gl, a3, qc, kc, vc, derr, loss, stats, acc, ot,
):
    acc[...] = jnp.zeros_like(acc)
    kk = nn(ctx[...], kvw[0]).astype(BF)
    vv = nn(ctx[...], kvw[1])
    for h in range(HEADS):
        kc[h] = head(kk, h)
        vc[h] = head(vv, h).astype(BF)
    vt = vv.T

    def trunk(rows):
        z = z0[rows, :] + nn(o[rows, :], mats[MSO]) + vec[SOB : SOB + 1, :]
        z1[rows, :] = z
        normed, _ = layer(z)
        x = (normed * vec[L2G : L2G + 1, :] + vec[L2B : L2B + 1, :]).astype(BF)
        x2[rows, :] = x
        qq = nn(x, mats[MCQ]).astype(BF)
        for h in range(HEADS):
            qh = head(qq, h)
            qc[h, rows, :] = qh
            p = cross_head(qh, kc[h], None).astype(BF)
            ot[HD * h : HD * (h + 1), :] = nn(vt[HD * h : HD * (h + 1), :].astype(BF), p)
        c = ot[...].T.astype(BF)
        oc[rows, :] = c
        z = z + nn(c, mats[MCO]) + vec[COB : COB + 1, :]
        z2[rows, :] = z
        normed, _ = layer(z)
        x = (normed * vec[L3G : L3G + 1, :] + vec[L3B : L3B + 1, :]).astype(BF)
        x3[rows, :] = x
        for j in range(4):
            a = nn(x, mats[MGV + j]) + gib[j : j + 1, :]
            g = nn(x, mats[MGG + j]) + gib[4 + j : 5 + j, :]
            y = (a * (0.5 * g * (1.0 + lax.erf(g * math.sqrt(0.5))))).astype(BF)
            gl[j, rows, :] = y
            z = z + nn(y, mats[MGO + j])
        zb = (z + vec[GOB : GOB + 1, :]).astype(BF)
        z3b[rows, :] = zb
        hh = h2[rows, :] + nn(zb, mats[MPO]) + vec[POB : POB + 1, :]
        h3[rows, :] = hh
        acc[1:2, :] += colsum(hh)

    tiles(trunk)
    mean, inv = group_stats(h3, acc, acc[1:2, :])
    stats[0:1, :], stats[1:2, :] = mean, inv

    def act(rows):
        y = silu((h3[rows, :] - mean) * inv * vec[NOG : NOG + 1, :] + vec[NOB : NOB + 1, :])
        a3[rows, :] = y.astype(BF)

    tiles(act)
    taps = nt(wout[...], a3[...])
    total = jnp.zeros((1,), F32)
    for ch in range(LAT):
        pred = jnp.zeros((1, N), F32)
        for t in range(9):
            pred += shift_lanes(taps[9 * ch + t : 9 * ch + t + 1, :], t)
        at = W * (ch // 2) + ch % 2
        err = pred + outb[0:1, at : at + 1] - noise[ch : ch + 1, :]
        weighed = mask[...] * err
        derr[ch : ch + 1, :] = 2.0 * weighed
        acc[2 + ch : 3 + ch, 0:1] = jnp.sum(weighed * err, axis=1, keepdims=True)
    loss[...] = acc[2:3, 0:1] + acc[3:4, 0:1] + acc[4:5, 0:1] + acc[5:6, 0:1]


def group_back(n_of, grads, gain, dgain, dbias):
    return group_mean(gain * dbias), group_mean(gain * dgain)


def back_one_kernel(
    derr, h3, stats, a3, z1, z2, x3, qc, kc, vc, mats, vec, gib, wout,
    dh3, dz1, dh3b, dz3b, dab, dgb, dz2b, dqc, dz1b, dos, dkv, dvec, dgib, dwout, dbout,
    tmp, acc, ot, kacc, pt,
):
    acc[...] = jnp.zeros_like(acc)
    dgib[...] = jnp.zeros_like(dgib)
    dvec[...] = jnp.zeros_like(dvec)
    kacc[...] = jnp.zeros_like(kacc)
    for ch in range(LAT):
        g = derr[ch : ch + 1, :]
        dbout[ch : ch + 1, :] = jnp.broadcast_to(jnp.sum(g, axis=1, keepdims=True), (1, 128))
        for t in range(9):
            pt[9 * ch + t : 9 * ch + t + 1, :] = shift_lanes(g, 8 - t)
    taps = pt[...].astype(BF)
    dwout[...] = nn(taps, a3[...])
    tmp[...] = tn(taps, wout[...])
    mean, inv = stats[0:1, :], stats[1:2, :]
    gain, bias = vec[NOG : NOG + 1, :], vec[NOB : NOB + 1, :]

    def one(rows):
        n = (h3[rows, :] - mean) * inv
        g = tmp[rows, :] * silu_slope(n * gain + bias)
        tmp[rows, :] = g
        dvec[NOG : NOG + 1, :] += colsum(g * n)
        dvec[NOB : NOB + 1, :] += colsum(g)

    tiles(one)
    m1 = group_mean(gain * dvec[NOB : NOB + 1, :])
    m2 = group_mean(gain * dvec[NOG : NOG + 1, :])

    def trunk(rows):
        n = (h3[rows, :] - mean) * inv
        g = inv * (tmp[rows, :] * gain - m1 - n * m2)
        dh3[rows, :] = g
        dvec[POB : POB + 1, :] += colsum(g)
        gb = g.astype(BF)
        dh3b[rows, :] = gb
        dz3 = nt(gb, mats[MPO])
        dvec[GOB : GOB + 1, :] += colsum(dz3)
        zb = dz3.astype(BF)
        dz3b[rows, :] = zb
        x = x3[rows, :]
        dx = jnp.zeros((T, D), F32)
        for j in range(4):
            a = nn(x, mats[MGV + j]) + gib[j : j + 1, :]
            g = nn(x, mats[MGG + j]) + gib[4 + j : 5 + j, :]
            dgl = nt(zb, mats[MGO + j])
            cdf = 0.5 * (1.0 + lax.erf(g * math.sqrt(0.5)))
            da = dgl * (g * cdf)
            dg = dgl * a * (cdf + g * jnp.exp(-0.5 * g * g) * (1.0 / math.sqrt(2.0 * math.pi)))
            dgib[j : j + 1, :] += colsum(da)
            dgib[4 + j : 5 + j, :] += colsum(dg)
            da, dg = da.astype(BF), dg.astype(BF)
            dab[j, rows, :] = da
            dgb[j, rows, :] = dg
            dx += nt(da, mats[MGV + j]) + nt(dg, mats[MGG + j])
        normed, li = layer(z2[rows, :])
        dvec[L3G : L3G + 1, :] += colsum(dx * normed)
        dvec[L3B : L3B + 1, :] += colsum(dx)
        dz2 = dz3 + layer_back(dx, normed, li, vec[L3G : L3G + 1, :])
        dvec[COB : COB + 1, :] += colsum(dz2)
        zb = dz2.astype(BF)
        dz2b[rows, :] = zb
        do = nt(zb, mats[MCO]).astype(BF)
        for h in range(HEADS):
            qh, kh, vh, doh = qc[h, rows, :], kc[h], vc[h], head(do, h)
            p = cross_head(qh, kh, vh)
            dp = nt(vh, doh)
            ds = (p * (dp - jnp.sum(p * dp, axis=0, keepdims=True)) * SCALE).astype(BF)
            kacc[0, h] += nn(ds, qh)
            kacc[1, h] += nn(p.astype(BF), doh)
            ot[HD * h : HD * (h + 1), :] = tn(kh, ds)
        dq = ot[...].T.astype(BF)
        dqc[rows, :] = dq
        dx = nt(dq, mats[MCQ])
        normed, li = layer(z1[rows, :])
        dvec[L2G : L2G + 1, :] += colsum(dx * normed)
        dvec[L2B : L2B + 1, :] += colsum(dx)
        dz = dz2 + layer_back(dx, normed, li, vec[L2G : L2G + 1, :])
        dz1[rows, :] = dz
        dvec[SOB : SOB + 1, :] += colsum(dz)
        zb = dz.astype(BF)
        dz1b[rows, :] = zb
        do = nt(zb, mats[MSO]).astype(BF)
        for h in range(HEADS):
            dos[h, rows, :] = head(do, h)

    tiles(trunk)
    for j in range(2):
        dkv[j] = jnp.concatenate([kacc[j, h] for h in range(HEADS)], axis=1).astype(BF)


def attend_back_kernel(q, k, v, do, lse, dq, dk, dv, qt, kacc, vacc):
    @pl.loop(0, HEADS)
    def _(h):
        kk, vv = k[h], v[h]
        kt = kk.astype(F32).T.astype(BF)
        for t in range(N // T):
            rows = pl.ds(t * T, T)
            qh, doh = q[h, rows, :], do[h, rows, :]
            p = jnp.exp2(nt(kk, qh) * (SCALE * LOG2E) - lse[h, :, rows])
            dp = nt(vv, doh)
            ds = (p * (dp - jnp.sum(p * dp, axis=0, keepdims=True)) * SCALE).astype(BF)
            dkt, dvt = nn(ds, qh), nn(p.astype(BF), doh)
            if t == 0:
                kacc[h], vacc[h] = dkt, dvt
            else:
                kacc[h] += dkt
                vacc[h] += dvt
            qt[pl.ds(pl.multiple_of(h * HD, HD), HD), rows] = nn(kt, ds)

    dq[...] = qt[...].T.astype(BF)

    def one(rows):
        for acc, dst in ((kacc, dk), (vacc, dv)):
            dst[rows, :] = jnp.concatenate([acc[h, rows, :] for h in range(HEADS)], axis=1).astype(BF)

    tiles(one)


def back_two_kernel(
    dq, dk, dv, dz1, dh3, z0, h2, h1, h0, stats, w1, mats, vec0, vec1,
    dz0b, g2, g1, dh0b, dvec0, dvec1, dtv,
    tmp, dh,
):
    dvec0[...] = jnp.zeros_like(dvec0)
    dvec1[...] = jnp.zeros_like(dvec1)
    dtv[...] = jnp.zeros_like(dtv)
    clear_margins(g1)
    clear_margins(g2)

    def trunk(rows):
        dx = nt(dq[rows, :], mats[MQ]) + nt(dk[rows, :], mats[MK]) + nt(dv[rows, :], mats[MV])
        normed, li = layer(z0[rows, :])
        dvec1[L1G : L1G + 1, :] += colsum(dx * normed)
        dvec1[L1B : L1B + 1, :] += colsum(dx)
        dz = dz1[rows, :] + layer_back(dx, normed, li, vec1[L1G : L1G + 1, :])
        dvec1[PIB : PIB + 1, :] += colsum(dz)
        zb = dz.astype(BF)
        dz0b[rows, :] = zb
        g = nt(zb, mats[MPI])
        tmp[rows, :] = g
        n = (h2[rows, :] - stats[4:5, :]) * stats[5:6, :]
        dvec1[NTG : NTG + 1, :] += colsum(g * n)
        dvec1[NTB : NTB + 1, :] += colsum(g)

    tiles(trunk)

    def norm_rows(rows, src, at, gain, m1, m2):
        n = (src[rows, :] - stats[at : at + 1, :]) * stats[at + 1 : at + 2, :]
        return stats[at + 1 : at + 2, :] * (tmp[rows, :] * gain - m1 - n * m2)

    gain = vec1[NTG : NTG + 1, :]
    m1 = group_mean(gain * dvec1[NTB : NTB + 1, :])
    m2 = group_mean(gain * dvec1[NTG : NTG + 1, :])

    def second(rows):
        g = dh3[rows, :] + norm_rows(rows, h2, 4, gain, m1, m2)
        dh[rows, :] = g
        dvec1[C2B : C2B + 1, :] += colsum(g)
        put_shifts(g2, rows, g)

    tiles(second)
    gain2, bias2 = vec1[N2G : N2G + 1, :], vec1[N2B : N2B + 1, :]

    def conv2(rows):
        n = (h1[rows, :] - stats[2:3, :]) * stats[3:4, :]
        g = conv_back_rows(g2, rows, mats) * silu_slope(n * gain2 + bias2)
        tmp[rows, :] = g
        dvec1[N2G : N2G + 1, :] += colsum(g * n)
        dvec1[N2B : N2B + 1, :] += colsum(g)

    tiles(conv2)
    n1 = group_mean(gain2 * dvec1[N2B : N2B + 1, :])
    n2 = group_mean(gain2 * dvec1[N2G : N2G + 1, :])

    def third(rows):
        g = norm_rows(rows, h1, 2, gain2, n1, n2)
        dtv[...] += colsum(g)
        put_shifts(g1, rows, g)

    tiles(third)
    gain1, bias1 = vec0[1:2, :], vec0[2:3, :]

    def conv1(rows):
        n = (h0[rows, :] - stats[0:1, :]) * stats[1:2, :]
        g = conv_back_rows(g1, rows, w1) * silu_slope(n * gain1 + bias1)
        tmp[rows, :] = g
        dvec0[1:2, :] += colsum(g * n)
        dvec0[2:3, :] += colsum(g)

    tiles(conv1)
    dvec0[3:4, :] = dtv[...]
    k1 = group_mean(gain1 * dvec0[2:3, :])
    k2 = group_mean(gain1 * dvec0[1:2, :])

    def last(rows):
        g = dh[rows, :] + norm_rows(rows, h0, 0, gain1, k1, k2)
        dvec0[0:1, :] += colsum(g)
        dh0b[rows, :] = g.astype(BF)

    tiles(last)


def own(c, v):
    return jnp.where(c == 0, v[..., :W], v[..., W:])


def put_rows(s_ref, start, v, step=1):
    n = v.shape[0]
    ds = pl.ds(start, n) if step == 1 else pl.ds(start, n, stride=step)
    s_ref[0, ds, :] = v[:, :128]
    s_ref[1, ds, :32] = v[:, 128:]


def roll_rows(s_ref, tmp, out_ref, chunks):
    q = 80

    @pl.loop(0, chunks)
    def _(c):
        g = []
        for i in range(4):
            ds = pl.ds(c * 4 * q + i, q, stride=4)
            g.append((s_ref[0, ds, :], s_ref[1, ds, :32]))
        tmp[pl.ds(0, q, stride=5), :] = g[0][0]
        for i in range(3):
            lo = 96 - 32 * i
            tmp[pl.ds(i + 1, q, stride=5), :] = jnp.concatenate(
                ([g[i][0][:, 128 - 32 * i :]] if i else []) + [g[i][1], g[i + 1][0][:, :lo]], axis=1
            )
        tmp[pl.ds(4, q, stride=5), :] = jnp.concatenate([g[3][0][:, 32:], g[3][1]], axis=1)
        out_ref[pl.ds(pl.multiple_of(c * 5 * q, 5 * q), 5 * q), :] = tmp[...].astype(BF)


def conv_grads(c, a_ref, g_ref, s_ref, start, gown):
    at = a_ref[...].astype(F32).T.astype(BF)
    for s in range(3):
        gown[s] = own(c, g_ref[s].astype(F32)).astype(BF)
    for t in range(9):
        u = 8 - t
        put_rows(s_ref, start + D * t, nn(at, gown[u % 3, SIDE * (u // 3) : SIDE * (u // 3) + N, :]))


def grads0_kernel(c_ref, noisy, a1, g1, dh0b, dvec, out, s_ref, tmp, gown):
    c = c_ref[0, 0]
    cols = jnp.concatenate([shift_lanes(noisy[...], t) for t in range(9)], axis=0).astype(BF)
    put_rows(s_ref, 0, nn(cols, own(c, dh0b[...].astype(F32)).astype(BF)))
    conv_grads(c, a1, g1, s_ref, 39, gown)
    for i, r in enumerate(VEC0):
        put_rows(s_ref, r, own(c, dvec[i : i + 1, :]))
    roll_rows(s_ref, tmp, out, R0 // 400)


def grads1_kernel(
    c_ref, a2, g2, ntr, dz0b, x1, dq, dk, dv, o, dz1b, x2, dqc, ctx, dkv, oc, dz2b,
    x3, dab, dgb, gl, dz3b, z3b, dh3b, dvec, dgib, dwout, dbout,
    out, s_ref, tmp, gown, o_ref,
):
    c = c_ref[0, 0]
    conv_grads(c, a2, g2, s_ref, C2, gown)

    def pick(v):
        return own(c, v.astype(F32)).astype(BF)

    for x, g, r in ((ntr, dz0b, PI), (o, dz1b, SO), (x2, dqc, CQ), (oc, dz2b, CO), (z3b, dh3b, PO)):
        put_rows(s_ref, r, tn(x[...], pick(g[...])))
    for j, g in enumerate((dq, dk, dv)):
        put_rows(s_ref, QKV + j, tn(x1[...], pick(g[...])), 3)
    for j in range(4):
        put_rows(s_ref, GI + j, tn(x3[...], pick(dab[j])), 8)
        put_rows(s_ref, GI + 4 + j, tn(x3[...], pick(dgb[j])), 8)
        rows = tn(gl[j], pick(dz3b[...]))
        for b in range(2):
            put_rows(s_ref, GO + 640 * b + W * j, rows[W * b : W * (b + 1), :])
    for j in range(2):
        put_rows(s_ref, CKV + j, tn(ctx[...], pick(dkv[j])), 2)
    for i, r in enumerate(VEC1):
        put_rows(s_ref, r, own(c, dvec[i : i + 1, :]))
    put_rows(s_ref, GIB, own(c, dgib[...]))
    wide = jnp.where(c == 0, dwout[:18, :], dwout[18:36, :])
    for ch in range(2):
        for m in range(4):
            piece = wide[9 * ch : 9 * ch + 9, 80 * m : 80 * m + 80]
            o_ref[ch, pl.ds(m, 9, stride=4), :80] = piece
    lane = lax.broadcasted_iota(jnp.int32, (80, W), 0)
    col = lax.broadcasted_iota(jnp.int32, (80, W), 1)
    total = jnp.zeros((36, W), F32)
    for ch in range(2):
        spot = jnp.where(2 * lane + ch == col, 1.0, 0.0)
        total += jnp.dot(o_ref[ch, :36, :80], spot, precision=HI, preferred_element_type=F32)
    put_rows(s_ref, OUT, total)
    b0 = jnp.where(c == 0, dbout[0:1, 0:1], dbout[2:3, 0:1])
    b1 = jnp.where(c == 0, dbout[1:2, 0:1], dbout[3:4, 0:1])
    at = lax.broadcasted_iota(jnp.int32, (1, W), 1)
    put_rows(s_ref, OUTB, jnp.where(at == 0, b0, jnp.where(at == 1, b1, 0.0)))
    s_ref[:, OUTB + 1 :, :] = jnp.zeros((2, 10880 - OUTB - 1, 128), F32)
    roll_rows(s_ref, tmp, out, R1 // 400)


def spread_wide(u, count):
    rep = jnp.repeat(u, 5, axis=1)
    line = jnp.arange(5)[:, None] == (jnp.arange(rep.shape[1]) % 5)[None, :]
    return jnp.where(line[None], rep[:, None, :], 0.0).astype(u.dtype)


FIRST = (0, 0, 1, 2, 3)
SECOND = (0, 1, 2, 3, 3)


def spread_narrow(u):
    s, total = u.shape
    four = u.reshape(s, total // 4, 4)
    out = []
    for picks in (FIRST, SECOND):
        rep = jnp.stack([four[:, :, i] for i in picks], axis=2).reshape(s, -1)
        line = jnp.arange(5)[:, None] == (jnp.arange(rep.shape[1]) % 5)[None, :]
        out.append(jnp.where(line[None], rep[:, None, :], 0.0))
    return jnp.concatenate(out, axis=1).astype(u.dtype)


def lines_wide(g):
    return g.reshape(g.shape[0], 5, 128)


def lines_narrow(g):
    def pad(v, lo, hi):
        return jnp.pad(v, ((0, 0), (lo, hi)))

    a = [g[:, :128], pad(g[:, 128:], 0, 96), pad(g[:, 96:], 0, 64), pad(g[:, 64:], 0, 32), g[:, 32:]]
    b = [jnp.zeros_like(g[:, :128]), pad(g[:, :96], 32, 0), pad(g[:, :64], 64, 0), pad(g[:, :32], 96, 0)]
    return jnp.stack(a + b + [b[0]], axis=1)


def fold_narrow(y):
    def pad(v, lo, hi):
        return jnp.pad(v, (lo, hi))

    return (
        pad(y[0], 0, 32) + pad(y[1, :32], 128, 0) + pad(y[2, :64], 96, 0) + pad(y[3, :96], 64, 0) + pad(y[4], 32, 0)
        + pad(y[6, 32:], 0, 64) + pad(y[7, 64:], 0, 96) + pad(y[8, 96:], 0, 128)
    )


def extend(u, length):
    one = jnp.ones((u.shape[0], 1), u.dtype)
    rest = jnp.zeros((u.shape[0], length - u.shape[1] - 1), u.dtype)
    return jnp.concatenate([u, one, rest], axis=1)


def time_forward(part, steps):
    ladder = jnp.arange(D // 2, dtype=F32)
    freq = jnp.exp(-math.log(10000.0) * ladder / (D // 2))
    angles = steps.astype(F32)[:, None] * freq[None, :]
    e = jnp.concatenate([jnp.cos(angles), jnp.sin(angles)], axis=1).astype(BF)

    def wide(u, start):
        lines = spread_wide(extend(u, u.shape[1] + 1), 5)[0]
        rows = part[:, start : start + lines.shape[1]]
        return jnp.einsum("jr,brl->bjl", lines, rows, preferred_element_type=F32).reshape(1, -1)

    p1 = wide(e, T1)
    u1 = silu(p1).astype(BF)
    p2 = wide(u1, T2)
    u2 = silu(p2).astype(BF)
    lines = spread_narrow(extend(u2, u2.shape[1] + 4))[0]
    y = jnp.einsum("jr,brl->bjl", lines, part[:, T3 : T3 + lines.shape[1]], preferred_element_type=F32)
    tv = jnp.concatenate([fold_narrow(y[0]), fold_narrow(y[1])])[None, :]
    return tv, (e, u1, u2, p1, p2)


def time_backward(part, kept, dtv):
    e, u1, u2, p1, p2 = kept
    count = 4 * D
    g3 = dtv.astype(BF)
    lines = jnp.concatenate([lines_narrow(g3[:, :W]), lines_narrow(g3[:, W:])], axis=0)
    y = jnp.einsum("brl,bjl->rj", part[:, T3 : T3 + 5 * count // 4], lines, preferred_element_type=F32)
    y = y.reshape(count // 4, 5, 10)
    cols = [0.0] * 4
    for j in range(5):
        cols[FIRST[j]] += y[:, j, j]
        cols[SECOND[j]] += y[:, j, 5 + j]
    du2 = jnp.stack(cols, axis=1).reshape(1, count)
    d2 = du2 * silu_slope(p2)
    g2 = d2.astype(BF).reshape(2, 5, 128)
    y = jnp.einsum("brl,bjl->rj", part[:, T2 : T2 + 5 * count], g2, preferred_element_type=F32)
    y = y.reshape(count, 5, 5)
    du1 = jnp.sum(jnp.where(jnp.eye(5, dtype=bool)[None], y, 0.0), axis=(1, 2)).reshape(1, count)
    d1 = du1 * silu_slope(p1)
    return d1, d2, dtv


def time_rows(e, u1, u2, d1, d2, d3, first, count):
    total = jnp.zeros((count, 128), F32)

    def add(total, lines, grads, start):
        room = lines.shape[2]
        flat = lines.reshape(-1, room)
        flat = jnp.pad(flat, ((0, 0), (start, 0)))
        flat = jnp.pad(flat, ((0, 0), (0, max(0, 128 * 112 - flat.shape[1]))))
        mine = lax.dynamic_slice_in_dim(flat, first, count, 1)
        return total + jnp.einsum(
            "kr,kl->rl", mine, grads.reshape(-1, 128), precision=HI, preferred_element_type=F32
        )

    def parts(u, length):
        zero = jnp.zeros_like(u)
        weights = jnp.concatenate([u, jnp.zeros((u.shape[0], length - u.shape[1]), u.dtype)], axis=1)
        biases = jnp.concatenate([zero, jnp.ones((u.shape[0], 1), u.dtype)], axis=1)
        biases = jnp.pad(biases, ((0, 0), (0, length - biases.shape[1])))
        return weights.astype(F32), biases.astype(F32)

    for u, g, start in ((e, d1, T1), (u1, d2, T2)):
        w, b = parts(u, u.shape[1] + 1)
        total = add(total, spread_wide(w, 5), lines_wide(g.astype(BF).astype(F32)), start)
        total = add(total, spread_wide(b, 5), lines_wide(g), start)
    w, b = parts(u2, u2.shape[1] + 4)
    total = add(total, spread_narrow(w), lines_narrow(d3.astype(BF).astype(F32)), T3)
    total = add(total, spread_narrow(b), lines_narrow(d3), T3)
    return total


def alpha_bar(step_ids):
    levels = jnp.arange(1000, dtype=F32)
    lowest, highest = 0.00085**0.5, 0.012**0.5
    beta = jnp.square(lowest + (highest - lowest) * levels / 999.0)
    table = jnp.cumprod(1.0 - beta)
    matches = levels[None, :] == step_ids.astype(F32)[:, None]
    return jnp.sum(jnp.where(matches, table[None, :], 0.0), axis=1)


def shards(params, momentum, ema_params, latents, noise_eps, timesteps, pixel_mask, context):
    c = lax.axis_index(CH)
    d = lax.axis_index(DP)
    n_dp = lax.axis_size(DP)
    rows_dev = params.shape[2]
    rows_all = rows_dev * n_dp
    low = params.astype(BF)
    part0 = lax.all_gather(lax.all_gather(low[:, 0], CH, axis=0, tiled=True), DP, axis=1, tiled=True)
    part1 = lax.all_gather(lax.all_gather(low[:, 1], CH, axis=0, tiled=True), DP, axis=1, tiled=True)

    alpha = alpha_bar(timesteps)[:, None]
    noise = noise_eps[0]
    noisy = jnp.sqrt(alpha) * latents[0] + jnp.sqrt(1.0 - alpha) * noise
    mask = pixel_mask.astype(F32)

    px = (N, D)
    hx = (HEADS, N, HD)
    sh = (3, N + 2 * SIDE, D)
    win, w1, vec0 = kcall(
        unpack0_kernel,
        (sds((36, D), BF), sds((9, D, D), BF), sds((8, D))),
        (part0[:, :R0],),
        (pltpu.VMEM((2, 400, 128), F32), pltpu.VMEM((3, 4 * R0 // 5, 128), F32)),
    )
    mats, kvw, vec1, gib, wout, outb = kcall(
        unpack1_kernel,
        (sds((NMAT, D, D), BF), sds((2, CTX, D), BF), sds((24, D)), sds((8, D)), sds((36, D), BF), sds((1, D))),
        (part1[:, :R1],),
        (pltpu.VMEM((2, 400, 128), F32), pltpu.VMEM((3, 4 * R1 // 5, 128), F32), pltpu.VMEM((2, 40, 128), F32)),
    )
    tv, kept = time_forward(part0, timesteps)
    h0, h1, h2, z0, a1, a2, ntr, x1, q, k, v, stats = kcall(
        front_kernel,
        (sds(px),) * 4 + (sds(px, BF),) * 4 + (sds(hx, BF),) * 3 + (sds((8, D)),),
        (noisy, tv, win, w1, vec0, mats, vec1),
        (pltpu.VMEM(sh, BF), pltpu.VMEM((8, D), F32)),
    )
    o, lse = kcall(
        attend_kernel, (sds(px, BF), sds((HEADS, 1, N))), (q, k, v), (pltpu.VMEM((D, N), F32),)
    )
    z1, z2, h3, x2, x3, oc, z3b, gl, a3, qc, kc, vc, derr, loss, stats_out = kcall(
        back_half_kernel,
        (sds(px),) * 3 + (sds(px, BF),) * 4
        + (sds((4, N, D), BF), sds(px, BF), sds(hx, BF), sds((HEADS, TXT, HD), BF), sds((HEADS, TXT, HD), BF))
        + (sds((LAT, N)), sds((1, 1)), sds((8, D))),
        (o, z0, h2, context[0], noise, mask, mats, kvw, vec1, gib, wout, outb),
        (pltpu.VMEM((8, D), F32), pltpu.VMEM((D, T), F32)),
    )
    dh3, dz1, dh3b, dz3b, dab, dgb, dz2b, dqc, dz1b, dos, dkv, dvec_a, dgib, dwout, dbout = kcall(
        back_one_kernel,
        (sds(px),) * 2 + (sds(px, BF),) * 2 + (sds((4, N, D), BF),) * 2 + (sds(px, BF),) * 3
        + (sds(hx, BF), sds((2, TXT, D), BF), sds((24, D)), sds((8, D)), sds((36, D)), sds((8, 128))),
        (derr, h3, stats_out, a3, z1, z2, x3, qc, kc, vc, mats, vec1, gib, wout),
        (
            pltpu.VMEM(px, F32),
            pltpu.VMEM((8, D), F32),
            pltpu.VMEM((D, T), F32),
            pltpu.VMEM((2, HEADS, TXT, HD), F32),
            pltpu.VMEM((36, N), F32),
        ),
    )
    dq, dk, dv = kcall(
        attend_back_kernel,
        (sds(px, BF),) * 3,
        (q, k, v, dos, lse),
        (pltpu.VMEM((D, N), F32), pltpu.VMEM(hx, F32), pltpu.VMEM(hx, F32)),
    )
    dz0b, g2, g1, dh0b, dvec0, dvec_b, dtv = kcall(
        back_two_kernel,
        (sds(px, BF), sds(sh, BF), sds(sh, BF), sds(px, BF), sds((8, D)), sds((24, D)), sds((1, D))),
        (dq, dk, dv, dz1, dh3, z0, h2, h1, h0, stats, w1, mats, vec0, vec1),
        (pltpu.VMEM(px, F32), pltpu.VMEM(px, F32)),
    )
    which = jnp.full((1, 1), c, jnp.int32)
    flat1 = kcall(
        grads1_kernel,
        sds((R1, 128), BF),
        (which, a2, g2, ntr, dz0b, x1, dq, dk, dv, o, dz1b, x2, dqc, context[0], dkv, oc, dz2b,
         x3, dab, dgb, gl, dz3b, z3b, dh3b, dvec_a + dvec_b, dgib, dwout, dbout),
        (
            pltpu.VMEM((2, 4 * R1 // 5, 128), F32),
            pltpu.VMEM((400, 128), F32),
            pltpu.VMEM((3, N + 2 * SIDE, W), BF),
            pltpu.VMEM((2, 40, 128), F32),
        ),
    )
    flat0 = kcall(
        grads0_kernel,
        sds((R0, 128), BF),
        (which, noisy, a1, g1, dh0b, dvec0),
        (
            pltpu.VMEM((2, 4 * R0 // 5, 128), F32),
            pltpu.VMEM((400, 128), F32),
            pltpu.VMEM((3, N + 2 * SIDE, W), BF),
        ),
    )
    d1, d2, d3 = time_backward(part0, kept, dtv)
    mine = [lax.dynamic_slice_in_dim(g, c * (g.shape[1] // 2), g.shape[1] // 2, 1) for g in (d1, d2, d3)]
    facts = [f.astype(F32) for f in kept[:3]] + mine
    sizes = [f.shape[1] for f in facts]
    everyone = lax.all_gather(jnp.concatenate(facts, axis=1), DP, axis=0, tiled=True)
    facts = []
    at = 0
    for size in sizes:
        facts.append(everyone[:, at : at + size])
        at += size
    grad0 = time_rows(*facts, d * rows_dev, rows_dev)

    step = 16 * n_dp
    front = -(-FRONT // step) * step
    flat1 = jnp.pad(flat1, ((0, rows_all - R1), (0, 0)))
    keep = jnp.arange(front)[:, None] < FRONT
    flat0 = jnp.pad(flat0, ((0, max(0, front - R0)), (0, 0)))[:front]
    flat0 = jnp.where(keep, flat0, 0.0).astype(BF)
    sum1 = lax.psum_scatter(flat1, DP, scatter_dimension=0, tiled=True).astype(F32)
    some0 = lax.psum_scatter(flat0, DP, scatter_dimension=0, tiled=True)
    sum0 = lax.all_gather(some0, DP, axis=0, tiled=True)
    sum0 = jnp.pad(sum0, ((0, rows_all - front), (0, 0)))
    sum0 = lax.dynamic_slice_in_dim(sum0, d * rows_dev, rows_dev, 0).astype(F32)
    grad = jnp.stack([grad0 + sum0, sum1])[None]

    loss_sum, pixel_count = lax.psum((loss[0, 0], jnp.sum(mask)), DP)
    scaled = grad / (LAT * jnp.maximum(pixel_count, 1.0))
    new_momentum = MU * momentum + scaled
    new_params = params - LR * (scaled + MU * new_momentum)
    new_ema = ED * ema_params + (1.0 - ED) * new_params
    return (new_params, new_momentum, new_ema, loss_sum, pixel_count)


def solution(mesh):
    packed = P(CH, None, DP, None)
    row = P(DP, None, None)
    return jax.shard_map(
        shards,
        mesh=mesh,
        in_specs=(packed, packed, packed, row, row, P(DP), P(DP, None), row),
        out_specs=(packed, packed, packed, P(), P()),
        check_vma=False,
    )
```

profile of v0, /device:TPU:1, one launch (start us, length us, event | category | flops | bytes accessed | tf_op | source)
XLA Modules:
  0.0 568.0 jit_solution(1141016610819328350)
XLA Ops:
  8.5 8.1 %all-gather = bf16[2,1,856,128]{3,2,1,0:T(8,128)(2,1)} all-gather(bf16[1,1,856,128]{3,2,1,0:T(8,128)(2,1)S(1)} %get-tuple-element.149), channel_id=2, replica_groups=mesh['dp'=16,'chan'=2] {'chan'}, dimensions={0}, use_global_device_ids=true | all-gather | bytes 657408 | tf_op jit(solution)/shard_map/all_gather | solution.py:850
  16.6 6.4 %all-gather.2 = bf16[2,1,856,128]{3,2,1,0:T(8,128)(2,1)} all-gather(bf16[1,1,856,128]{3,2,1,0:T(8,128)(2,1)S(1)} %get-tuple-element.148), channel_id=4, replica_groups=mesh['dp'=16,'chan'=2] {'chan'}, dimensions={0}, use_global_device_ids=true | all-gather | bytes 657408 | tf_op jit(solution)/shard_map/all_gather | solution.py:851
  31.2 4.4 broadcast_in_dim.295
  35.6 3.7 broadcast_in_dim.296
  43.3 42.1 %all-gather.8.cloned.1.call-done = bf16[2,1,13696,128]{3,2,0,1:T(8,128)(2,1)} async-done(((bf16[2,1,856,128]{3,2,0,1:T(8,128)(2,1)}), bf16[2,1,13696,128]{3,2,0,1:T(8,128)(2,1)}) %all-gather.8.cloned.1.call-update) | async-done | bytes 7012368 | tf_op jit(solution)/shard_map/all_gather | solution.py:850
  97.4 54.9 %all-gather.10.cloned.1.call-done = bf16[2,1,13696,128]{3,2,0,1:T(8,128)(2,1)} async-done(((bf16[2,1,856,128]{3,2,0,1:T(8,128)(2,1)}), bf16[2,1,13696,128]{3,2,0,1:T(8,128)(2,1)}) %all-gather.10.cloned.1.call-update) | async-done | bytes 7012368 | tf_op jit(solution)/shard_map/all_gather | solution.py:851
  152.3 6.8 %slice.428.a_ref = bf16[2,13600,128]{2,1,0:T(8,128)(2,1)} slice(bf16[2,13696,128]{2,1,0:T(8,128)(2,1)} %bitcast.186), slice={[0:2], [0:13600], [0:128]} | slice | bytes 13926400 | tf_op jit(solution)/shard_map/slice | solution.py:870
  159.2 13.6 %shard_map.120 = (bf16[29,320,320]{2,1,0:T(8,128)(2,1)}, bf16[2,768,320]{2,1,0:T(8,128)(2,1)}, f32[24,320]{1,0:T(8,128)}, f32[8,320]{1,0:T(8,128)}, bf16[36,320]{1,0:T(8,128)(2,1)}, /*index=5*/f32[1,320]{1,0:T(1,128)}) custom-call(bf16[2,13600,128]{2,1,0:T(8,128)(2,1)} %slice.428.a_ref), custom_call_target="tpu_custom_call" | custom-call | tf_op jit(solution)/shard_map/pallas_call | solution.py:58
  172.7 4.9 shard_map.119
  177.7 29.3 %shard_map.121 = (f32[1024,320]{1,0:T(8,128)}, f32[1024,320]{1,0:T(8,128)}, f32[1024,320]{1,0:T(8,128)}, f32[1024,320]{1,0:T(8,128)}, bf16[1024,320]{1,0:T(8,128...) custom-call(f32[4,1024]{1,0:T(4,128)} %bitcast_add_fusion.noisy, ...), custom_call_target="tpu_custom_call" | custom-call | tf_op jit(solution)/shard_map/pallas_call | solution.py:58
  206.9 30.8 %shard_map.122 = (bf16[1024,320]{1,0:T(8,128)(2,1)}, f32[8,1,1024]{2,1,0:T(1,128)}) custom-call(bf16[8,1024,40]{2,1,0:T(8,128)(2,1)} %get-tuple-element.73.q, bf16[8,1024,40]{2,1,0:T(8,128)(2,1)} %get-tuple-element.74.k, bf16[8,1024,40]{2,1,0:T(8,128)(2,1)} %get-tuple-element.75.v), custom_call_target="tpu_custom_call" | custom-call | tf_op jit(solution)/shard_map/pallas_call | solution.py:58
  237.7 31.7 %shard_map.123 = (f32[1024,320]{1,0:T(8,128)}, f32[1024,320]{1,0:T(8,128)}, f32[1024,320]{1,0:T(8,128)}, bf16[1024,320]{1,0:T(8,128)(2,1)}, bf16[1024,320]{1,0:T...) custom-call(bf16[1024,320]{1,0:T(8,128)(2,1)} %get-tuple-element.76., ...), custom_call_target="tpu_custom_call" | custom-call | tf_op jit(solution)/shard_map/pallas_call | solution.py:58
  269.4 39.9 %shard_map.124 = (f32[1024,320]{1,0:T(8,128)}, f32[1024,320]{1,0:T(8,128)}, bf16[1024,320]{1,0:T(8,128)(2,1)}, bf16[1024,320]{1,0:T(8,128)(2,1)}, bf16[4,1024,32...) custom-call(f32[4,1024]{1,0:T(4,128)} %get-tuple-element.83.derr, ...), custom_call_target="tpu_custom_call" | custom-call | tf_op jit(solution)/shard_map/pallas_call | solution.py:58
  309.3 38.7 %shard_map.125 = (bf16[1024,320]{1,0:T(8,128)(2,1)}, bf16[1024,320]{1,0:T(8,128)(2,1)}, bf16[1024,320]{1,0:T(8,128)(2,1)}) custom-call(bf16[8,1024,40]{2,1,0:T(8,128)(2,1)} %get-tuple-element.73.q, bf16[8,1024,40]{2,1,0:T(8,128)(2,1)} %get-tuple-element.74.k, bf16[8,1024,40]{2,1,0:T(8,128)(2,1)} %get-tuple-element.75.v, ...), custom_call_target="tpu_custom_call" | custom-call | tf_op jit(solution)/shard_map/pallas_call | solution.py:58
  348.0 29.4 %shard_map.126 = (bf16[1024,320]{1,0:T(8,128)(2,1)}, bf16[3,1088,320]{2,1,0:T(8,128)(2,1)}, bf16[3,1088,320]{2,1,0:T(8,128)(2,1)}, bf16[1024,320]{1,0:T(8,128)(2...) custom-call(bf16[1024,320]{1,0:T(8,128)(2,1)} %get-tuple-element.95.dq, ...), custom_call_target="tpu_custom_call" | custom-call | tf_op jit(solution)/shard_map/pallas_call | solution.py:58
  387.1 19.8 %all-gather.4 = f32[16,1,4320]{2,1,0:T(1,128)S(1)} all-gather(f32[1,1,4320]{2,1,0:T(1,128)S(1)} %bitcast.207), channel_id=1, replica_groups=mesh['dp'=16,'chan'=2] {'dp'}, dimensions={0}, use_global_device_ids=true | all-gather | bytes 293760 | tf_op jit(solution)/shard_map/all_gather | solution.py:943
  410.3 7.2 %shard_map.127 = bf16[4000,128]{1,0:T(8,128)(2,1)} custom-call(s32[1,1]{1,0:T(1,128)} %bitcast.72.c_ref, f32[4,1024]{1,0:T(4,128)} %bitcast_add_fusion.noisy, bf16[1024,320]{1,0:T(8,128)(2,1)} %get-tuple-element.104.a1, bf16[3,1088,320]{2,1,0:T(8,128)(2,1)} %get-tuple-element.105.g1, bf16[1024,320]{1,0:T(8,128)(2,1)} %get-tuple-element.106.dh0b, ...), custom_call_target="tpu_custom_call" | custom-call | tf_op jit(solution)/shard_map/pallas_call | solution.py:58
  417.5 4.1 slice_select_fusion
  434.7 25.5 %shard_map.128 = bf16[13600,128]{1,0:T(8,128)(2,1)} custom-call(s32[1,1]{1,0:T(1,128)} %bitcast.72.c_ref, bf16[1024,320]{1,0:T(8,128)(2,1)} %get-tuple-element.108.a2, bf16[3,1088,320]{2,1,0:T(8,128)(2,1)} %get-tuple-element.109.g2, bf16[1024,320]{1,0:T(8,128)(2,1)} %get-tuple-element.110.ntr, bf16[1024,320]{1,0:T(8,128)(2,1)} %get-tuple-element.111.dz0b, ...), custom_call_target="tpu_custom_call" | custom-call | tf_op jit(solution)/shard_map/pallas_call | solution.py:58
  464.5 29.7 %all-reduce.58 = (f32[]{:T(128)}, f32[]{:T(128)}) all-reduce(f32[]{:T(128)} %convert_reduce_fusion, f32[]{:T(128)} %bitcast.75), channel_id=1, replica_groups=mesh['dp'=16,'chan'=2] {'dp'}, use_global_device_ids=true, to_apply=%region_8.9 | all-reduce | flops 2 | bytes 16 | tf_op jit(solution)/shard_map/psum | solution.py:964
  495.5 4.3 broadcast_in_dim.291
  499.8 3.8 broadcast_in_dim.292
  528.0 23.5 %all_gather.23 = bf16[3840,128]{1,0:T(8,128)(2,1)S(1)} all-gather(bf16[240,128]{1,0:T(8,128)(2,1)} %reduce-scatter.5.cloned.1.call-done), channel_id=1, replica_groups=mesh['dp'=16,'chan'=2] {'dp'}, dimensions={0}, use_global_device_ids=true | all-gather | bytes 1044480 | tf_op jit(solution)/shard_map/all_gather | solution.py:959
  553.3 3.9 reduce-scatter.7.cloned.1.call-done
  (238 shorter events, 84.1 us)
Async XLA Ops:
  7.2 19.8 %copy-start.22 = (s32[1,1024]{1,0:T(1,128)S(1)}, s32[1,1024]{1,0:T(1,128)}, u32[]{:S(2)}) copy-start(s32[1,1024]{1,0:T(1,128)} %param.14) | copy-start | bytes 12292
  7.2 78.2 %all-gather.8.cloned.1.call-start = ((), (), s32[]{:S(2)}) async-start(), calls=%async_computation.3 | async-start | bytes 7450624 | tf_op jit(solution)/shard_map/all_gather | solution.py:850
  8.5 21.5 %copy-start.11 = (f32[16,321]{0,1:T(8,128)S(1)}, f32[16,321]{0,1:T(8,128)}, u32[]{:S(2)}) copy-start(f32[16,321]{0,1:T(8,128)} %constant.122.clone.1) | copy-start | bytes 61636
  16.6 135.7 %all-gather.10.cloned.1.call-start = ((), (), s32[]{:S(2)}) async-start(), calls=%async_computation.4 | async-start | bytes 7450624 | tf_op jit(solution)/shard_map/all_gather | solution.py:851
  23.1 504.9 %reduce-scatter.5.cloned.1.call-start = ((), (), s32[]{:S(2)}) async-start(), calls=%async_computation.2 | async-start | bytes 1044480 | tf_op jit(solution)/shard_map/reduce_scatter | solution.py:958
  39.3 2.8 copy-start.15
  39.3 2.8 copy-start.21
  383.1 3.7 copy-start.23
  406.9 2.8 copy-start.5
  421.6 135.5 %reduce-scatter.7.cloned.1.call-start = ((), (), s32[]{:S(2)}) async-start(), calls=%async_computation.5 | async-start | bytes 3725312
  423.6 2.0 copy-start.24
  430.3 1.2 copy-start.20
  432.8 1.2 copy-start.16
  432.8 1.2 copy-start.17
  464.4 30.9 %copy-start.9 = (f32[16,1280]{1,0:T(8,128)S(1)}, f32[16,1280]{1,0:T(8,128)}, u32[]{:S(2)}) copy-start(f32[16,1280]{1,0:T(8,128)} %get-tuple-element.157) | copy-start | bytes 245764
  503.6 2.0 copy-start.10
  519.7 2.4 copy-start.14
  519.7 3.2 copy-start.12
  521.3 2.8 copy-start
  522.9 2.0 copy-start.1
  524.9 1.2 copy-start.2
  524.9 1.2 copy-start.8
  526.2 25.3 %copy-start.3 = (f32[160,1605]{1,0:T(8,128)S(1)}, f32[160,1605]{1,0:T(8,128)}, u32[]{:S(2)}) copy-start(f32[160,1605]{1,0:T(8,128)} %reshape.727) | copy-start | bytes 3081604
  527.9 30.2 %copy-start.4 = (f32[1,2,856,128]{3,2,1,0:T(8,128)S(1)}, f32[1,2,856,128]{3,2,1,0:T(8,128)}, u32[]{:S(2)}) copy-start(f32[1,2,856,128]{3,2,1,0:T(8,128)} %param.8) | copy-start | bytes 2629636
  (5 other events, 5.5 us)
Sparse Core Ops, SparseCore 0:
  16.7 68.6 all-gather.7
  87.6 64.6 all-gather.9
  421.8 51.5 reduce-scatter.4
  477.6 79.4 reduce-scatter.6
where the time goes:
time: 575 us; the launch traced here: 568 us
  Pallas kernels  251 us (44%)
  waiting for transfers between devices  101 us (18%)
  blocking collectives  87.5 us (15%)
  local copies, waits for them, and re-layouts  68.2 us (12%)
  other arithmetic  24.7 us (4%)
  matrix products  17.6 us (3%)
  between operations  17.6 us (3%)
    pallas_call x10, Pallas kernels, kcall(): pl.pallas_call(body, out_shape=outs, in_specs=[vm] * len(ins), out_specs=...  251 us
    all_gather x1, waiting for transfers between devices, shards(): lax.all_gather(lax.all_gather(low[:, 1], CH, axis=0, tiled=True), DP, axi...  54.9 us
    all_gather x1, waiting for transfers between devices, shards(): lax.all_gather(lax.all_gather(low[:, 0], CH, axis=0, tiled=True), DP, axi...  42.1 us
    psum x1, blocking collectives, shards(): loss_sum, pixel_count = lax.psum((loss[0, 0], jnp.sum(mask)), DP)  29.7 us
    all_gather x1, blocking collectives, shards(): sum0 = lax.all_gather(some0, DP, axis=0, tiled=True)  23.5 us
    all_gather x1, blocking collectives, shards(): lax.all_gather(jnp.concatenate(facts, axis=1), DP, axis=0, tiled=True)  19.8 us
    broadcast_in_dim x8, local copies, waits for them, and re-layouts, spread_wide(): return jnp.where(line[None], rep[:, None, :], 0.0).astype(u.dtype)  13 us
  transfers between devices with their start and end apart: 4, of which 3 were waited for; matrix products, arithmetic and copies ran while one was open for 14% of the time, Pallas kernels for 4%

commit v1 on v0

--- a/solution.py
+++ b/solution.py
@@ -1,4 +1,5 @@
 import math
+from functools import partial
 
 import jax
 import jax.numpy as jnp
@@ -30,6 +31,7 @@
 LOG2E = 1.0 / math.log(2.0)
 
 R0 = 4000
+U1, U2, U3 = 2920, 4204, 9328
 FRONT = 3650
 T1, T2, T3 = 3650, 5255, 11660
 C2 = 2
@@ -61,7 +63,7 @@
         in_specs=[vm] * len(ins),
         out_specs=jax.tree.map(lambda _: vm, outs),
         scratch_shapes=list(scratch),
-        compiler_params=pltpu.CompilerParams(vmem_limit_bytes=60 * 2**20),
+        compiler_params=pltpu.CompilerParams(vmem_limit_bytes=63 * 2**20),
     )(*ins)
 
 
@@ -91,15 +93,15 @@
     return jnp.sum(v, axis=0, keepdims=True)
 
 
-def unroll_rows(a_ref, tmp, s_ref, chunks):
+def unroll_rows(a_ref, flat, s_ref, chunks, rows):
     q = 80
+    for b in range(2):
+        for t in range(a_ref.shape[1]):
+            flat[b, t * rows : (t + 1) * rows, :] = a_ref[b, t, :rows, :].astype(F32)
 
     @pl.loop(0, chunks)
     def _(c):
-        src = pl.ds(pl.multiple_of(c * 5 * q, 5 * q), 5 * q)
-        for b in range(2):
-            tmp[b] = a_ref[b, src, :].astype(F32)
-        f = [[tmp[b, pl.ds(j, q, stride=5), :] for j in range(5)] for b in range(2)]
+        f = [[flat[b, pl.ds(c * 5 * q + j, q, stride=5), :] for j in range(5)] for b in range(2)]
         for i in range(4):
             row = []
             for b in range(2):
@@ -116,17 +118,49 @@
     return jnp.concatenate([s_ref[0, ds, :], s_ref[1, ds, :], s_ref[2, ds, :64]], axis=1)
 
 
-def unpack0_kernel(a_ref, win, w1, vec, tmp, s_ref):
-    unroll_rows(a_ref, tmp, s_ref, R0 // 400)
+def unit_row(parts):
+    out = [p[:, W * b : W * (b + 1)] for b in range(2) for p in parts]
+    return jnp.broadcast_to(jnp.concatenate(out, axis=1), (8, 4 * D))
+
+
+def unit_parts(row):
+    return [
+        jnp.concatenate([row[:, W * i : W * (i + 1)], row[:, 640 + W * i : 640 + W * (i + 1)]], axis=1)
+        for i in range(4)
+    ]
+
+
+def unpack0_kernel(rows, a_ref, e, win, w1, vec, tw2, tw3, tv, p1, p2, flat, s_ref):
+    unroll_rows(a_ref, flat, s_ref, R1 // 400, rows)
     win[...] = get_rows(s_ref, 0, 36).astype(BF)
     for t in range(9):
         w1[t] = get_rows(s_ref, 39 + D * t, D).astype(BF)
     for i, r in enumerate(VEC0):
         vec[i : i + 1, :] = get_rows(s_ref, r, 1)
-
-
-def unpack1_kernel(a_ref, mats, kv, vec, gib, wout, outb, tmp, s_ref, o_ref):
-    unroll_rows(a_ref, tmp, s_ref, R1 // 400)
+    for i in range(4):
+        tw2[i] = get_rows(s_ref, U2 + i, 4 * D, 4).astype(BF)
+    tw3[...] = get_rows(s_ref, U3, 4 * D).astype(BF)
+    u = e[...].astype(BF)
+    p1[...] = unit_row(
+        [nn(u, get_rows(s_ref, U1 + i, D, 4).astype(BF))[:1] + get_rows(s_ref, U1 + 4 * D + i, 1) for i in range(4)]
+    )
+    u = silu(p1[...]).astype(BF)
+    p2[...] = unit_row([nn(u, tw2[i])[:1] + get_rows(s_ref, U2 + 16 * D + i, 1) for i in range(4)])
+    u = silu(p2[...]).astype(BF)
+    tv[...] = nn(u, tw3[...])[:1] + get_rows(s_ref, U3 + 4 * D, 1)
+
+
+def time_back_kernel(dtv, tw2, tw3, p1, p2, d1, d2):
+    g = jnp.broadcast_to(dtv[...], (8, D)).astype(BF)
+    d2[...] = nt(g, tw3[...]) * silu_slope(p2[...])
+    total = jnp.zeros((8, 4 * D), F32)
+    for i, part in enumerate(unit_parts(d2[...])):
+        total += nt(part.astype(BF), tw2[i])
+    d1[...] = total * silu_slope(p1[...])
+
+
+def unpack1_kernel(rows, a_ref, mats, kv, vec, gib, wout, outb, flat, s_ref, o_ref):
+    unroll_rows(a_ref, flat, s_ref, R1 // 400, rows)
     for t in range(9):
         mats[t] = get_rows(s_ref, C2 + D * t, D).astype(BF)
     for m, r in ((MPI, PI), (MSO, SO), (MCQ, CQ), (MCO, CO), (MPO, PO)):
@@ -255,6 +289,10 @@
     return inv * (ghat - m1 - normed * m2)
 
 
+def own(v):
+    return jnp.where(lax.axis_index(CH) == 0, v[..., :W], v[..., W:])
+
+
 def head(v, h):
     return v[:, HD * h : HD * (h + 1)]
 
@@ -446,11 +484,11 @@
         dh3[rows, :] = g
         dvec[POB : POB + 1, :] += colsum(g)
         gb = g.astype(BF)
-        dh3b[rows, :] = gb
+        dh3b[rows, :] = own(g).astype(BF)
         dz3 = nt(gb, mats[MPO])
         dvec[GOB : GOB + 1, :] += colsum(dz3)
         zb = dz3.astype(BF)
-        dz3b[rows, :] = zb
+        dz3b[rows, :] = own(dz3).astype(BF)
         x = x3[rows, :]
         dx = jnp.zeros((T, D), F32)
         for j in range(4):
@@ -462,9 +500,9 @@
             dg = dgl * a * (cdf + g * jnp.exp(-0.5 * g * g) * (1.0 / math.sqrt(2.0 * math.pi)))
             dgib[j : j + 1, :] += colsum(da)
             dgib[4 + j : 5 + j, :] += colsum(dg)
+            dab[j, rows, :] = own(da).astype(BF)
+            dgb[j, rows, :] = own(dg).astype(BF)
             da, dg = da.astype(BF), dg.astype(BF)
-            dab[j, rows, :] = da
-            dgb[j, rows, :] = dg
             dx += nt(da, mats[MGV + j]) + nt(dg, mats[MGG + j])
         normed, li = layer(z2[rows, :])
         dvec[L3G : L3G + 1, :] += colsum(dx * normed)
@@ -472,7 +510,7 @@
         dz2 = dz3 + layer_back(dx, normed, li, vec[L3G : L3G + 1, :])
         dvec[COB : COB + 1, :] += colsum(dz2)
         zb = dz2.astype(BF)
-        dz2b[rows, :] = zb
+        dz2b[rows, :] = own(dz2).astype(BF)
         do = nt(zb, mats[MCO]).astype(BF)
         for h in range(HEADS):
             qh, kh, vh, doh = qc[h, rows, :], kc[h], vc[h], head(do, h)
@@ -482,8 +520,9 @@
             kacc[0, h] += nn(ds, qh)
             kacc[1, h] += nn(p.astype(BF), doh)
             ot[HD * h : HD * (h + 1), :] = tn(kh, ds)
-        dq = ot[...].T.astype(BF)
-        dqc[rows, :] = dq
+        dq = ot[...].T
+        dqc[rows, :] = own(dq).astype(BF)
+        dq = dq.astype(BF)
         dx = nt(dq, mats[MCQ])
         normed, li = layer(z1[rows, :])
         dvec[L2G : L2G + 1, :] += colsum(dx * normed)
@@ -492,14 +531,14 @@
         dz1[rows, :] = dz
         dvec[SOB : SOB + 1, :] += colsum(dz)
         zb = dz.astype(BF)
-        dz1b[rows, :] = zb
+        dz1b[rows, :] = own(dz).astype(BF)
         do = nt(zb, mats[MSO]).astype(BF)
         for h in range(HEADS):
             dos[h, rows, :] = head(do, h)
 
     tiles(trunk)
     for j in range(2):
-        dkv[j] = jnp.concatenate([kacc[j, h] for h in range(HEADS)], axis=1).astype(BF)
+        dkv[j] = own(jnp.concatenate([kacc[j, h] for h in range(HEADS)], axis=1)).astype(BF)
 
 
 def attend_back_kernel(q, k, v, do, lse, dq, dk, dv, qt, kacc, vacc):
@@ -532,14 +571,14 @@
 
 def back_two_kernel(
     dq, dk, dv, dz1, dh3, z0, h2, h1, h0, stats, w1, mats, vec0, vec1,
-    dz0b, g2, g1, dh0b, dvec0, dvec1, dtv,
-    tmp, dh,
+    dz0b, g2o, g1o, dh0b, dvec0, dvec1, dtv,
+    tmp, dh, g2, g1,
 ):
     dvec0[...] = jnp.zeros_like(dvec0)
     dvec1[...] = jnp.zeros_like(dvec1)
     dtv[...] = jnp.zeros_like(dtv)
-    clear_margins(g1)
-    clear_margins(g2)
+    for ref in (g1, g2, g1o, g2o):
+        clear_margins(ref)
 
     def trunk(rows):
         dx = nt(dq[rows, :], mats[MQ]) + nt(dk[rows, :], mats[MK]) + nt(dv[rows, :], mats[MV])
@@ -549,7 +588,7 @@
         dz = dz1[rows, :] + layer_back(dx, normed, li, vec1[L1G : L1G + 1, :])
         dvec1[PIB : PIB + 1, :] += colsum(dz)
         zb = dz.astype(BF)
-        dz0b[rows, :] = zb
+        dz0b[rows, :] = own(dz).astype(BF)
         g = nt(zb, mats[MPI])
         tmp[rows, :] = g
         n = (h2[rows, :] - stats[4:5, :]) * stats[5:6, :]
@@ -571,6 +610,7 @@
         dh[rows, :] = g
         dvec1[C2B : C2B + 1, :] += colsum(g)
         put_shifts(g2, rows, g)
+        put_shifts(g2o, rows, own(g))
 
     tiles(second)
     gain2, bias2 = vec1[N2G : N2G + 1, :], vec1[N2B : N2B + 1, :]
@@ -590,6 +630,7 @@
         g = norm_rows(rows, h1, 2, gain2, n1, n2)
         dtv[...] += colsum(g)
         put_shifts(g1, rows, g)
+        put_shifts(g1o, rows, own(g))
 
     tiles(third)
     gain1, bias1 = vec0[1:2, :], vec0[2:3, :]
@@ -609,13 +650,9 @@
     def last(rows):
         g = dh[rows, :] + norm_rows(rows, h0, 0, gain1, k1, k2)
         dvec0[0:1, :] += colsum(g)
-        dh0b[rows, :] = g.astype(BF)
+        dh0b[rows, :] = own(g).astype(BF)
 
     tiles(last)
-
-
-def own(c, v):
-    return jnp.where(c == 0, v[..., :W], v[..., W:])
 
 
 def put_rows(s_ref, start, v, step=1):
@@ -625,70 +662,83 @@
     s_ref[1, ds, :32] = v[:, 128:]
 
 
-def roll_rows(s_ref, tmp, out_ref, chunks):
+def roll_rows(s_ref, out_ref, lo_chunk, hi_chunk):
     q = 80
 
-    @pl.loop(0, chunks)
+    @pl.loop(lo_chunk, hi_chunk)
     def _(c):
         g = []
         for i in range(4):
             ds = pl.ds(c * 4 * q + i, q, stride=4)
             g.append((s_ref[0, ds, :], s_ref[1, ds, :32]))
-        tmp[pl.ds(0, q, stride=5), :] = g[0][0]
+        base = (c - lo_chunk) * 5 * q
+        out_ref[pl.ds(base, q, stride=5), :] = g[0][0]
         for i in range(3):
             lo = 96 - 32 * i
-            tmp[pl.ds(i + 1, q, stride=5), :] = jnp.concatenate(
+            out_ref[pl.ds(base + i + 1, q, stride=5), :] = jnp.concatenate(
                 ([g[i][0][:, 128 - 32 * i :]] if i else []) + [g[i][1], g[i + 1][0][:, :lo]], axis=1
             )
-        tmp[pl.ds(4, q, stride=5), :] = jnp.concatenate([g[3][0][:, 32:], g[3][1]], axis=1)
-        out_ref[pl.ds(pl.multiple_of(c * 5 * q, 5 * q), 5 * q), :] = tmp[...].astype(BF)
-
-
-def conv_grads(c, a_ref, g_ref, s_ref, start, gown):
+        out_ref[pl.ds(base + 4, q, stride=5), :] = jnp.concatenate([g[3][0][:, 32:], g[3][1]], axis=1)
+
+
+def by_owner(s_ref, flat, out, total):
+    owners, room = math.prod(out.shape[:-2]), out.shape[-2]
+    size = room if total < owners * room and len(out.shape) == 3 else min(room, ROWS)
+    half = owners // 2 * size
+    for lo, hi, first in ((0, min(-(-half // 400), total // 400), 0), (half // 400, total // 400, owners // 2)):
+        if hi > lo:
+            roll_rows(s_ref, flat, lo, hi)
+        at = 400 * max(hi - lo, 0)
+        if at < flat.shape[0]:
+            flat[at:, :] = jnp.zeros((flat.shape[0] - at, 128), F32)
+        for t in range(first, first + owners // 2):
+            spot = (t % 2, t // 2) if len(out.shape) == 4 else (t,)
+            row = t * size - 400 * lo
+            out[(*spot, slice(0, size))] = flat[row : row + size, :].astype(BF)
+            if room > size:
+                out[(*spot, slice(size, room))] = jnp.zeros((room - size, 128), BF)
+
+
+def conv_grads(a_ref, g_ref, s_ref, start):
     at = a_ref[...].astype(F32).T.astype(BF)
-    for s in range(3):
-        gown[s] = own(c, g_ref[s].astype(F32)).astype(BF)
     for t in range(9):
         u = 8 - t
-        put_rows(s_ref, start + D * t, nn(at, gown[u % 3, SIDE * (u // 3) : SIDE * (u // 3) + N, :]))
-
-
-def grads0_kernel(c_ref, noisy, a1, g1, dh0b, dvec, out, s_ref, tmp, gown):
-    c = c_ref[0, 0]
+        put_rows(s_ref, start + D * t, nn(at, g_ref[u % 3, SIDE * (u // 3) : SIDE * (u // 3) + N, :]))
+
+
+def grads0_kernel(noisy, a1, g1, dh0b, dvec, out, s_ref, flat):
     cols = jnp.concatenate([shift_lanes(noisy[...], t) for t in range(9)], axis=0).astype(BF)
-    put_rows(s_ref, 0, nn(cols, own(c, dh0b[...].astype(F32)).astype(BF)))
-    conv_grads(c, a1, g1, s_ref, 39, gown)
+    put_rows(s_ref, 0, nn(cols, dh0b[...]))
+    conv_grads(a1, g1, s_ref, 39)
     for i, r in enumerate(VEC0):
-        put_rows(s_ref, r, own(c, dvec[i : i + 1, :]))
-    roll_rows(s_ref, tmp, out, R0 // 400)
+        put_rows(s_ref, r, own(dvec[i : i + 1, :]))
+    s_ref[:, 4 * FRONT // 5 :, :] = jnp.zeros((2, s_ref.shape[1] - 4 * FRONT // 5, 128), F32)
+    by_owner(s_ref, flat, out, R0)
 
 
 def grads1_kernel(
-    c_ref, a2, g2, ntr, dz0b, x1, dq, dk, dv, o, dz1b, x2, dqc, ctx, dkv, oc, dz2b,
+    a2, g2, ntr, dz0b, x1, dq, dk, dv, o, dz1b, x2, dqc, ctx, dkv, oc, dz2b,
     x3, dab, dgb, gl, dz3b, z3b, dh3b, dvec, dgib, dwout, dbout,
-    out, s_ref, tmp, gown, o_ref,
+    out, s_ref, flat, o_ref,
 ):
-    c = c_ref[0, 0]
-    conv_grads(c, a2, g2, s_ref, C2, gown)
-
-    def pick(v):
-        return own(c, v.astype(F32)).astype(BF)
+    c = lax.axis_index(CH)
+    conv_grads(a2, g2, s_ref, C2)
 
     for x, g, r in ((ntr, dz0b, PI), (o, dz1b, SO), (x2, dqc, CQ), (oc, dz2b, CO), (z3b, dh3b, PO)):
-        put_rows(s_ref, r, tn(x[...], pick(g[...])))
+        put_rows(s_ref, r, tn(x[...], g[...]))
     for j, g in enumerate((dq, dk, dv)):
-        put_rows(s_ref, QKV + j, tn(x1[...], pick(g[...])), 3)
+        put_rows(s_ref, QKV + j, tn(x1[...], own(g[...].astype(F32)).astype(BF)), 3)
     for j in range(4):
-        put_rows(s_ref, GI + j, tn(x3[...], pick(dab[j])), 8)
-        put_rows(s_ref, GI + 4 + j, tn(x3[...], pick(dgb[j])), 8)
-        rows = tn(gl[j], pick(dz3b[...]))
+        put_rows(s_ref, GI + j, tn(x3[...], dab[j]), 8)
+        put_rows(s_ref, GI + 4 + j, tn(x3[...], dgb[j]), 8)
+        rows = tn(gl[j], dz3b[...])
         for b in range(2):
             put_rows(s_ref, GO + 640 * b + W * j, rows[W * b : W * (b + 1), :])
     for j in range(2):
-        put_rows(s_ref, CKV + j, tn(ctx[...], pick(dkv[j])), 2)
+        put_rows(s_ref, CKV + j, tn(ctx[...], dkv[j]), 2)
     for i, r in enumerate(VEC1):
-        put_rows(s_ref, r, own(c, dvec[i : i + 1, :]))
-    put_rows(s_ref, GIB, own(c, dgib[...]))
+        put_rows(s_ref, r, own(dvec[i : i + 1, :]))
+    put_rows(s_ref, GIB, own(dgib[...]))
     wide = jnp.where(c == 0, dwout[:18, :], dwout[18:36, :])
     for ch in range(2):
         for m in range(4):
@@ -706,129 +756,334 @@
     at = lax.broadcasted_iota(jnp.int32, (1, W), 1)
     put_rows(s_ref, OUTB, jnp.where(at == 0, b0, jnp.where(at == 1, b1, 0.0)))
     s_ref[:, OUTB + 1 :, :] = jnp.zeros((2, 10880 - OUTB - 1, 128), F32)
-    roll_rows(s_ref, tmp, out, R1 // 400)
-
-
-def spread_wide(u, count):
-    rep = jnp.repeat(u, 5, axis=1)
-    line = jnp.arange(5)[:, None] == (jnp.arange(rep.shape[1]) % 5)[None, :]
-    return jnp.where(line[None], rep[:, None, :], 0.0).astype(u.dtype)
+    by_owner(s_ref, flat, out, R1)
 
 
 FIRST = (0, 0, 1, 2, 3)
 SECOND = (0, 1, 2, 3, 3)
 
 
-def spread_narrow(u):
-    s, total = u.shape
-    four = u.reshape(s, total // 4, 4)
-    out = []
-    for picks in (FIRST, SECOND):
-        rep = jnp.stack([four[:, :, i] for i in picks], axis=2).reshape(s, -1)
-        line = jnp.arange(5)[:, None] == (jnp.arange(rep.shape[1]) % 5)[None, :]
-        out.append(jnp.where(line[None], rep[:, None, :], 0.0))
-    return jnp.concatenate(out, axis=1).astype(u.dtype)
-
-
-def lines_wide(g):
-    return g.reshape(g.shape[0], 5, 128)
-
-
-def lines_narrow(g):
-    def pad(v, lo, hi):
-        return jnp.pad(v, ((0, 0), (lo, hi)))
-
-    a = [g[:, :128], pad(g[:, 128:], 0, 96), pad(g[:, 96:], 0, 64), pad(g[:, 64:], 0, 32), g[:, 32:]]
-    b = [jnp.zeros_like(g[:, :128]), pad(g[:, :96], 32, 0), pad(g[:, :64], 64, 0), pad(g[:, :32], 96, 0)]
-    return jnp.stack(a + b + [b[0]], axis=1)
-
-
-def fold_narrow(y):
-    def pad(v, lo, hi):
-        return jnp.pad(v, (lo, hi))
-
-    return (
-        pad(y[0], 0, 32) + pad(y[1, :32], 128, 0) + pad(y[2, :64], 96, 0) + pad(y[3, :96], 64, 0) + pad(y[4], 32, 0)
-        + pad(y[6, 32:], 0, 64) + pad(y[7, 64:], 0, 96) + pad(y[8, 96:], 0, 128)
-    )
-
-
-def extend(u, length):
-    one = jnp.ones((u.shape[0], 1), u.dtype)
-    rest = jnp.zeros((u.shape[0], length - u.shape[1] - 1), u.dtype)
-    return jnp.concatenate([u, one, rest], axis=1)
-
-
-def time_forward(part, steps):
+FE, FU1, FU2, FD1, FD2, FD3, FL = 0, 3, 13, 23, 28, 33, 35
+FACTS = 40
+
+
+def time_rows_kernel(first, facts, out):
+    count = out.shape[0]
+    row = first[0, 0] + lax.broadcasted_iota(jnp.int32, (count, 1), 0)
+
+    def wide(at, n):
+        return jnp.concatenate([facts[:, at + i, :] for i in range(n)], axis=1)
+
+    def meets(u, k):
+        spot = jnp.where(k == lax.broadcasted_iota(jnp.int32, (1, u.shape[1]), 1), 1.0, 0.0).astype(BF)
+        return nt(spot, u.astype(BF))
+
+    total = jnp.zeros((count, 128), F32)
+    for u, at, start, size in ((wide(FE, 3)[:, :D], FD1, T1, D), (wide(FU1, 10), FD2, T2, 4 * D)):
+        rel = row - start
+        k, line = rel // 5, rel % 5
+        met = meets(u, jnp.where(rel < 0, -1, k))
+        for j in range(5):
+            g = facts[:, at + j, :]
+            total += nn(jnp.where(line == j, met, 0.0).astype(BF), g.astype(BF))
+            total += jnp.where((rel >= 0) & (k == size) & (line == j), colsum(g), 0.0)
+    rel = row - T3
+    group, line = rel // 5, rel % 5
+    d3 = wide(FD3, 2)[:, :W]
+    zero = jnp.zeros((d3.shape[0], 128), F32)
+    u = wide(FU2, 10)
+    for picks, shift in ((FIRST, 0), (SECOND, 1)):
+        k = jnp.full_like(rel, -1)
+        for j in range(5):
+            k = jnp.where((rel >= 0) & (line == j), 4 * group + picks[j], k)
+        met = meets(u, k)
+        for j in range(5):
+            if shift == 0:
+                lo = (0, 128, 96, 64, 32)[j]
+                g = d3[:, lo : min(lo + 128, W)]
+                g = jnp.concatenate([g, zero[:, : 128 - g.shape[1]]], axis=1) if g.shape[1] < 128 else g
+            else:
+                if j in (0, 4):
+                    continue
+                g = jnp.concatenate([zero[:, : 32 * j], d3[:, : 128 - 32 * j]], axis=1)
+            total += nn(jnp.where(line == j, met, 0.0).astype(BF), g.astype(BF))
+            total += jnp.where((k == 4 * D) & (line == j), colsum(g), 0.0)
+    out[...] = total
+
+
+ROWS = 856
+SLAB = 864
+SOME = 240
+CUT = 736
+
+
+def send(src, dst, sems, i, j, target):
+    copy = pltpu.make_async_remote_copy(
+        src_ref=src, dst_ref=dst, send_sem=sems[0].at[i], recv_sem=sems[1].at[j],
+        device_id={DP: target}, device_id_type=pl.DeviceIdType.MESH,
+    )
+    copy.start()
+    return copy
+
+
+PIECES = tuple(slice(16 * a, 16 * b) for a, b in ((0, 7), (7, 14), (14, 21), (21, 28), (28, 35), (35, 42), (42, 48), (48, 54)))
+
+
+def gather_kernel(low, g0, g1, send_sem, recv_sem, keep_sem):
+    me, y = lax.axis_index(DP), lax.axis_index(CH)
+    k, x, z = me % 2, (me // 2) % 2, me // 4
+    core = {DP: me + 1 - 2 * k}
+    side = {DP: me + 2 - 4 * x}
+    other = {CH: 1 - y}
+    ring = [{DP: (me + 4 * o) % 16} for o in range(4)]
+    barrier = pltpu.get_barrier_semaphore()
+    for target in [core, side, other] + ring[1:]:
+        pl.semaphore_signal(barrier, inc=1, device_id=target, device_id_type=pl.DeviceIdType.MESH)
+    pl.semaphore_wait(barrier, 6)
+    count = [0]
+    started = []
+
+    def push(ref, target):
+        i = count[0]
+        count[0] += 1
+        return [start(ref, ref, i, i, target)]
+
+    def start(src, dst, i, j, target):
+        copy = pltpu.make_async_remote_copy(
+            src_ref=src, dst_ref=dst, send_sem=send_sem.at[i], recv_sem=recv_sem.at[j],
+            device_id=target, device_id_type=pl.DeviceIdType.MESH,
+        )
+        copy.start()
+        started.append(copy)
+        return copy
+
+    def push_ring(ref):
+        i = count[0]
+        count[0] += 3
+        return [start(ref, ref, i + o - 1, i + 3 - o, ring[o]) for o in (2, 1, 3)]
+
+    def arrive(copies):
+        for copy in copies:
+            copy.wait_recv()
+
+    keeps = []
+    for p, g in enumerate((g0, g1)):
+        keep = pltpu.make_async_copy(low.at[p], g.at[y, z, x, k], keep_sem.at[p])
+        keep.start()
+        keeps.append(keep)
+    work = [(p, g, rows, i % 2) for p, g in enumerate((g0, g1)) for i, rows in enumerate(PIECES)]
+    first, second, third, last = {}, {}, {}, []
+
+    def begin(i):
+        p, g, rows, _ = work[i]
+        if i % len(PIECES) == 0:
+            keeps[p].wait()
+        first[i] = push_ring(g.at[y, z, x, k, rows])
+
+    def middle(i):
+        _, g, rows, turn = work[i]
+        arrive(first[i])
+        second[i] = push(g.at[y, :, x, k, rows], other if turn else side)
+        last.extend(push(g.at[y, :, x, k, rows], core))
+
+    def finish(i):
+        _, g, rows, turn = work[i]
+        arrive(second[i])
+        if turn:
+            third[i] = push(g.at[:, :, x, k, rows], side)
+            last.extend(push(g.at[1 - y, :, x, k, rows], core))
+        else:
+            third[i] = push(g.at[y, :, :, k, rows], other)
+            last.extend(push(g.at[y, :, 1 - x, k, rows], core))
+
+    def pass_on(i):
+        _, g, rows, turn = work[i]
+        arrive(third[i])
+        last.extend(push(g.at[:, :, 1 - x, k, rows] if turn else g.at[1 - y, :, :, k, rows], core))
+
+    ahead = 4
+    for i in range(ahead):
+        begin(i)
+    for i in range(len(work) + 2):
+        if i < len(work):
+            middle(i)
+            if i + ahead < len(work):
+                begin(i + ahead)
+        if 0 <= i - 1 < len(work):
+            finish(i - 1)
+        if 0 <= i - 3 < len(work):
+            pass_on(i - 3)
+    pass_on(len(work) - 1)
+    arrive(last)
+    for copy in started:
+        copy.wait_send()
+
+
+def gather_weights(low):
+    hbm = pl.BlockSpec(memory_space=pl.ANY)
+    whole = sds((2, 4, 2, 2, SLAB, 128), BF)
+    dma = pltpu.SemaphoreType.DMA
+    return pl.pallas_call(
+        gather_kernel,
+        out_shape=(whole, whole),
+        in_specs=[hbm],
+        out_specs=(hbm, hbm),
+        scratch_shapes=[dma((128,)), dma((128,)), dma((2,))],
+        compiler_params=pltpu.CompilerParams(collective_id=2, has_side_effects=True),
+    )(low)
+
+
+def add_up(*terms):
+    total = terms[0].astype(F32)
+    for term in terms[1:]:
+        total += term.astype(F32)
+    return total
+
+
+def reduce_kernel(
+    p1, p0, facts, sum1, sum0, all_facts,
+    r1, sa, sb, rax, rbz, ta, raz, tb, rbx, some, land, fx, send_sem, recv_sem, fsend, frecv, gsend, grecv,
+):
+    me = lax.axis_index(DP)
+    k, x, z = me % 2, (me // 2) % 2, me // 4
+    barrier = pltpu.get_barrier_semaphore()
+    for o in range(1, 16):
+        pl.semaphore_signal(barrier, inc=1, device_id={DP: (me + o) % 16}, device_id_type=pl.DeviceIdType.MESH)
+    pl.semaphore_wait(barrier, 15)
+    sems = (send_sem, recv_sem)
+    core = me + 1 - 2 * k
+    side = me + 2 - 4 * x
+    other = 1 - k
+    first = [
+        send(p1.at[other, :, :CUT], r1.at[:, :CUT], sems, 0, 0, core),
+        send(p1.at[other, :, CUT:], r1.at[:, CUT:SLAB], sems, 1, 1, core),
+        send(p0.at[other], r1.at[:, SLAB:], sems, 2, 2, core),
+    ]
+    fact_copies = [send(facts, fx.at[me], (fsend, frecv), o - 1, o - 1, (me + o) % 16) for o in range(1, 16)]
+    first[0].wait_recv()
+    for m in range(8):
+        sa[m % 2, m // 2] = add_up(p1[k, m, :CUT], r1[m, :CUT]).astype(BF)
+    ax = send(sa.at[1 - x], rax, sems, 3, 3, side)
+    first[1].wait_recv()
+    first[2].wait_recv()
+    for m in range(8):
+        sb[m // 2, m % 2, : SLAB - CUT] = add_up(p1[k, m, CUT:], r1[m, CUT:SLAB]).astype(BF)
+        sb[m // 2, m % 2, SLAB - CUT :] = add_up(p0[k, m], r1[m, SLAB:]).astype(BF)
+    bz = [send(sb.at[(z + o) % 4], rbz.at[3 - o], sems, 3 + o, 7 - o, (me + 4 * o) % 16) for o in (2, 1, 3)]
+    ax.wait_recv()
+    for m in range(4):
+        ta[m] = add_up(sa[x, m], rax[m]).astype(BF)
+    az = [send(ta.at[(z + o) % 4], raz.at[3 - o], sems, 6 + o, 10 - o, (me + 4 * o) % 16) for o in (2, 1, 3)]
+    for copy in bz:
+        copy.wait_recv()
+    for m in range(2):
+        tb[m] = add_up(sb[z, m], rbz[0, m], rbz[1, m], rbz[2, m]).astype(BF)
+    bx = send(tb.at[1 - x], rbx, sems, 10, 10, side)
+    bx.wait_recv()
+    last = add_up(tb[x], rbx[...])
+    sum1[CUT:, :] = last[: 856 - CUT]
+    some[...] = last[SLAB - CUT :]
+    fx[me] = facts[...]
+
+    @pl.when(me > 0)
+    def _():
+        @pl.loop(0, SOME // 8)
+        def _(g):
+            row = SOME * me + 8 * g
+            owner = row // ROWS
+            at = pl.multiple_of(row - ROWS * owner, 8)
+            pltpu.make_async_remote_copy(
+                src_ref=some.at[pl.ds(pl.multiple_of(8 * g, 8), 8)], dst_ref=land.at[pl.ds(at, 8)],
+                send_sem=gsend, recv_sem=grecv, device_id={DP: owner}, device_id_type=pl.DeviceIdType.MESH,
+            ).start()
+
+    for copy in az:
+        copy.wait_recv()
+    sum1[:CUT, :] = add_up(ta[z], raz[0], raz[1], raz[2])
+    for copy in fact_copies:
+        copy.wait_recv()
+    all_facts[...] = fx[...]
+
+    def landed(lo, hi):
+        part = land.at[lo:hi]
+        pltpu.make_async_remote_copy(
+            src_ref=part, dst_ref=part, send_sem=gsend, recv_sem=grecv,
+            device_id={DP: me}, device_id_type=pl.DeviceIdType.MESH,
+        ).wait_recv()
+        sum0[lo:hi, :] = land[lo:hi, :]
+
+    @pl.when(me == 0)
+    def _():
+        landed(SOME, ROWS)
+        sum0[:SOME, :] = some[...]
+
+    @pl.when((me > 0) & (me < 4))
+    def _():
+        landed(0, ROWS)
+
+    @pl.when(me == 4)
+    def _():
+        landed(0, 16 * SOME - 4 * ROWS)
+        sum0[16 * SOME - 4 * ROWS :, :] = jnp.zeros((5 * ROWS - 16 * SOME, 128), F32)
+
+    @pl.when(me > 4)
+    def _():
+        sum0[...] = jnp.zeros_like(sum0)
+
+    @pl.when(me > 0)
+    def _():
+        pltpu.make_async_remote_copy(
+            src_ref=some, dst_ref=some, send_sem=gsend, recv_sem=grecv,
+            device_id={DP: me}, device_id_type=pl.DeviceIdType.MESH,
+        ).wait_send()
+
+    for copy in first + [ax] + bz + az + [bx] + fact_copies:
+        copy.wait_send()
+
+
+def sum_over_samples(p1, p0, facts):
+    vm = pl.BlockSpec(memory_space=pltpu.VMEM)
+    dma = pltpu.SemaphoreType.DMA
+    return pl.pallas_call(
+        reduce_kernel,
+        out_shape=(sds((ROWS, 128)), sds((ROWS, 128)), sds((16, FACTS, 128))),
+        in_specs=[vm] * 3,
+        out_specs=(vm,) * 3,
+        scratch_shapes=[
+            pltpu.VMEM((8, SLAB + SOME, 128), BF),
+            pltpu.VMEM((2, 4, CUT, 128), BF),
+            pltpu.VMEM((4, 2, SLAB + SOME - CUT, 128), BF),
+            pltpu.VMEM((4, CUT, 128), BF),
+            pltpu.VMEM((3, 2, SLAB + SOME - CUT, 128), BF),
+            pltpu.VMEM((4, CUT, 128), BF),
+            pltpu.VMEM((3, CUT, 128), BF),
+            pltpu.VMEM((2, SLAB + SOME - CUT, 128), BF),
+            pltpu.VMEM((SLAB + SOME - CUT, 128), BF),
+            pltpu.VMEM((SOME, 128), F32),
+            pltpu.VMEM((ROWS, 128), F32),
+            pltpu.VMEM((16, FACTS, 128), F32),
+            dma((11,)),
+            dma((11,)),
+            dma((15,)),
+            dma((15,)),
+            dma,
+            dma,
+        ],
+        compiler_params=pltpu.CompilerParams(
+            collective_id=1, has_side_effects=True, vmem_limit_bytes=40 * 2**20
+        ),
+    )(p1, p0, facts)
+
+
+def time_features(steps):
     ladder = jnp.arange(D // 2, dtype=F32)
     freq = jnp.exp(-math.log(10000.0) * ladder / (D // 2))
     angles = steps.astype(F32)[:, None] * freq[None, :]
-    e = jnp.concatenate([jnp.cos(angles), jnp.sin(angles)], axis=1).astype(BF)
-
-    def wide(u, start):
-        lines = spread_wide(extend(u, u.shape[1] + 1), 5)[0]
-        rows = part[:, start : start + lines.shape[1]]
-        return jnp.einsum("jr,brl->bjl", lines, rows, preferred_element_type=F32).reshape(1, -1)
-
-    p1 = wide(e, T1)
-    u1 = silu(p1).astype(BF)
-    p2 = wide(u1, T2)
-    u2 = silu(p2).astype(BF)
-    lines = spread_narrow(extend(u2, u2.shape[1] + 4))[0]
-    y = jnp.einsum("jr,brl->bjl", lines, part[:, T3 : T3 + lines.shape[1]], preferred_element_type=F32)
-    tv = jnp.concatenate([fold_narrow(y[0]), fold_narrow(y[1])])[None, :]
-    return tv, (e, u1, u2, p1, p2)
-
-
-def time_backward(part, kept, dtv):
-    e, u1, u2, p1, p2 = kept
-    count = 4 * D
-    g3 = dtv.astype(BF)
-    lines = jnp.concatenate([lines_narrow(g3[:, :W]), lines_narrow(g3[:, W:])], axis=0)
-    y = jnp.einsum("brl,bjl->rj", part[:, T3 : T3 + 5 * count // 4], lines, preferred_element_type=F32)
-    y = y.reshape(count // 4, 5, 10)
-    cols = [0.0] * 4
-    for j in range(5):
-        cols[FIRST[j]] += y[:, j, j]
-        cols[SECOND[j]] += y[:, j, 5 + j]
-    du2 = jnp.stack(cols, axis=1).reshape(1, count)
-    d2 = du2 * silu_slope(p2)
-    g2 = d2.astype(BF).reshape(2, 5, 128)
-    y = jnp.einsum("brl,bjl->rj", part[:, T2 : T2 + 5 * count], g2, preferred_element_type=F32)
-    y = y.reshape(count, 5, 5)
-    du1 = jnp.sum(jnp.where(jnp.eye(5, dtype=bool)[None], y, 0.0), axis=(1, 2)).reshape(1, count)
-    d1 = du1 * silu_slope(p1)
-    return d1, d2, dtv
-
-
-def time_rows(e, u1, u2, d1, d2, d3, first, count):
-    total = jnp.zeros((count, 128), F32)
-
-    def add(total, lines, grads, start):
-        room = lines.shape[2]
-        flat = lines.reshape(-1, room)
-        flat = jnp.pad(flat, ((0, 0), (start, 0)))
-        flat = jnp.pad(flat, ((0, 0), (0, max(0, 128 * 112 - flat.shape[1]))))
-        mine = lax.dynamic_slice_in_dim(flat, first, count, 1)
-        return total + jnp.einsum(
-            "kr,kl->rl", mine, grads.reshape(-1, 128), precision=HI, preferred_element_type=F32
-        )
-
-    def parts(u, length):
-        zero = jnp.zeros_like(u)
-        weights = jnp.concatenate([u, jnp.zeros((u.shape[0], length - u.shape[1]), u.dtype)], axis=1)
-        biases = jnp.concatenate([zero, jnp.ones((u.shape[0], 1), u.dtype)], axis=1)
-        biases = jnp.pad(biases, ((0, 0), (0, length - biases.shape[1])))
-        return weights.astype(F32), biases.astype(F32)
-
-    for u, g, start in ((e, d1, T1), (u1, d2, T2)):
-        w, b = parts(u, u.shape[1] + 1)
-        total = add(total, spread_wide(w, 5), lines_wide(g.astype(BF).astype(F32)), start)
-        total = add(total, spread_wide(b, 5), lines_wide(g), start)
-    w, b = parts(u2, u2.shape[1] + 4)
-    total = add(total, spread_narrow(w), lines_narrow(d3.astype(BF).astype(F32)), T3)
-    total = add(total, spread_narrow(b), lines_narrow(d3), T3)
-    return total
+    return jnp.concatenate([jnp.cos(angles), jnp.sin(angles)], axis=1)
+
+
+def rounded_silu(v):
+    return silu(v).astype(BF).astype(F32)
 
 
 def alpha_bar(step_ids):
@@ -846,9 +1101,13 @@
     n_dp = lax.axis_size(DP)
     rows_dev = params.shape[2]
     rows_all = rows_dev * n_dp
-    low = params.astype(BF)
-    part0 = lax.all_gather(lax.all_gather(low[:, 0], CH, axis=0, tiled=True), DP, axis=1, tiled=True)
-    part1 = lax.all_gather(lax.all_gather(low[:, 1], CH, axis=0, tiled=True), DP, axis=1, tiled=True)
+    quick = n_dp == 16 and rows_dev == ROWS
+    low = params[0].astype(BF)
+    if quick:
+        part0, part1 = gather_weights(jnp.pad(low, ((0, 0), (0, SLAB - ROWS), (0, 0))))
+        part0, part1 = part0.reshape(2, 16, SLAB, 128), part1.reshape(2, 16, SLAB, 128)
+    else:
+        part0, part1 = (lax.all_gather(lax.all_gather(low[i], CH, axis=0), DP, axis=1) for i in range(2))
 
     alpha = alpha_bar(timesteps)[:, None]
     noise = noise_eps[0]
@@ -856,21 +1115,26 @@
     mask = pixel_mask.astype(F32)
 
     px = (N, D)
+    hp = (N, W)
     hx = (HEADS, N, HD)
     sh = (3, N + 2 * SIDE, D)
-    win, w1, vec0 = kcall(
-        unpack0_kernel,
-        (sds((36, D), BF), sds((9, D, D), BF), sds((8, D))),
-        (part0[:, :R0],),
-        (pltpu.VMEM((2, 400, 128), F32), pltpu.VMEM((3, 4 * R0 // 5, 128), F32)),
+    e = time_features(timesteps)
+    flat = pltpu.VMEM((2, rows_all, 128), F32)
+    unrolled = pltpu.VMEM((3, 4 * R1 // 5, 128), F32)
+    units = sds((8, 4 * D))
+    win, w1, vec0, tw2, tw3, tv, p1, p2 = kcall(
+        partial(unpack0_kernel, rows_dev),
+        (sds((36, D), BF), sds((9, D, D), BF), sds((8, D)), sds((4, 4 * D, D), BF), sds((4 * D, D), BF), sds((1, D)))
+        + (units, units),
+        (part0, jnp.broadcast_to(e, (8, D))),
+        (flat, unrolled),
     )
     mats, kvw, vec1, gib, wout, outb = kcall(
-        unpack1_kernel,
+        partial(unpack1_kernel, rows_dev),
         (sds((NMAT, D, D), BF), sds((2, CTX, D), BF), sds((24, D)), sds((8, D)), sds((36, D), BF), sds((1, D))),
-        (part1[:, :R1],),
-        (pltpu.VMEM((2, 400, 128), F32), pltpu.VMEM((3, 4 * R1 // 5, 128), F32), pltpu.VMEM((2, 40, 128), F32)),
-    )
-    tv, kept = time_forward(part0, timesteps)
+        (part1,),
+        (flat, unrolled, pltpu.VMEM((2, 40, 128), F32)),
+    )
     h0, h1, h2, z0, a1, a2, ntr, x1, q, k, v, stats = kcall(
         front_kernel,
         (sds(px),) * 4 + (sds(px, BF),) * 4 + (sds(hx, BF),) * 3 + (sds((8, D)),),
@@ -890,8 +1154,8 @@
     )
     dh3, dz1, dh3b, dz3b, dab, dgb, dz2b, dqc, dz1b, dos, dkv, dvec_a, dgib, dwout, dbout = kcall(
         back_one_kernel,
-        (sds(px),) * 2 + (sds(px, BF),) * 2 + (sds((4, N, D), BF),) * 2 + (sds(px, BF),) * 3
-        + (sds(hx, BF), sds((2, TXT, D), BF), sds((24, D)), sds((8, D)), sds((36, D)), sds((8, 128))),
+        (sds(px),) * 2 + (sds(hp, BF),) * 2 + (sds((4, N, W), BF),) * 2 + (sds(hp, BF),) * 3
+        + (sds(hx, BF), sds((2, TXT, W), BF), sds((24, D)), sds((8, D)), sds((36, D)), sds((8, 128))),
         (derr, h3, stats_out, a3, z1, z2, x3, qc, kc, vc, mats, vec1, gib, wout),
         (
             pltpu.VMEM(px, F32),
@@ -909,59 +1173,54 @@
     )
     dz0b, g2, g1, dh0b, dvec0, dvec_b, dtv = kcall(
         back_two_kernel,
-        (sds(px, BF), sds(sh, BF), sds(sh, BF), sds(px, BF), sds((8, D)), sds((24, D)), sds((1, D))),
+        (sds(hp, BF), sds(sh[:2] + (W,), BF), sds(sh[:2] + (W,), BF), sds(hp, BF), sds((8, D)), sds((24, D)), sds((1, D))),
         (dq, dk, dv, dz1, dh3, z0, h2, h1, h0, stats, w1, mats, vec0, vec1),
-        (pltpu.VMEM(px, F32), pltpu.VMEM(px, F32)),
-    )
-    which = jnp.full((1, 1), c, jnp.int32)
-    flat1 = kcall(
+        (pltpu.VMEM(px, F32), pltpu.VMEM(px, F32), pltpu.VMEM(sh, BF), pltpu.VMEM(sh, BF)),
+    )
+    step = 16 * n_dp
+    front = -(-FRONT // step) * step
+    lead = (2, 8) if quick else (n_dp,)
+    own1 = kcall(
         grads1_kernel,
-        sds((R1, 128), BF),
-        (which, a2, g2, ntr, dz0b, x1, dq, dk, dv, o, dz1b, x2, dqc, context[0], dkv, oc, dz2b,
+        sds(lead + (SLAB if quick else rows_dev, 128), BF),
+        (a2, g2, ntr, dz0b, x1, dq, dk, dv, o, dz1b, x2, dqc, context[0], dkv, oc, dz2b,
          x3, dab, dgb, gl, dz3b, z3b, dh3b, dvec_a + dvec_b, dgib, dwout, dbout),
         (
             pltpu.VMEM((2, 4 * R1 // 5, 128), F32),
-            pltpu.VMEM((400, 128), F32),
-            pltpu.VMEM((3, N + 2 * SIDE, W), BF),
+            pltpu.VMEM((7600, 128), F32),
             pltpu.VMEM((2, 40, 128), F32),
         ),
     )
-    flat0 = kcall(
+    own0 = kcall(
         grads0_kernel,
-        sds((R0, 128), BF),
-        (which, noisy, a1, g1, dh0b, dvec0),
+        sds(lead + (front // n_dp, 128), BF),
+        (noisy, a1, g1, dh0b, dvec0),
         (
             pltpu.VMEM((2, 4 * R0 // 5, 128), F32),
-            pltpu.VMEM((400, 128), F32),
-            pltpu.VMEM((3, N + 2 * SIDE, W), BF),
+            pltpu.VMEM((2600, 128), F32),
         ),
     )
-    d1, d2, d3 = time_backward(part0, kept, dtv)
-    mine = [lax.dynamic_slice_in_dim(g, c * (g.shape[1] // 2), g.shape[1] // 2, 1) for g in (d1, d2, d3)]
-    facts = [f.astype(F32) for f in kept[:3]] + mine
-    sizes = [f.shape[1] for f in facts]
-    everyone = lax.all_gather(jnp.concatenate(facts, axis=1), DP, axis=0, tiled=True)
-    facts = []
-    at = 0
-    for size in sizes:
-        facts.append(everyone[:, at : at + size])
-        at += size
-    grad0 = time_rows(*facts, d * rows_dev, rows_dev)
-
-    step = 16 * n_dp
-    front = -(-FRONT // step) * step
-    flat1 = jnp.pad(flat1, ((0, rows_all - R1), (0, 0)))
-    keep = jnp.arange(front)[:, None] < FRONT
-    flat0 = jnp.pad(flat0, ((0, max(0, front - R0)), (0, 0)))[:front]
-    flat0 = jnp.where(keep, flat0, 0.0).astype(BF)
-    sum1 = lax.psum_scatter(flat1, DP, scatter_dimension=0, tiled=True).astype(F32)
-    some0 = lax.psum_scatter(flat0, DP, scatter_dimension=0, tiled=True)
-    sum0 = lax.all_gather(some0, DP, axis=0, tiled=True)
-    sum0 = jnp.pad(sum0, ((0, rows_all - front), (0, 0)))
-    sum0 = lax.dynamic_slice_in_dim(sum0, d * rows_dev, rows_dev, 0).astype(F32)
+    d1, d2 = kcall(time_back_kernel, (units, units), (dtv, tw2, tw3, p1, p2))
+    mine = [lax.dynamic_slice_in_dim(g[0], c * (g.shape[1] // 2), g.shape[1] // 2, 0) for g in (d1, d2, dtv)]
+    e, u1, u2 = e[0].astype(BF).astype(F32), rounded_silu(p1[0]), rounded_silu(p2[0])
+    facts = jnp.concatenate(
+        [e, jnp.zeros((64,), F32), u1, u2, *mine, jnp.zeros((96,), F32), loss[0], jnp.sum(mask, axis=1)]
+    )
+    facts = jnp.pad(facts, (0, FACTS * 128 - facts.shape[0])).reshape(FACTS, 128)
+    if quick:
+        sum1, sum0, all_facts = sum_over_samples(own1, own0, facts)
+    else:
+        sum1 = lax.psum_scatter(own1, DP, scatter_dimension=0).astype(F32)
+        sum0 = lax.all_gather(lax.psum_scatter(own0, DP, scatter_dimension=0), DP, axis=0, tiled=True)
+        sum0 = jnp.pad(sum0, ((0, rows_all - front), (0, 0)))
+        sum0 = lax.dynamic_slice_in_dim(sum0, d * rows_dev, rows_dev, 0).astype(F32)
+        all_facts = lax.all_gather(facts, DP, axis=0)
+    grad0 = kcall(
+        time_rows_kernel, sds((rows_dev, 128)), (jnp.full((1, 1), d * rows_dev, jnp.int32), all_facts)
+    )
     grad = jnp.stack([grad0 + sum0, sum1])[None]
-
-    loss_sum, pixel_count = lax.psum((loss[0, 0], jnp.sum(mask)), DP)
+    loss_sum = jnp.sum(all_facts[:, FL, 0])
+    pixel_count = jnp.sum(all_facts[:, FL, 1])
     scaled = grad / (LAT * jnp.maximum(pixel_count, 1.0))
     new_momentum = MU * momentum + scaled
     new_params = params - LR * (scaled + MU * new_momentum)

time: 575 us -> 432 us (0.75)
  Pallas kernels: 251 us -> 398 us
  waiting for transfers between devices: 101 us -> 0 us
  blocking collectives: 87.5 us -> 0 us
  local copies, waits for them, and re-layouts: 68.2 us -> 11.8 us
  matrix products: 17.6 us -> 0 us
  between operations: 17.6 us -> 3.75 us
  other arithmetic: 24.7 us -> 11 us
    pallas_call x0 -> x2, Pallas kernels: none -> 130 us  [the longest x1 85.1 us: gather_weights(): pl.pallas_call(gather_kernel, out_shape=(whole, whole), in_specs=[hbm], o...]
    all_gather x2 -> x0, waiting for transfers between devices: 97 us -> none  [the longest x1 54.9 us: shards(): lax.all_gather(lax.all_gather(low[:, 1], CH, axis=0, tiled=True), DP, axi...]
    all_gather x4 -> x0, blocking collectives: 57.8 us -> none  [the longest x1 23.5 us: shards(): sum0 = lax.all_gather(some0, DP, axis=0, tiled=True)]
    psum x1 -> x0, blocking collectives: 29.7 us -> none  [shards(): loss_sum, pixel_count = lax.psum((loss[0, 0], jnp.sum(mask)), DP)]
    broadcast_in_dim x25 -> x3, local copies, waits for them, and re-layouts: 28.4 us -> 0.61 us  [the longest x1 0.6 us: shards(): jnp.broadcast_to(e, (8, D))]
    dot_general x11 -> x0, matrix products: 17.6 us -> none  [the longest x6 7.44 us: add(): jnp.einsum('kr,kl->rl', mine, grads.reshape(-1, 128), precision=HI, prefe...]
    pallas_call x10 -> x12, Pallas kernels: 251 us -> 268 us  [kcall(): pl.pallas_call(body, out_shape=outs, in_specs=[vm] * len(ins), out_specs=...]
    slice x18 -> x5, local copies, waits for them, and re-layouts: 15.3 us -> 3.24 us  [the longest x2 1.56 us: shards(): g[0]]
  transfers between devices with their start and end apart: 4 -> 0, of which waited for: 3 -> 0; matrix products, arithmetic and copies ran while one was open for 14% -> 0% of each run, Pallas kernels for 4% -> 0%
where the time goes in v1:
time: 432 us; the launch traced here: 425 us
  Pallas kernels  398 us (92%)
  local copies, waits for them, and re-layouts  11.8 us (3%)
  other arithmetic  11 us (3%)
    pallas_call x12, Pallas kernels, kcall(): pl.pallas_call(body, out_shape=outs, in_specs=[vm] * len(ins), out_specs=...  268 us
    pallas_call x1, Pallas kernels, gather_weights(): pl.pallas_call(gather_kernel, out_shape=(whole, whole), in_specs=[hbm], o...  85.1 us
    pallas_call x1, Pallas kernels, sum_over_samples(): pl.pallas_call(reduce_kernel, out_shape=(sds((ROWS, 128)), sds((ROWS, 128...  45.3 us

profile of v1, /device:TPU:1, one launch (start us, length us, event | category | flops | bytes accessed | tf_op | source)
XLA Modules:
  0.0 424.6 jit_solution(4119647730296426237)
XLA Ops:
  2.0 1.2 convert_bitcast_fusion
  3.3 0.8 pad.12.low
  4.1 85.1 %shard_map.119 = (bf16[2,4,2,2,864,128]{5,4,3,2,1,0:T(8,128)(2,1)}, bf16[2,4,2,2,864,128]{5,4,3,2,1,0:T(8,128)(2,1)}) custom-call(bf16[2,864,128]{2,1,0:T(8,128)(2,1)} %pad.12.low), custom_call_target="tpu_custom_call" | custom-call | tf_op jit(solution)/shard_map/pallas_call | solution.py:926
  89.2 15.1 %shard_map.120 = (bf16[36,320]{1,0:T(8,128)(2,1)}, bf16[9,320,320]{2,1,0:T(8,128)(2,1)}, f32[8,320]{1,0:T(8,128)}, bf16[4,1280,320]{2,1,0:T(8,128)(2,1)}, bf16[1...) custom-call(bf16[2,16,864,128]{3,2,1,0:T(8,128)(2,1)} %bitcast.25, ...), custom_call_target="tpu_custom_call" | custom-call | tf_op jit(solution)/shard_map/pallas_call | solution.py:60
  104.3 15.6 %shard_map.121 = (bf16[29,320,320]{2,1,0:T(8,128)(2,1)}, bf16[2,768,320]{2,1,0:T(8,128)(2,1)}, f32[24,320]{1,0:T(8,128)}, f32[8,320]{1,0:T(8,128)}, bf16[36,320]{1,0:T(8,128)(2,1)}, /*index=5*/f32[1,320]{1,0:T(1,128)}) custom-call(bf16[2,16,864,128]{3,2,1,0:T(8,128)(2,1)} %bitcast.24), custom_call_target="tpu_custom_call" | custom-call | tf_op jit(solution)/shard_map/pallas_call | solution.py:60
  123.1 29.1 %shard_map.122 = (f32[1024,320]{1,0:T(8,128)}, f32[1024,320]{1,0:T(8,128)}, f32[1024,320]{1,0:T(8,128)}, f32[1024,320]{1,0:T(8,128)}, bf16[1024,320]{1,0:T(8,128...) custom-call(f32[4,1024]{1,0:T(4,128)} %bitcast_add_fusion.noisy, ...), custom_call_target="tpu_custom_call" | custom-call | tf_op jit(solution)/shard_map/pallas_call | solution.py:60
  152.2 31.0 %shard_map.123 = (bf16[1024,320]{1,0:T(8,128)(2,1)}, f32[8,1,1024]{2,1,0:T(1,128)}) custom-call(bf16[8,1024,40]{2,1,0:T(8,128)(2,1)} %get-tuple-element.89.q, bf16[8,1024,40]{2,1,0:T(8,128)(2,1)} %get-tuple-element.90.k, bf16[8,1024,40]{2,1,0:T(8,128)(2,1)} %get-tuple-element.91.v), custom_call_target="tpu_custom_call" | custom-call | tf_op jit(solution)/shard_map/pallas_call | solution.py:60
  183.8 31.7 %shard_map.124 = (f32[1024,320]{1,0:T(8,128)}, f32[1024,320]{1,0:T(8,128)}, f32[1024,320]{1,0:T(8,128)}, bf16[1024,320]{1,0:T(8,128)(2,1)}, bf16[1024,320]{1,0:T...) custom-call(bf16[1024,320]{1,0:T(8,128)(2,1)} %get-tuple-element.92., ...), custom_call_target="tpu_custom_call" | custom-call | tf_op jit(solution)/shard_map/pallas_call | solution.py:60
  215.5 38.6 %shard_map.125 = (f32[1024,320]{1,0:T(8,128)}, f32[1024,320]{1,0:T(8,128)}, bf16[1024,160]{1,0:T(8,128)(2,1)}, bf16[1024,160]{1,0:T(8,128)(2,1)}, bf16[4,1024,16...) custom-call(f32[4,1024]{1,0:T(4,128)} %get-tuple-element.99.derr, ...), custom_call_target="tpu_custom_call" | custom-call | tf_op jit(solution)/shard_map/pallas_call | solution.py:60
  254.1 38.7 %shard_map.126 = (bf16[1024,320]{1,0:T(8,128)(2,1)}, bf16[1024,320]{1,0:T(8,128)(2,1)}, bf16[1024,320]{1,0:T(8,128)(2,1)}) custom-call(bf16[8,1024,40]{2,1,0:T(8,128)(2,1)} %get-tuple-element.89.q, bf16[8,1024,40]{2,1,0:T(8,128)(2,1)} %get-tuple-element.90.k, bf16[8,1024,40]{2,1,0:T(8,128)(2,1)} %get-tuple-element.91.v, ...), custom_call_target="tpu_custom_call" | custom-call | tf_op jit(solution)/shard_map/pallas_call | solution.py:60
  292.8 28.7 %shard_map.127 = (bf16[1024,160]{1,0:T(8,128)(2,1)}, bf16[3,1088,160]{2,1,0:T(8,128)(2,1)}, bf16[3,1088,160]{2,1,0:T(8,128)(2,1)}, bf16[1024,160]{1,0:T(8,128)(2...) custom-call(bf16[1024,320]{1,0:T(8,128)(2,1)} %get-tuple-element.111.dq, ...), custom_call_target="tpu_custom_call" | custom-call | tf_op jit(solution)/shard_map/pallas_call | solution.py:60
  321.5 4.7 %shard_map.130 = (f32[8,1280]{1,0:T(8,128)}, f32[8,1280]{1,0:T(8,128)}) custom-call(f32[1,320]{1,0:T(1,128)} %get-tuple-element.146.dtv, bf16[4,1280,320]{2,1,0:T(8,128)(2,1)} %get-tuple-element.147.tw2, bf16[1280,320]{1,0:T(8,128)(2,1)} %get-tuple-element.148.tw3, f32[8,1280]{1,0:T(8,128)} %get-tuple-element.144.p1, f32[8,1280]{1,0:T(8,128)} %get-tuple-element.145.p2), custom_call_target="tpu_custom_call" | custom-call | tf_op jit(solution)/shard_map/pallas_call | solution.py:60
  327.1 0.8 slice.33
  328.0 0.8 slice_reduce_fusion.3
  328.8 0.8 slice_reduce_fusion.2
  330.2 1.4 concatenate.14
  332.2 6.5 %shard_map.129.p0 = bf16[2,8,240,128]{3,2,1,0:T(8,128)(2,1)} custom-call(f32[4,1024]{1,0:T(4,128)} %bitcast_add_fusion.noisy, bf16[1024,320]{1,0:T(8,128)(2,1)} %get-tuple-element.140.a1, bf16[3,1088,160]{2,1,0:T(8,128)(2,1)} %get-tuple-element.141.g1, bf16[1024,160]{1,0:T(8,128)(2,1)} %get-tuple-element.142.dh0b, f32[8,320]{1,0:T(8,128)} %get-tuple-element.143.dvec), custom_call_target="tpu_custom_call" | custom-call | tf_op jit(solution)/shard_map/pallas_call | solution.py:60
  339.3 19.7 %shard_map.128.p1 = bf16[2,8,864,128]{3,2,1,0:T(8,128)(2,1)} custom-call(bf16[1024,320]{1,0:T(8,128)(2,1)} %get-tuple-element.88.a2, bf16[3,1088,160]{2,1,0:T(8,128)(2,1)} %get-tuple-element.119.g2, bf16[1024,320]{1,0:T(8,128)(2,1)} %get-tuple-element.120.ntr, bf16[1024,160]{1,0:T(8,128)(2,1)} %get-tuple-element.121.dz0b, ...), custom_call_target="tpu_custom_call" | custom-call | tf_op jit(solution)/shard_map/pallas_call | solution.py:60
  359.0 2.0 copy-done
  361.8 45.3 %shard_map.131 = (f32[856,128]{1,0:T(8,128)S(1)}, f32[856,128]{1,0:T(8,128)S(1)}, f32[16,40,128]{2,1,0:T(8,128)S(1)}) custom-call(bf16[2,8,864,128]{3,2,1,0:T(8,128)(2,1)S(1)} %copy-done, bf16[2,8,240,128]{3,2,1,0:T(8,128)(2,1)S(1)} %copy-done.1, f32[40,128]{1,0:T(8,128)S(1)} %copy-done.6), custom_call_target="tpu_custom_call" | custom-call | tf_op jit(solution)/shard_map/pallas_call | solution.py:1047
  409.2 8.2 %shard_map.132 = f32[856,128]{1,0:T(8,128)} custom-call(s32[1,1]{1,0:T(1,128)} %bitcast.first, f32[16,40,128]{2,1,0:T(8,128)} %copy-done.5), custom_call_target="tpu_custom_call" | custom-call | tf_op jit(solution)/shard_map/pallas_call | solution.py:60
  417.4 1.2 add_bitcast_fusion
  418.6 1.6 slice_reduce_fusion
  420.9 3.4 multiply_add_fusion
  (50 shorter events, 8.9 us)
Async XLA Ops:
  104.3 18.2 %copy-start.7 = (f32[1,4,1024]{2,1,0:T(4,128)S(1)}, f32[1,4,1024]{2,1,0:T(4,128)}, u32[]{:S(2)}) copy-start(f32[1,4,1024]{2,1,0:T(4,128)} %param.12) | copy-start | bytes 49156
  104.3 18.2 %copy-start.10 = (f32[1,4,1024]{2,1,0:T(4,128)S(1)}, f32[1,4,1024]{2,1,0:T(4,128)}, u32[]{:S(2)}) copy-start(f32[1,4,1024]{2,1,0:T(4,128)} %param.11) | copy-start | bytes 49156
  152.2 31.0 %copy-start.11 = (s32[1,1024]{1,0:T(1,128)S(1)}, s32[1,1024]{1,0:T(1,128)}, u32[]{:S(2)}) copy-start(s32[1,1024]{1,0:T(1,128)} %param.14) | copy-start | bytes 12292
  321.5 6.4 %copy-start.12 = (f32[1,320]{1,0:T(1,128)S(1)}, f32[1,320]{1,0:T(1,128)}, u32[]{:S(2)}) copy-start(f32[1,320]{1,0:T(1,128)} %get-tuple-element.146.dtv) | copy-start | bytes 3844
  327.9 10.8 %copy-start.8 = (f32[24,320]{1,0:T(8,128)S(1)}, f32[24,320]{1,0:T(8,128)}, u32[]{:S(2)}) copy-start(f32[24,320]{1,0:T(8,128)} %get-tuple-element.135) | copy-start | bytes 92164
  327.9 10.8 %copy-start.9 = (f32[24,320]{1,0:T(8,128)S(1)}, f32[24,320]{1,0:T(8,128)}, u32[]{:S(2)}) copy-start(f32[24,320]{1,0:T(8,128)} %get-tuple-element.136) | copy-start | bytes 92164
  339.3 19.7 %copy-start.1 = (bf16[2,8,240,128]{3,2,1,0:T(8,128)(2,1)S(1)}, bf16[2,8,240,128]{3,2,1,0:T(8,128)(2,1)}, u32[]{:S(2)}) copy-start(bf16[2,8,240,128]{3,2,1,0:T(8,128)(2,1)} %shard_map.129.p0) | copy-start | bytes 2949124
  359.0 2.0 copy-start
  361.0 0.7 copy-start.6
  407.0 0.8 copy-start.2
  407.8 0.8 copy-start.3
  408.5 0.7 copy-start.5
  409.2 11.6 %copy-start.4 = (f32[856,128]{1,0:T(8,128)S(1)}, f32[856,128]{1,0:T(8,128)}, u32[]{:S(2)}) copy-start(f32[856,128]{1,0:T(8,128)} %copy-done.3) | copy-start | bytes 1314820

commit v2 on v1

v2 whole, which is shorter than its diff:
```python
import math
from functools import partial

import jax
import jax.numpy as jnp
from jax import lax
from jax.experimental import pallas as pl
from jax.experimental.pallas import tpu as pltpu
from jax.sharding import PartitionSpec as P

D = 320
W = 160
HEADS = 8
HD = 40
CTX = 768
TXT = 77
LAT = 4
SIDE = 32
N = 1024
EPS = 1e-5
LR = 0.2
MU = 0.9
ED = 0.9
CH = "chan"
DP = "dp"
F32 = jnp.float32
BF = jnp.bfloat16
HI = lax.Precision.HIGHEST
SCALE = HD**-0.5
LOG2E = 1.0 / math.log(2.0)

R0 = 4000
U1, U2, U3 = 2920, 4204, 9328
FRONT = 3650
T1, T2, T3 = 3650, 5255, 11660
C2 = 2
PI = 2885
QKV = 3208
SO = 4168
CQ = 4491
CKV = 4811
CO = 6347
GI = 6670
GIB = 9230
GO = 9238
PO = 10519
OUT = 10842
OUTB = 10878
R1 = 13600
VEC0 = (36, 37, 38, 2919)
VEC1 = (0, 1, 2882, 2883, 2884, 3205, 3206, 3207, 4488, 4489, 4490, 6667, 6668, 6669, 10518, 10839, 10840, 10841)
(N2G, N2B, C2B, NTG, NTB, PIB, L1G, L1B, SOB, L2G, L2B, COB, L3G, L3B, GOB, POB, NOG, NOB) = range(18)
MPI, MQ, MK, MV = range(4)
MSO, MCQ, MCO, MPO, MGV, MGG, MGO = 0, 1, 2, 3, 4, 8, 12


def kcall(body, outs, ins, scratch=()):
    vm = pl.BlockSpec(memory_space=pltpu.VMEM)
    return pl.pallas_call(
        body,
        out_shape=outs,
        in_specs=[vm] * len(ins),
        out_specs=jax.tree.map(lambda _: vm, outs),
        scratch_shapes=list(scratch),
        compiler_params=pltpu.CompilerParams(vmem_limit_bytes=63 * 2**20),
    )(*ins)


def sds(shape, dtype=F32):
    return jax.ShapeDtypeStruct(shape, dtype)


def tiles(fn, size=256, total=N):
    for t in range(total // size):
        fn(pl.ds(t * size, size))


def nn(a, b):
    return jnp.dot(a, b, preferred_element_type=F32)


def nt(a, b):
    return lax.dot_general(a, b, (((1,), (1,)), ((), ())), preferred_element_type=F32)


def tn(a, b):
    return lax.dot_general(a, b, (((0,), (0,)), ((), ())), preferred_element_type=F32)


def colsum(v):
    return jnp.sum(v, axis=0, keepdims=True)


def unroll_rows(a_ref, flat, s_ref, chunks, rows):
    q = 80
    for b in range(2):
        for t in range(a_ref.shape[1]):
            flat[b, t * rows : (t + 1) * rows, :] = a_ref[b, t, :rows, :].astype(F32)

    @pl.loop(0, chunks)
    def _(c):
        f = [[flat[b, pl.ds(c * 5 * q + j, q, stride=5), :] for j in range(5)] for b in range(2)]
        for i in range(4):
            row = []
            for b in range(2):
                lo = 32 * i
                first, second = f[b][i], f[b][i + 1]
                row += [first[:, lo:], second[:, : lo + 32]] if lo else [first, second[:, :32]]
            full = jnp.concatenate(row, axis=1)
            for k, (lo, hi) in enumerate(((0, 128), (128, 256), (256, 320))):
                s_ref[k, pl.ds(c * 4 * q + i, q, stride=4), : hi - lo] = full[:, lo:hi]


def get_rows(s_ref, start, count, step=1):
    ds = pl.ds(start, count) if step == 1 else pl.ds(start, count, stride=step)
    return jnp.concatenate([s_ref[0, ds, :], s_ref[1, ds, :], s_ref[2, ds, :64]], axis=1)


def put_taps(s_ref, start, w, back):
    for r in range(3):
        taps = [get_rows(s_ref, start + D * (3 * r + i), D).astype(BF) for i in range(3)]
        for i in range(3):
            w[r, D * i : D * (i + 1), :] = taps[i]
        back[r] = jnp.concatenate(taps[::-1], axis=1)


def unit_row(parts):
    out = [p[:, W * b : W * (b + 1)] for b in range(2) for p in parts]
    return jnp.broadcast_to(jnp.concatenate(out, axis=1), (8, 4 * D))


def unit_parts(row):
    return [
        jnp.concatenate([row[:, W * i : W * (i + 1)], row[:, 640 + W * i : 640 + W * (i + 1)]], axis=1)
        for i in range(4)
    ]


def unpack0_kernel(rows, a_ref, e, win, w1, w1b, vec, tw2, tw3, tv, p1, p2, flat, s_ref):
    unroll_rows(a_ref, flat, s_ref, R1 // 400, rows)
    win[...] = get_rows(s_ref, 0, 36).astype(BF)
    put_taps(s_ref, 39, w1, w1b)
    for i, r in enumerate(VEC0):
        vec[i : i + 1, :] = get_rows(s_ref, r, 1)
    for i in range(4):
        tw2[i] = get_rows(s_ref, U2 + i, 4 * D, 4).astype(BF)
    tw3[...] = get_rows(s_ref, U3, 4 * D).astype(BF)
    u = e[...].astype(BF)
    p1[...] = unit_row(
        [nn(u, get_rows(s_ref, U1 + i, D, 4).astype(BF))[:1] + get_rows(s_ref, U1 + 4 * D + i, 1) for i in range(4)]
    )
    u = silu(p1[...]).astype(BF)
    p2[...] = unit_row([nn(u, tw2[i])[:1] + get_rows(s_ref, U2 + 16 * D + i, 1) for i in range(4)])
    u = silu(p2[...]).astype(BF)
    tv[...] = nn(u, tw3[...])[:1] + get_rows(s_ref, U3 + 4 * D, 1)


FE, FU1, FU2, FD1, FD2, FD3, FL = 0, 3, 13, 23, 28, 33, 35
FACTS = 40


def time_back_kernel(dtv, tw2, tw3, p1, p2, e, mask, loss, facts):
    first = lax.axis_index(CH) == 0
    g = jnp.broadcast_to(dtv[...], (8, D)).astype(BF)
    d2 = nt(g, tw3[...]) * silu_slope(p2[...])
    total = jnp.zeros((8, 4 * D), F32)
    for i, part in enumerate(unit_parts(d2)):
        total += nt(part.astype(BF), tw2[i])
    d1 = total * silu_slope(p1[...])
    facts[...] = jnp.zeros_like(facts)

    def put(at, v):
        for i in range(0, v.shape[1], 128):
            n = min(128, v.shape[1] - i)
            facts[at + i // 128 : at + i // 128 + 1, :n] = v[:1, i : i + n]

    put(FE, e[...].astype(BF).astype(F32))
    put(FU1, silu(p1[...]).astype(BF).astype(F32))
    put(FU2, silu(p2[...]).astype(BF).astype(F32))
    put(FD1, jnp.where(first, d1[:, : 2 * D], d1[:, 2 * D :]))
    put(FD2, jnp.where(first, d2[:, : 2 * D], d2[:, 2 * D :]))
    put(FD3, own(dtv[...]))
    facts[FL : FL + 1, 0:1] = loss[...]
    facts[FL : FL + 1, 1:2] = jnp.sum(mask[...].astype(F32), axis=1, keepdims=True)


def unpack1_kernel(rows, a_ref, c2, c2b, tr, mats, kv, vec, gib, wout, outb, flat, s_ref, o_ref):
    unroll_rows(a_ref, flat, s_ref, R1 // 400, rows)
    put_taps(s_ref, C2, c2, c2b)
    tr[MPI] = get_rows(s_ref, PI, D).astype(BF)
    for m, r in ((MSO, SO), (MCQ, CQ), (MCO, CO), (MPO, PO)):
        mats[m] = get_rows(s_ref, r, D).astype(BF)
    for j in range(3):
        tr[MQ + j] = get_rows(s_ref, QKV + j, D, 3).astype(BF)
    for j in range(8):
        mats[MGV + j] = get_rows(s_ref, GI + j, D, 8).astype(BF)
    for j in range(4):
        for b in range(2):
            mats[MGO + j, b * W : (b + 1) * W, :] = get_rows(s_ref, GO + 640 * b + W * j, W).astype(BF)
    for j in range(2):
        kv[j] = get_rows(s_ref, CKV + j, CTX, 2).astype(BF)
    for i, r in enumerate(VEC1):
        vec[i : i + 1, :] = get_rows(s_ref, r, 1)
    gib[...] = get_rows(s_ref, GIB, 8)
    outb[...] = get_rows(s_ref, OUTB, 1)
    lane = lax.broadcasted_iota(jnp.int32, (W, W), 0)
    col = lax.broadcasted_iota(jnp.int32, (W, W), 1)
    pick = ((lane % 2) * 80 + lane // 2 == col).astype(BF)
    raw = get_rows(s_ref, OUT, 36).astype(BF)
    for b in range(2):
        moved = nn(raw[:, W * b : W * (b + 1)], pick)
        o_ref[0, :36, :] = moved[:, :128]
        o_ref[1, :36, :32] = moved[:, 128:]
        for ch in range(2):
            pieces = []
            for m in range(4):
                ds = pl.ds(m, 9, stride=4)
                both = jnp.concatenate([o_ref[0, ds, :], o_ref[1, ds, :32]], axis=1)
                pieces.append(both[:, 80 * ch : 80 * ch + 80])
            at = (2 * b + ch) * 9
            wout[at : at + 9, :] = jnp.concatenate(pieces, axis=1).astype(BF)


def pixel_col(n, axis):
    shape = (n, 1) if axis == 0 else (1, n)
    return lax.broadcasted_iota(jnp.int32, shape, axis)


def shift_lanes(v, tap):
    r, s = tap // 3 - 1, tap % 3 - 1
    pix = pixel_col(N, 1)
    i, j = pix // SIDE + r, pix % SIDE + s
    ok = (i >= 0) & (i < SIDE) & (j >= 0) & (j < SIDE)
    move = -(r * SIDE + s) % N
    moved = pltpu.roll(v, move, 1) if move else v
    return jnp.where(ok, moved, 0.0)


def put_shifts(ref, v):
    j = pixel_col(N, 0) % SIDE
    left = jnp.where(j == 0, 0.0, pltpu.roll(v, 1, 0)).astype(BF)
    right = jnp.where(j == SIDE - 1, 0.0, pltpu.roll(v, N - 1, 0)).astype(BF)
    ref[SIDE : SIDE + N, :] = jnp.concatenate([left, v.astype(BF), right], axis=1)


def clear_margins(ref):
    zero = jnp.zeros((SIDE, ref.shape[1]), BF)
    ref[:SIDE, :] = zero
    ref[SIDE + N :, :] = zero


def conv_rows(ref, w_ref):
    return sum(nn(ref[SIDE * r : SIDE * r + N, :], w_ref[r]) for r in range(3))


def conv_back_rows(ref, w_ref):
    return sum(nt(ref[SIDE * (2 - r) : SIDE * (2 - r) + N, :], w_ref[r]) for r in range(3))


def group_mean(sums):
    a = lax.broadcasted_iota(jnp.int32, (D, D), 0) // 10
    b = lax.broadcasted_iota(jnp.int32, (D, D), 1) // 10
    pool = jnp.where(a == b, 1.0, 0.0)
    wide = jnp.broadcast_to(sums, (8, D))
    out = jnp.dot(wide, pool, precision=HI, preferred_element_type=F32)
    return out[:1] * (1.0 / (10 * N))


def group_stats(v_ref, acc, sums):
    mean = group_mean(sums)
    acc[0:1, :] = colsum(jnp.square(v_ref[...] - mean))
    return mean, lax.rsqrt(group_mean(acc[0:1, :]) + EPS)


def silu(v):
    return v * jax.nn.sigmoid(v)


def silu_slope(v):
    sig = jax.nn.sigmoid(v)
    return sig * (1.0 + v * (1.0 - sig))


def layer(v):
    mean = jnp.sum(v, axis=1, keepdims=True) * (1.0 / D)
    sq = jnp.sum(v * v, axis=1, keepdims=True) * (1.0 / D)
    inv = lax.rsqrt(sq - mean * mean + EPS)
    return (v - mean) * inv, inv


def layer_back(grad, normed, inv, gain):
    ghat = grad * gain
    m1 = jnp.sum(ghat, axis=1, keepdims=True) * (1.0 / D)
    m2 = jnp.sum(ghat * normed, axis=1, keepdims=True) * (1.0 / D)
    return inv * (ghat - m1 - normed * m2)


def own(v):
    return jnp.where(lax.axis_index(CH) == 0, v[..., :W], v[..., W:])


def head(v, h):
    return v[:, HD * h : HD * (h + 1)]


def front_kernel(noisy, tv, win, w1, vec0, c2, tr, vec1, h0, h1, h2, z0, a1, a2, ntr, x1, q, k, v, stats, sh, acc):
    cols = jnp.concatenate([shift_lanes(noisy[...], t) for t in range(9)], axis=0).astype(BF)
    clear_margins(sh)

    def norm(src, total, at):
        mean, inv = group_stats(src, acc, total)
        stats[at : at + 1, :], stats[at + 1 : at + 2, :] = mean, inv
        return (src[...] - mean) * inv

    h = tn(cols, win[...]) + vec0[0:1, :]
    h0[...] = h
    y = silu(norm(h0, colsum(h), 0) * vec0[1:2, :] + vec0[2:3, :])
    put_shifts(sh, y)
    a1[...] = y.astype(BF)
    h = conv_rows(sh, w1) + (vec0[3:4, :] + tv[...])
    h1[...] = h
    y = silu(norm(h1, colsum(h), 2) * vec1[N2G : N2G + 1, :] + vec1[N2B : N2B + 1, :])
    put_shifts(sh, y)
    a2[...] = y.astype(BF)
    h = h0[...] + conv_rows(sh, c2) + vec1[C2B : C2B + 1, :]
    h2[...] = h
    n = (norm(h2, colsum(h), 4) * vec1[NTG : NTG + 1, :] + vec1[NTB : NTB + 1, :]).astype(BF)
    ntr[...] = n
    z = nn(n, tr[MPI]) + vec1[PIB : PIB + 1, :]
    z0[...] = z
    normed, _ = layer(z)
    x = (normed * vec1[L1G : L1G + 1, :] + vec1[L1B : L1B + 1, :]).astype(BF)
    x1[...] = x
    for at, dst in ((MQ, q), (MK, k), (MV, v)):
        y = nn(x, tr[at]).astype(BF)
        for hd in range(HEADS):
            dst[hd] = head(y, hd)


AT = 512


def attend_kernel(q, k, v, o, lse, ot):
    steps = [(h, pl.ds(t * AT, AT)) for h in range(HEADS) for t in range(N // AT)]

    def scores(h, rows):
        return nt(k[h], q[h, rows, :])

    now = scores(*steps[0])
    for i, (h, rows) in enumerate(steps):
        later = scores(*steps[i + 1]) if i + 1 < len(steps) else None
        if i % (N // AT) == 0:
            vt = v[h].astype(F32).T.astype(BF)
        s = now * (SCALE * LOG2E)
        top = jnp.max(s, axis=0, keepdims=True)
        e = jnp.exp2(s - top)
        total = jnp.sum(e, axis=0, keepdims=True)
        lse[h, :, rows] = top + jnp.log(total) * LOG2E
        ot[h * HD : (h + 1) * HD, rows] = nn(vt, (e * (1.0 / total)).astype(BF))
        now = later
    o[...] = ot[...].T.astype(BF)


def cross_head(qh, kh):
    s = nt(kh, qh) * (SCALE * LOG2E)
    e = jnp.exp2(s - jnp.max(s, axis=0, keepdims=True))
    return e * (1.0 / jnp.sum(e, axis=0, keepdims=True))


def transposed(v):
    return v.astype(F32).T.astype(BF)


def middle_kernel(
    o, z0, h2, ctx, noise, mask, mats, kvw, vec, gib, wout, outb,
    dz1, dh3, dos, loss, gd, ggi, ggo, gkv, dvec, dgib, dwout, dbout,
    z1, z2, h3, x2, x3, oc, z3b, gl, a3, qc, kc, vc, derr, acc, ot, pt,
):
    def row(i):
        return vec[i : i + 1, :]

    def put(i, v):
        dvec[i : i + 1, :] = v

    kk = nn(ctx[...], kvw[0]).astype(BF)
    vv = nn(ctx[...], kvw[1])
    for h in range(HEADS):
        kc[h] = head(kk, h)
        vc[h] = head(vv, h).astype(BF)
    vt = vv.T
    z = z0[...] + nn(o[...], mats[MSO]) + row(SOB)
    z1[...] = z
    normed, _ = layer(z)
    x = (normed * row(L2G) + row(L2B)).astype(BF)
    x2[...] = x
    qq = nn(x, mats[MCQ]).astype(BF)
    for h in range(HEADS):
        qh = head(qq, h)
        qc[h] = qh
        p = cross_head(qh, kc[h]).astype(BF)
        ot[HD * h : HD * (h + 1), :] = nn(vt[HD * h : HD * (h + 1), :].astype(BF), p)
    c = ot[...].T.astype(BF)
    oc[...] = c
    z = z1[...] + nn(c, mats[MCO]) + row(COB)
    z2[...] = z
    normed, _ = layer(z)
    x = (normed * row(L3G) + row(L3B)).astype(BF)
    x3[...] = x
    for j in range(4):
        a = nn(x, mats[MGV + j]) + gib[j : j + 1, :]
        g = nn(x, mats[MGG + j]) + gib[4 + j : 5 + j, :]
        y = (a * (0.5 * g * (1.0 + lax.erf(g * math.sqrt(0.5))))).astype(BF)
        gl[j] = y
        z = z + nn(y, mats[MGO + j])
    zb = (z + row(GOB)).astype(BF)
    z3b[...] = zb
    h = h2[...] + nn(zb, mats[MPO]) + row(POB)
    h3[...] = h
    mean, inv = group_stats(h3, acc, colsum(h))
    gain, bias = row(NOG), row(NOB)
    a3[...] = silu((h3[...] - mean) * inv * gain + bias).astype(BF)
    taps = nt(wout[...], a3[...])
    for ch in range(LAT):
        pred = jnp.zeros((1, N), F32)
        for t in range(9):
            pred += shift_lanes(taps[9 * ch + t : 9 * ch + t + 1, :], t)
        at = W * (ch // 2) + ch % 2
        err = pred + outb[0:1, at : at + 1] - noise[ch : ch + 1, :]
        weighed = mask[...].astype(F32) * err
        g = 2.0 * weighed
        acc[2 + ch : 3 + ch, 0:1] = jnp.sum(weighed * err, axis=1, keepdims=True)
        dbout[ch : ch + 1, :] = jnp.broadcast_to(jnp.sum(g, axis=1, keepdims=True), (1, 128))
        for t in range(9):
            pt[9 * ch + t : 9 * ch + t + 1, :] = shift_lanes(g, 8 - t)
    loss[...] = acc[2:3, 0:1] + acc[3:4, 0:1] + acc[4:5, 0:1] + acc[5:6, 0:1]

    dvec[...] = jnp.zeros_like(dvec)
    taps = pt[...].astype(BF)
    dwout[...] = nn(taps, a3[...])
    n = (h3[...] - mean) * inv
    g = tn(taps, wout[...]) * silu_slope(n * gain + bias)
    dgain, dbias = colsum(g * n), colsum(g)
    put(NOG, dgain)
    put(NOB, dbias)
    g = inv * (g * gain - group_mean(gain * dbias) - n * group_mean(gain * dgain))
    dh3[...] = g
    put(POB, colsum(g))
    gd[0] = nn(transposed(z3b[...]), own(g).astype(BF)).astype(BF)
    dz3 = nt(g.astype(BF), mats[MPO])
    z1b = dz3.astype(BF)
    put(GOB, colsum(dz3))
    mine = own(dz3).astype(BF)
    x = x3[...]
    xt = transposed(x)
    dx = jnp.zeros((N, D), F32)
    for j in range(4):
        a = nn(x, mats[MGV + j]) + gib[j : j + 1, :]
        g = nn(x, mats[MGG + j]) + gib[4 + j : 5 + j, :]
        dgl = nt(z1b, mats[MGO + j])
        ggo[j] = tn(gl[j], mine).astype(BF)
        cdf = 0.5 * (1.0 + lax.erf(g * math.sqrt(0.5)))
        da = dgl * (g * cdf)
        dg = dgl * a * (cdf + g * jnp.exp(-0.5 * g * g) * (1.0 / math.sqrt(2.0 * math.pi)))
        dgib[j : j + 1, :] = colsum(da)
        dgib[4 + j : 5 + j, :] = colsum(dg)
        ggi[j] = nn(xt, own(da).astype(BF)).astype(BF)
        ggi[4 + j] = nn(xt, own(dg).astype(BF)).astype(BF)
        dx += nt(da.astype(BF), mats[MGV + j]) + nt(dg.astype(BF), mats[MGG + j])
    normed, li = layer(z2[...])
    put(L3G, colsum(dx * normed))
    put(L3B, colsum(dx))
    dz = dz3 + layer_back(dx, normed, li, row(L3G))
    z2[...] = dz
    put(COB, colsum(dz))
    gd[1] = tn(oc[...], own(dz).astype(BF)).astype(BF)
    do = nt(dz.astype(BF), mats[MCO]).astype(BF)
    dks, dvs = [], []
    for h in range(HEADS):
        qh, kh, vh, doh = qc[h], kc[h], vc[h], head(do, h)
        p = cross_head(qh, kh)
        dp = nt(vh, doh)
        ds = (p * (dp - jnp.sum(p * dp, axis=0, keepdims=True)) * SCALE).astype(BF)
        dks.append(nn(ds, qh))
        dvs.append(nn(p.astype(BF), doh))
        ot[HD * h : HD * (h + 1), :] = tn(kh, ds)
    for j, g in enumerate((dks, dvs)):
        gkv[j] = tn(ctx[...], own(jnp.concatenate(g, axis=1)).astype(BF)).astype(BF)
    dq = ot[...].T
    gd[2] = tn(x2[...], own(dq).astype(BF)).astype(BF)
    dx = nt(dq.astype(BF), mats[MCQ])
    normed, li = layer(z1[...])
    put(L2G, colsum(dx * normed))
    put(L2B, colsum(dx))
    dz = z2[...] + layer_back(dx, normed, li, row(L2G))
    dz1[...] = dz
    put(SOB, colsum(dz))
    gd[3] = tn(o[...], own(dz).astype(BF)).astype(BF)
    do = nt(dz.astype(BF), mats[MSO]).astype(BF)
    for h in range(HEADS):
        dos[h] = head(do, h)


ABT = 256


def attend_back_kernel(q, k, v, do, lse, dq, dk, dv, qt, kacc, vacc):
    steps = [(h, pl.ds(t * ABT, ABT)) for h in range(HEADS) for t in range(N // ABT)]

    def scores(h, rows):
        return nt(k[h], q[h, rows, :]), nt(v[h], do[h, rows, :])

    now = scores(*steps[0])
    for i, (h, rows) in enumerate(steps):
        later = scores(*steps[i + 1]) if i + 1 < len(steps) else None
        s, dp = now
        p = jnp.exp2(s * (SCALE * LOG2E) - lse[h, :, rows])
        ds = (p * (dp - jnp.sum(p * dp, axis=0, keepdims=True)) * SCALE).astype(BF)
        dkt, dvt = nn(ds, q[h, rows, :]), nn(p.astype(BF), do[h, rows, :])
        if i % (N // ABT) == 0:
            kt = k[h].astype(F32).T.astype(BF)
            kacc[h], vacc[h] = dkt, dvt
        else:
            kacc[h] += dkt
            vacc[h] += dvt
        qt[h * HD : (h + 1) * HD, rows] = nn(kt, ds)
        now = later

    dq[...] = qt[...].T.astype(BF)

    def one(rows):
        for acc, dst in ((kacc, dk), (vacc, dv)):
            dst[rows, :] = jnp.concatenate([acc[h, rows, :] for h in range(HEADS)], axis=1).astype(BF)

    tiles(one)


def put_rows(s_ref, start, v, step=1):
    n = v.shape[0]
    ds = pl.ds(start, n) if step == 1 else pl.ds(start, n, stride=step)
    s_ref[0, ds, :] = v[:, :128]
    s_ref[1, ds, :32] = v[:, 128:]


def roll_rows(s_ref, out_ref, lo_chunk, hi_chunk):
    q = 80

    @pl.loop(lo_chunk, hi_chunk)
    def _(c):
        g = []
        for i in range(4):
            ds = pl.ds(c * 4 * q + i, q, stride=4)
            g.append((s_ref[0, ds, :], s_ref[1, ds, :32]))
        base = (c - lo_chunk) * 5 * q
        out_ref[pl.ds(base, q, stride=5), :] = g[0][0]
        for i in range(3):
            lo = 96 - 32 * i
            out_ref[pl.ds(base + i + 1, q, stride=5), :] = jnp.concatenate(
                ([g[i][0][:, 128 - 32 * i :]] if i else []) + [g[i][1], g[i + 1][0][:, :lo]], axis=1
            )
        out_ref[pl.ds(base + 4, q, stride=5), :] = jnp.concatenate([g[3][0][:, 32:], g[3][1]], axis=1)


def by_owner(s_ref, flat, out, total):
    owners, room = math.prod(out.shape[:-2]), out.shape[-2]
    size = room if total < owners * room and len(out.shape) == 3 else min(room, ROWS)
    half = owners // 2 * size
    for lo, hi, first in ((0, min(-(-half // 400), total // 400), 0), (half // 400, total // 400, owners // 2)):
        if hi > lo:
            roll_rows(s_ref, flat, lo, hi)
        at = 400 * max(hi - lo, 0)
        if at < flat.shape[0]:
            flat[at:, :] = jnp.zeros((flat.shape[0] - at, 128), F32)
        for t in range(first, first + owners // 2):
            spot = (t % 2, t // 2) if len(out.shape) == 4 else (t,)
            row = t * size - 400 * lo
            out[(*spot, slice(0, size))] = flat[row : row + size, :].astype(BF)
            if room > size:
                out[(*spot, slice(size, room))] = jnp.zeros((room - size, 128), BF)


def conv_grads(a_ref, g_ref, s_ref, start):
    at = transposed(a_ref[...])
    for r in range(3):
        rows = SIDE * (2 - r)
        three = nn(at, g_ref[rows : rows + N, :])
        for i in range(3):
            put_rows(s_ref, start + D * (3 * r + i), three[:, W * (2 - i) : W * (3 - i)])


def back_kernel(
    dq, dk, dv, dz1, dh3, z0, h2, h1, h0, stats, w1, c2, tr, vec0, vec1, a1, a2, ntr, x1, noisy,
    gd, ggi, ggo, gkv, dvec_in, dgib, dwout, dbout,
    out1, out0, dtv,
    dh, g_ref, go_ref, dvec, s_ref, flat, o_ref,
):
    c = lax.axis_index(CH)
    clear_margins(g_ref)
    clear_margins(go_ref)
    dvec[...] = dvec_in[...]

    def row(i):
        return vec1[i : i + 1, :]

    def put(i, v):
        dvec[i : i + 1, :] = v

    dx = nt(dq[...], tr[MQ]) + nt(dk[...], tr[MK]) + nt(dv[...], tr[MV])
    xt = transposed(x1[...])
    for j, g in enumerate((dq, dk, dv)):
        put_rows(s_ref, QKV + j, nn(xt, own(g[...].astype(F32)).astype(BF)), 3)
    normed, li = layer(z0[...])
    put(L1G, colsum(dx * normed))
    put(L1B, colsum(dx))
    dz = dz1[...] + layer_back(dx, normed, li, row(L1G))
    put(PIB, colsum(dz))
    put_rows(s_ref, PI, tn(ntr[...], own(dz).astype(BF)))
    g = nt(dz.astype(BF), tr[MPI])

    def norm_back(g, n, at, gain):
        dgain, dbias = colsum(g * n), colsum(g)
        back = stats[at + 1 : at + 2, :] * (g * gain - group_mean(gain * dbias) - n * group_mean(gain * dgain))
        return back, dgain, dbias

    def normed_of(src, at):
        return (src[...] - stats[at : at + 1, :]) * stats[at + 1 : at + 2, :]

    g, dgain, dbias = norm_back(g, normed_of(h2, 4), 4, row(NTG))
    put(NTG, dgain)
    put(NTB, dbias)
    g = dh3[...] + g
    dh[...] = g
    put(C2B, colsum(g))
    put_shifts(g_ref, g)
    put_shifts(go_ref, own(g))
    conv_grads(a2, go_ref, s_ref, C2)
    n = normed_of(h1, 2)
    g = conv_back_rows(g_ref, c2) * silu_slope(n * row(N2G) + row(N2B))
    g, dgain, dbias = norm_back(g, n, 2, row(N2G))
    put(N2G, dgain)
    put(N2B, dbias)
    total = colsum(g)
    dtv[...] = total
    put_shifts(g_ref, g)
    put_shifts(go_ref, own(g))

    for i, r in enumerate((PO, CO, CQ, SO)):
        put_rows(s_ref, r, gd[i].astype(F32))
    for j in range(8):
        put_rows(s_ref, GI + j, ggi[j].astype(F32), 8)
    for j in range(4):
        rows = ggo[j].astype(F32)
        for b in range(2):
            put_rows(s_ref, GO + 640 * b + W * j, rows[W * b : W * (b + 1), :])
    for j in range(2):
        put_rows(s_ref, CKV + j, gkv[j].astype(F32), 2)
    for i, r in enumerate(VEC1):
        put_rows(s_ref, r, own(dvec[i : i + 1, :]))
    put_rows(s_ref, GIB, own(dgib[...]))
    wide = jnp.where(c == 0, dwout[:18, :], dwout[18:36, :])
    for ch in range(2):
        for m in range(4):
            o_ref[ch, pl.ds(m, 9, stride=4), :80] = wide[9 * ch : 9 * ch + 9, 80 * m : 80 * m + 80]
    lane = lax.broadcasted_iota(jnp.int32, (80, W), 0)
    col = lax.broadcasted_iota(jnp.int32, (80, W), 1)
    moved = jnp.zeros((36, W), F32)
    for ch in range(2):
        spot = jnp.where(2 * lane + ch == col, 1.0, 0.0)
        moved += jnp.dot(o_ref[ch, :36, :80], spot, precision=HI, preferred_element_type=F32)
    put_rows(s_ref, OUT, moved)
    b0 = jnp.where(c == 0, dbout[0:1, 0:1], dbout[2:3, 0:1])
    b1 = jnp.where(c == 0, dbout[1:2, 0:1], dbout[3:4, 0:1])
    at = lax.broadcasted_iota(jnp.int32, (1, W), 1)
    put_rows(s_ref, OUTB, jnp.where(at == 0, b0, jnp.where(at == 1, b1, 0.0)))
    s_ref[:, OUTB + 1 :, :] = jnp.zeros((2, 4 * R1 // 5 - OUTB - 1, 128), F32)
    by_owner(s_ref, flat, out1, R1)

    conv_grads(a1, go_ref, s_ref, 39)
    n = normed_of(h0, 0)
    g = conv_back_rows(g_ref, w1) * silu_slope(n * vec0[1:2, :] + vec0[2:3, :])
    g, dgain, dbias = norm_back(g, n, 0, vec0[1:2, :])
    g = dh[...] + g
    cols = jnp.concatenate([shift_lanes(noisy[...], t) for t in range(9)], axis=0).astype(BF)
    put_rows(s_ref, 0, nn(cols, own(g).astype(BF)))
    for r, v in zip(VEC0, (colsum(g), dgain, dbias, total)):
        put_rows(s_ref, r, own(v))
    s_ref[:, 4 * FRONT // 5 : 4 * R0 // 5, :] = jnp.zeros((2, 4 * (R0 - FRONT) // 5, 128), F32)
    by_owner(s_ref, flat, out0, R0)


FIRST = (0, 0, 1, 2, 3)
SECOND = (0, 1, 2, 3, 3)


def time_rows(facts, count):
    row = lax.axis_index(DP) * count + lax.broadcasted_iota(jnp.int32, (count, 1), 0)

    def wide(at, n):
        return jnp.concatenate([facts[:, at + i, :] for i in range(n)], axis=1)

    def meets(u, k):
        spot = jnp.where(k == lax.broadcasted_iota(jnp.int32, (1, u.shape[1]), 1), 1.0, 0.0).astype(BF)
        return nt(spot, u.astype(BF))

    total = jnp.zeros((count, 128), F32)
    for u, at, start, size in ((wide(FE, 3)[:, :D], FD1, T1, D), (wide(FU1, 10), FD2, T2, 4 * D)):
        rel = row - start
        k, line = rel // 5, rel % 5
        met = meets(u, jnp.where(rel < 0, -1, k))
        for j in range(5):
            g = facts[:, at + j, :]
            total += nn(jnp.where(line == j, met, 0.0).astype(BF), g.astype(BF))
            total += jnp.where((rel >= 0) & (k == size) & (line == j), colsum(g), 0.0)
    rel = row - T3
    group, line = rel // 5, rel % 5
    d3 = wide(FD3, 2)[:, :W]
    zero = jnp.zeros((d3.shape[0], 128), F32)
    u = wide(FU2, 10)
    for picks, shift in ((FIRST, 0), (SECOND, 1)):
        k = jnp.full_like(rel, -1)
        for j in range(5):
            k = jnp.where((rel >= 0) & (line == j), 4 * group + picks[j], k)
        met = meets(u, k)
        for j in range(5):
            if shift == 0:
                lo = (0, 128, 96, 64, 32)[j]
                g = d3[:, lo : min(lo + 128, W)]
                g = jnp.concatenate([g, zero[:, : 128 - g.shape[1]]], axis=1) if g.shape[1] < 128 else g
            else:
                if j in (0, 4):
                    continue
                g = jnp.concatenate([zero[:, : 32 * j], d3[:, : 128 - 32 * j]], axis=1)
            total += nn(jnp.where(line == j, met, 0.0).astype(BF), g.astype(BF))
            total += jnp.where((k == 4 * D) & (line == j), colsum(g), 0.0)
    return total


def update_kernel(with_time, params, momentum, ema, sum1, sum0, facts, new_params, new_momentum, new_ema, sums):
    total = facts[0, FL : FL + 1, :]
    for i in range(1, facts.shape[0]):
        total += facts[i, FL : FL + 1, :]
    sums[...] = total
    scale = 1.0 / (LAT * jnp.maximum(total[:, 1:2], 1.0))
    first = sum0[...]
    if with_time:
        first += time_rows(facts, sum0.shape[0])
    for p, g in enumerate((first, sum1[...])):
        g = g * scale
        m = MU * momentum[p] + g
        new_momentum[p] = m
        w = params[p] - LR * (g + MU * m)
        new_params[p] = w
        new_ema[p] = ED * ema[p] + (1.0 - ED) * w


ROWS = 856
SLAB = 864
SOME = 240
REST = SLAB - 3 * SOME


def send(src, dst, sems, i, j, target):
    copy = pltpu.make_async_remote_copy(
        src_ref=src, dst_ref=dst, send_sem=sems[0].at[i], recv_sem=sems[1].at[j],
        device_id={DP: target}, device_id_type=pl.DeviceIdType.MESH,
    )
    copy.start()
    return copy


PIECES = tuple(slice(16 * a, 16 * b) for a, b in ((0, 7), (7, 14), (14, 21), (21, 28), (28, 35), (35, 42), (42, 48), (48, 54)))


def gather_kernel(params, g0, g1, low, send_sem, recv_sem, keep_sem):
    low[:, :ROWS, :] = params[...].astype(BF)
    low[:, ROWS:, :] = jnp.zeros((2, SLAB - ROWS, 128), BF)
    me, y = lax.axis_index(DP), lax.axis_index(CH)
    k, x, z = me % 2, (me // 2) % 2, me // 4
    core = {DP: me + 1 - 2 * k}
    side = {DP: me + 2 - 4 * x}
    other = {CH: 1 - y}
    ring = [{DP: (me + 4 * o) % 16} for o in range(4)]
    barrier = pltpu.get_barrier_semaphore()
    for target in [core, side, other] + ring[1:]:
        pl.semaphore_signal(barrier, inc=1, device_id=target, device_id_type=pl.DeviceIdType.MESH)
    pl.semaphore_wait(barrier, 6)
    count = [0]
    started = []

    def push(ref, target):
        i = count[0]
        count[0] += 1
        return [start(ref, ref, i, i, target)]

    def start(src, dst, i, j, target):
        copy = pltpu.make_async_remote_copy(
            src_ref=src, dst_ref=dst, send_sem=send_sem.at[i], recv_sem=recv_sem.at[j],
            device_id=target, device_id_type=pl.DeviceIdType.MESH,
        )
        copy.start()
        started.append(copy)
        return copy

    def push_ring(ref):
        i = count[0]
        count[0] += 3
        return [start(ref, ref, i + o - 1, i + 3 - o, ring[o]) for o in (2, 1, 3)]

    def arrive(copies):
        for copy in copies:
            copy.wait_recv()

    keeps = []
    for p, g in enumerate((g0, g1)):
        keep = pltpu.make_async_copy(low.at[p], g.at[y, z, x, k], keep_sem.at[p])
        keep.start()
        keeps.append(keep)
    work = [(p, g, rows, i % 2) for p, g in enumerate((g0, g1)) for i, rows in enumerate(PIECES)]
    first, second, third, last = {}, {}, {}, []

    def begin(i):
        p, g, rows, _ = work[i]
        if i % len(PIECES) == 0:
            keeps[p].wait()
        first[i] = push_ring(g.at[y, z, x, k, rows])

    def middle(i):
        _, g, rows, turn = work[i]
        arrive(first[i])
        second[i] = push(g.at[y, :, x, k, rows], other if turn else side)
        last.extend(push(g.at[y, :, x, k, rows], core))

    def finish(i):
        _, g, rows, turn = work[i]
        arrive(second[i])
        if turn:
            third[i] = push(g.at[:, :, x, k, rows], side)
            last.extend(push(g.at[1 - y, :, x, k, rows], core))
        else:
            third[i] = push(g.at[y, :, :, k, rows], other)
            last.extend(push(g.at[y, :, 1 - x, k, rows], core))

    def pass_on(i):
        _, g, rows, turn = work[i]
        arrive(third[i])
        last.extend(push(g.at[:, :, 1 - x, k, rows] if turn else g.at[1 - y, :, :, k, rows], core))

    ahead = 4
    for i in range(ahead):
        begin(i)
    for i in range(len(work) + 2):
        if i < len(work):
            middle(i)
            if i + ahead < len(work):
                begin(i + ahead)
        if 0 <= i - 1 < len(work):
            finish(i - 1)
        if 0 <= i - 3 < len(work):
            pass_on(i - 3)
    pass_on(len(work) - 1)
    arrive(last)
    for copy in started:
        copy.wait_send()


def gather_weights(params):
    hbm = pl.BlockSpec(memory_space=pl.ANY)
    whole = sds((2, 4, 2, 2, SLAB, 128), BF)
    dma = pltpu.SemaphoreType.DMA
    return pl.pallas_call(
        gather_kernel,
        out_shape=(whole, whole),
        in_specs=[pl.BlockSpec(memory_space=pltpu.VMEM)],
        out_specs=(hbm, hbm),
        scratch_shapes=[pltpu.VMEM((2, SLAB, 128), BF), dma((128,)), dma((128,)), dma((2,))],
        compiler_params=pltpu.CompilerParams(collective_id=2, has_side_effects=True),
    )(params)


def add_up(*terms):
    total = terms[0].astype(F32)
    for term in terms[1:]:
        total += term.astype(F32)
    return total


def reduce_kernel(
    p1, p0, facts, sum1, sum0, all_facts,
    r1, sa, rx, ta, rz, r1b, sb, rbz, tb, rbx, some, land, fx, send_sem, recv_sem, fsend, frecv, gsend, grecv,
):
    me = lax.axis_index(DP)
    k, x, z = me % 2, (me // 2) % 2, me // 4
    barrier = pltpu.get_barrier_semaphore()
    for o in range(1, 16):
        pl.semaphore_signal(barrier, inc=1, device_id={DP: (me + o) % 16}, device_id_type=pl.DeviceIdType.MESH)
    pl.semaphore_wait(barrier, 15)
    sems = (send_sem, recv_sem)
    core = me + 1 - 2 * k
    side = me + 2 - 4 * x
    chunks = [p0] + [p1.at[:, :, SOME * i : SOME * (i + 1)] for i in range(3)]
    rest = p1.at[:, :, 3 * SOME :]

    def over_z(src, dst, base):
        return [
            send(src.at[(z + o) % 4], dst.at[3 - o], sems, base + o - 1, base + 3 - o, (me + 4 * o) % 16)
            for o in (2, 1, 3)
        ]

    over_core_b = send(rest.at[1 - k], r1b, sems, 20, 20, core)
    over_core = [send(ref.at[1 - k], r1.at[i], sems, i, i, core) for i, ref in enumerate(chunks)]
    fact_copies = [send(facts, fx.at[me], (fsend, frecv), o - 1, o - 1, (me + o) % 16) for o in range(1, 16)]
    over_core_b.wait_recv()
    for m in range(8):
        sb[m // 2, m % 2] = add_up(rest[k, m], r1b[m]).astype(BF)
    over_z_b = over_z(sb, rbz, 21)
    over_x = []
    for i, ref in enumerate(chunks):
        over_core[i].wait_recv()
        for m in range(8):
            sa[i, m % 2, m // 2] = add_up(ref[k, m], r1[i, m]).astype(BF)
        over_x.append(send(sa.at[i, 1 - x], rx.at[i], sems, 4 + i, 4 + i, side))
    along = []
    for i in range(4):
        over_x[i].wait_recv()
        for m in range(4):
            ta[i, m] = add_up(sa[i, x, m], rx[i, m]).astype(BF)
        along.append(over_z(ta.at[i], rz.at[i], 8 + 3 * i))
    for copy in over_z_b:
        copy.wait_recv()
    for m in range(2):
        tb[m] = add_up(sb[z, m], rbz[0, m], rbz[1, m], rbz[2, m]).astype(BF)
    over_x_b = send(tb.at[1 - x], rbx, sems, 24, 24, side)

    def done(i):
        for copy in along[i]:
            copy.wait_recv()
        return add_up(ta[i, z], rz[i, 0], rz[i, 1], rz[i, 2])

    some[...] = done(0)
    fx[me] = facts[...]

    @pl.when(me > 0)
    def _():
        @pl.loop(0, SOME // 8)
        def _(g):
            row = SOME * me + 8 * g
            owner = row // ROWS
            at = pl.multiple_of(row - ROWS * owner, 8)
            pltpu.make_async_remote_copy(
                src_ref=some.at[pl.ds(pl.multiple_of(8 * g, 8), 8)], dst_ref=land.at[pl.ds(at, 8)],
                send_sem=gsend, recv_sem=grecv, device_id={DP: owner}, device_id_type=pl.DeviceIdType.MESH,
            ).start()

    for copy in fact_copies:
        copy.wait_recv()
    all_facts[...] = fx[...]
    for i in range(3):
        sum1[SOME * i : SOME * (i + 1), :] = done(i + 1)
    over_x_b.wait_recv()
    sum1[3 * SOME :, :] = add_up(tb[x, : ROWS - 3 * SOME], rbx[: ROWS - 3 * SOME])

    def landed(lo, hi):
        part = land.at[lo:hi]
        pltpu.make_async_remote_copy(
            src_ref=part, dst_ref=part, send_sem=gsend, recv_sem=grecv,
            device_id={DP: me}, device_id_type=pl.DeviceIdType.MESH,
        ).wait_recv()
        sum0[lo:hi, :] = land[lo:hi, :]

    @pl.when(me == 0)
    def _():
        landed(SOME, ROWS)
        sum0[:SOME, :] = some[...]

    @pl.when((me > 0) & (me < 4))
    def _():
        landed(0, ROWS)

    @pl.when(me == 4)
    def _():
        landed(0, 16 * SOME - 4 * ROWS)
        sum0[16 * SOME - 4 * ROWS :, :] = jnp.zeros((5 * ROWS - 16 * SOME, 128), F32)

    @pl.when(me > 4)
    def _():
        sum0[...] = jnp.zeros_like(sum0)

    @pl.when(me > 0)
    def _():
        pltpu.make_async_remote_copy(
            src_ref=some, dst_ref=some, send_sem=gsend, recv_sem=grecv,
            device_id={DP: me}, device_id_type=pl.DeviceIdType.MESH,
        ).wait_send()

    for copy in [over_core_b, over_x_b] + over_core + over_z_b + over_x + sum(along, []) + fact_copies:
        copy.wait_send()


def sum_over_samples(p1, p0, facts):
    vm = pl.BlockSpec(memory_space=pltpu.VMEM)
    dma = pltpu.SemaphoreType.DMA
    return pl.pallas_call(
        reduce_kernel,
        out_shape=(sds((ROWS, 128)), sds((ROWS, 128)), sds((16, FACTS, 128))),
        in_specs=[vm] * 3,
        out_specs=(vm,) * 3,
        scratch_shapes=[
            pltpu.VMEM((4, 8, SOME, 128), BF),
            pltpu.VMEM((4, 2, 4, SOME, 128), BF),
            pltpu.VMEM((4, 4, SOME, 128), BF),
            pltpu.VMEM((4, 4, SOME, 128), BF),
            pltpu.VMEM((4, 3, SOME, 128), BF),
            pltpu.VMEM((8, REST, 128), BF),
            pltpu.VMEM((4, 2, REST, 128), BF),
            pltpu.VMEM((3, 2, REST, 128), BF),
            pltpu.VMEM((2, REST, 128), BF),
            pltpu.VMEM((REST, 128), BF),
            pltpu.VMEM((SOME, 128), F32),
            pltpu.VMEM((ROWS, 128), F32),
            pltpu.VMEM((16, FACTS, 128), F32),
            dma((25,)),
            dma((25,)),
            dma((15,)),
            dma((15,)),
            dma,
            dma,
        ],
        compiler_params=pltpu.CompilerParams(
            collective_id=1, has_side_effects=True, vmem_limit_bytes=40 * 2**20
        ),
    )(p1, p0, facts)


def time_features(steps):
    ladder = jnp.arange(D // 2, dtype=F32)
    freq = jnp.exp(-math.log(10000.0) * ladder / (D // 2))
    angles = steps.astype(F32)[:, None] * freq[None, :]
    return jnp.concatenate([jnp.cos(angles), jnp.sin(angles)], axis=1)


def alpha_bar(step_ids):
    levels = jnp.arange(1000, dtype=F32)
    lowest, highest = 0.00085**0.5, 0.012**0.5
    beta = jnp.square(lowest + (highest - lowest) * levels / 999.0)
    table = jnp.cumprod(1.0 - beta)
    matches = levels[None, :] == step_ids.astype(F32)[:, None]
    return jnp.sum(jnp.where(matches, table[None, :], 0.0), axis=1)


def shards(params, momentum, ema_params, latents, noise_eps, timesteps, pixel_mask, context):
    c = lax.axis_index(CH)
    d = lax.axis_index(DP)
    n_dp = lax.axis_size(DP)
    rows_dev = params.shape[2]
    rows_all = rows_dev * n_dp
    quick = n_dp == 16 and rows_dev == ROWS
    if quick:
        part0, part1 = gather_weights(params[0])
        part0, part1 = part0.reshape(2, 16, SLAB, 128), part1.reshape(2, 16, SLAB, 128)
    else:
        low = params[0].astype(BF)
        part0, part1 = (lax.all_gather(lax.all_gather(low[i], CH, axis=0), DP, axis=1) for i in range(2))

    alpha = alpha_bar(timesteps)[:, None]
    noise = noise_eps[0]
    noisy = jnp.sqrt(alpha) * latents[0] + jnp.sqrt(1.0 - alpha) * noise

    px = (N, D)
    hx = (HEADS, N, HD)
    sh = (N + 2 * SIDE, 3 * D)
    taps, back = sds((3, 3 * D, D), BF), sds((3, D, 3 * D), BF)
    e = time_features(timesteps)
    flat = pltpu.VMEM((2, rows_all, 128), F32)
    unrolled = pltpu.VMEM((3, 4 * R1 // 5, 128), F32)
    units = sds((8, 4 * D))
    win, w1, w1b, vec0, tw2, tw3, tv, p1, p2 = kcall(
        partial(unpack0_kernel, rows_dev),
        (sds((36, D), BF), taps, back, sds((8, D)), sds((4, 4 * D, D), BF), sds((4 * D, D), BF), sds((1, D)))
        + (units, units),
        (part0, jnp.broadcast_to(e, (8, D))),
        (flat, unrolled),
    )
    c2, c2b, tr, mats, kvw, vec1, gib, wout, outb = kcall(
        partial(unpack1_kernel, rows_dev),
        (taps, back, sds((4, D, D), BF), sds((16, D, D), BF), sds((2, CTX, D), BF))
        + (sds((24, D)), sds((8, D)), sds((36, D), BF), sds((1, D))),
        (part1,),
        (flat, unrolled, pltpu.VMEM((2, 40, 128), F32)),
    )
    h0, h1, h2, z0, a1, a2, ntr, x1, q, k, v, stats = kcall(
        front_kernel,
        (sds(px),) * 4 + (sds(px, BF),) * 4 + (sds(hx, BF),) * 3 + (sds((8, D)),),
        (noisy, tv, win, w1, vec0, c2, tr, vec1),
        (pltpu.VMEM(sh, BF), pltpu.VMEM((8, D), F32)),
    )
    o, lse = kcall(
        attend_kernel, (sds(px, BF), sds((HEADS, 1, N))), (q, k, v), (pltpu.VMEM((D, N), F32),)
    )
    square = (D, W)
    dz1, dh3, dos, loss, gd, ggi, ggo, gkv, dvec, dgib, dwout, dbout = kcall(
        middle_kernel,
        (sds(px), sds(px), sds(hx, BF), sds((1, 1)))
        + (sds((4,) + square, BF), sds((8,) + square, BF), sds((4,) + square, BF), sds((2, CTX, W), BF))
        + (sds((24, D)), sds((8, D)), sds((36, D)), sds((8, 128))),
        (o, z0, h2, context[0], noise, pixel_mask, mats, kvw, vec1, gib, wout, outb),
        [pltpu.VMEM(px, F32)] * 3
        + [pltpu.VMEM(px, BF)] * 4
        + [
            pltpu.VMEM((4, N, D), BF),
            pltpu.VMEM(px, BF),
            pltpu.VMEM(hx, BF),
            pltpu.VMEM((HEADS, TXT, HD), BF),
            pltpu.VMEM((HEADS, TXT, HD), BF),
            pltpu.VMEM((LAT, N), F32),
            pltpu.VMEM((8, D), F32),
            pltpu.VMEM((D, N), F32),
            pltpu.VMEM((36, N), F32),
        ],
    )
    dq, dk, dv = kcall(
        attend_back_kernel,
        (sds(px, BF),) * 3,
        (q, k, v, dos, lse),
        (pltpu.VMEM((D, N), F32), pltpu.VMEM(hx, F32), pltpu.VMEM(hx, F32)),
    )
    step = 16 * n_dp
    front = -(-FRONT // step) * step
    lead = (2, 8) if quick else (n_dp,)
    own1, own0, dtv = kcall(
        back_kernel,
        (
            sds(lead + (SLAB if quick else rows_dev, 128), BF),
            sds(lead + (front // n_dp, 128), BF),
            sds((1, D)),
        ),
        (dq, dk, dv, dz1, dh3, z0, h2, h1, h0, stats, w1b, c2b, tr, vec0, vec1, a1, a2, ntr, x1, noisy,
         gd, ggi, ggo, gkv, dvec, dgib, dwout, dbout),
        (
            pltpu.VMEM(px, F32),
            pltpu.VMEM(sh, BF),
            pltpu.VMEM((sh[0], 3 * W), BF),
            pltpu.VMEM((24, D), F32),
            pltpu.VMEM((2, 4 * R1 // 5, 128), F32),
            pltpu.VMEM((7600, 128), F32),
            pltpu.VMEM((2, 40, 128), F32),
        ),
    )
    facts = kcall(
        time_back_kernel, sds((FACTS, 128)), (dtv, tw2, tw3, p1, p2, jnp.broadcast_to(e, (8, D)), pixel_mask, loss)
    )
    if quick:
        sum1, sum0, all_facts = sum_over_samples(own1, own0, facts)
    else:
        sum1 = lax.psum_scatter(own1, DP, scatter_dimension=0).astype(F32)
        sum0 = lax.all_gather(lax.psum_scatter(own0, DP, scatter_dimension=0), DP, axis=0, tiled=True)
        sum0 = jnp.pad(sum0, ((0, rows_all - front), (0, 0)))
        sum0 = lax.dynamic_slice_in_dim(sum0, d * rows_dev, rows_dev, 0).astype(F32)
        all_facts = lax.all_gather(facts, DP, axis=0)
    state = sds((2, rows_dev, 128))
    new_params, new_momentum, new_ema, sums = kcall(
        partial(update_kernel, True),
        (state, state, state, sds((1, 128))),
        (params[0], momentum[0], ema_params[0], sum1, sum0, all_facts),
    )
    return (new_params[None], new_momentum[None], new_ema[None], sums[0, 0], sums[0, 1])


def solution(mesh):
    packed = P(CH, None, DP, None)
    row = P(DP, None, None)
    return jax.shard_map(
        shards,
        mesh=mesh,
        in_specs=(packed, packed, packed, row, row, P(DP), P(DP, None), row),
        out_specs=(packed, packed, packed, P(), P()),
        check_vma=False,
    )
```

time: 432 us -> 342 us (0.79)
  the two profiles are of different devices: /device:TPU:1 before, /device:TPU:3 now
where the time goes in v2:
time: 342 us; the launch traced here: 337 us
  Pallas kernels  324 us (95%)
  local copies, waits for them, and re-layouts  7.04 us (2%)
    pallas_call x9, Pallas kernels, kcall(): pl.pallas_call(body, out_shape=outs, in_specs=[vm] * len(ins), out_specs=...  201 us
    pallas_call x1, Pallas kernels, gather_weights(): pl.pallas_call(gather_kernel, out_shape=(whole, whole), in_specs=[pl.Bloc...  77.4 us
    pallas_call x1, Pallas kernels, sum_over_samples(): pl.pallas_call(reduce_kernel, out_shape=(sds((ROWS, 128)), sds((ROWS, 128...  46.3 us

profile of v2, /device:TPU:3, one launch (start us, length us, event | category | flops | bytes accessed | tf_op | source)
XLA Modules:
  0.0 337.2 jit_solution(10544286415495699743)
XLA Ops:
  1.3 0.1 maximum_reduce_fusion
  1.5 0.3 reduce-window.9
  1.7 0.1 slice.16
  1.8 0.1 slice_reduce_fusion
  2.0 0.6 select_reduce_fusion
  4.0 0.6 broadcast_in_dim.16.e
  4.6 1.3 bitcast_add_fusion.noisy
  6.0 77.4 %shard_map.119 = (bf16[2,4,2,2,864,128]{5,4,3,2,1,0:T(8,128)(2,1)}, bf16[2,4,2,2,864,128]{5,4,3,2,1,0:T(8,128)(2,1)}) custom-call(f32[2,856,128]{2,1,0:T(8,128)} %bitcast.22), custom_call_target="tpu_custom_call" | custom-call | tf_op jit(solution)/shard_map/pallas_call | solution.py:869
  83.4 15.8 %shard_map.120 = (bf16[36,320]{1,0:T(8,128)(2,1)}, bf16[3,960,320]{2,1,0:T(8,128)(2,1)}, bf16[3,320,960]{2,1,0:T(8,128)(2,1)}, f32[8,320]{1,0:T(8,128)}, bf16[4,...) custom-call(bf16[2,16,864,128]{3,2,1,0:T(8,128)(2,1)} %bitcast.21, ...), custom_call_target="tpu_custom_call" | custom-call | tf_op jit(solution)/shard_map/pallas_call | solution.py:59
  99.2 15.5 %shard_map.121 = (bf16[3,960,320]{2,1,0:T(8,128)(2,1)}, bf16[3,320,960]{2,1,0:T(8,128)(2,1)}, bf16[4,320,320]{2,1,0:T(8,128)(2,1)}, bf16[16,320,320]{2,1,0:T(8,1...) custom-call(bf16[2,16,864,128]{3,2,1,0:T(8,128)(2,1)} %bitcast.20), custom_call_target="tpu_custom_call" | custom-call | tf_op jit(solution)/shard_map/pallas_call | solution.py:59
  114.8 22.0 %shard_map.122 = (f32[1024,320]{1,0:T(8,128)}, f32[1024,320]{1,0:T(8,128)}, f32[1024,320]{1,0:T(8,128)}, f32[1024,320]{1,0:T(8,128)}, bf16[1024,320]{1,0:T(8,128...) custom-call(f32[4,1024]{1,0:T(4,128)} %bitcast_add_fusion.noisy, ...), custom_call_target="tpu_custom_call" | custom-call | tf_op jit(solution)/shard_map/pallas_call | solution.py:59
  136.8 16.5 %shard_map.123 = (bf16[1024,320]{1,0:T(8,128)(2,1)}, f32[8,1,1024]{2,1,0:T(1,128)}) custom-call(bf16[8,1024,40]{2,1,0:T(8,128)(2,1)} %get-tuple-element.73.q, bf16[8,1024,40]{2,1,0:T(8,128)(2,1)} %get-tuple-element.74.k, bf16[8,1024,40]{2,1,0:T(8,128)(2,1)} %get-tuple-element.75.v), custom_call_target="tpu_custom_call" | custom-call | tf_op jit(solution)/shard_map/pallas_call | solution.py:59
  153.3 47.5 %shard_map.124 = (f32[1024,320]{1,0:T(8,128)}, f32[1024,320]{1,0:T(8,128)}, bf16[8,1024,40]{2,1,0:T(8,128)(2,1)}, f32[1,1]{1,0:T(1,128)}, bf16[4,320,160]{2,1,0:...) custom-call(bf16[1024,320]{1,0:T(8,128)(2,1)} %get-tuple-element.76., ...), custom_call_target="tpu_custom_call" | custom-call | tf_op jit(solution)/shard_map/pallas_call | solution.py:59
  200.8 29.7 %shard_map.125 = (bf16[1024,320]{1,0:T(8,128)(2,1)}, bf16[1024,320]{1,0:T(8,128)(2,1)}, bf16[1024,320]{1,0:T(8,128)(2,1)}) custom-call(bf16[8,1024,40]{2,1,0:T(8,128)(2,1)} %get-tuple-element.73.q, bf16[8,1024,40]{2,1,0:T(8,128)(2,1)} %get-tuple-element.74.k, bf16[8,1024,40]{2,1,0:T(8,128)(2,1)} %get-tuple-element.75.v, ...), custom_call_target="tpu_custom_call" | custom-call | tf_op jit(solution)/shard_map/pallas_call | solution.py:59
  230.4 38.1 %shard_map.126 = (bf16[2,8,864,128]{3,2,1,0:T(8,128)(2,1)}, bf16[2,8,240,128]{3,2,1,0:T(8,128)(2,1)}, f32[1,320]{1,0:T(1,128)}) custom-call(bf16[1024,320]{1,0:T(8,128)(2,1)} %get-tuple-element.86.dq, bf16[1024,320]{1,0:T(8,128)(2,1)} %get-tuple-element.87.dk, bf16[1024,320]{1,0:T(8,128)(2,1)} %get-tuple-element.88.dv, f32[1024,320]{1,0:T(8,128)} %get-tuple-element.89.dz1, ...), custom_call_target="tpu_custom_call" | custom-call | tf_op jit(solution)/shard_map/pallas_call | solution.py:59
  268.6 5.5 %shard_map.127.facts = f32[40,128]{1,0:T(8,128)} custom-call(f32[1,320]{1,0:T(1,128)} %get-tuple-element.110.dtv, bf16[4,1280,320]{2,1,0:T(8,128)(2,1)} %get-tuple-element.111.tw2, bf16[1280,320]{1,0:T(8,128)(2,1)} %get-tuple-element.112.tw3, f32[8,1280]{1,0:T(8,128)} %get-tuple-element.113.p1, f32[8,1280]{1,0:T(8,128)} %get-tuple-element.114.p2, ...), custom_call_target="tpu_custom_call" | custom-call | tf_op jit(solution)/shard_map/pallas_call | solution.py:59
  274.0 2.0 copy-done
  276.0 0.7 copy-done.5
  276.8 46.3 %shard_map.128 = (f32[856,128]{1,0:T(8,128)S(1)}, f32[856,128]{1,0:T(8,128)S(1)}, f32[16,40,128]{2,1,0:T(8,128)S(1)}) custom-call(bf16[2,8,864,128]{3,2,1,0:T(8,128)(2,1)S(1)} %copy-done, bf16[2,8,240,128]{3,2,1,0:T(8,128)(2,1)S(1)} %copy-done.1, f32[40,128]{1,0:T(8,128)S(1)} %copy-done.5), custom_call_target="tpu_custom_call" | custom-call | tf_op jit(solution)/shard_map/pallas_call | solution.py:1001
  323.1 0.8 copy-done.2
  323.9 0.8 copy-done.3
  324.7 0.7 copy-done.4
  325.4 10.1 %shard_map.129 = (f32[2,856,128]{2,1,0:T(8,128)}, f32[2,856,128]{2,1,0:T(8,128)}, f32[2,856,128]{2,1,0:T(8,128)}, f32[1,128]{1,0:T(1,128)}) custom-call(f32[2,856,128]{2,1,0:T(8,128)} %bitcast.23, f32[2,856,128]{2,1,0:T(8,128)} %bitcast.24, f32[2,856,128]{2,1,0:T(8,128)} %bitcast.25, f32[856,128]{1,0:T(8,128)} %copy-done.2, f32[856,128]{1,0:T(8,128)} %copy-done.3, ...), custom_call_target="tpu_custom_call" | custom-call | tf_op jit(solution)/shard_map/pallas_call | solution.py:59
  335.5 1.3 fusion.2
  (12 shorter events, 0.2 us)
Async XLA Ops:
  268.5 5.5 %copy-start.1 = (bf16[2,8,240,128]{3,2,1,0:T(8,128)(2,1)S(1)}, bf16[2,8,240,128]{3,2,1,0:T(8,128)(2,1)}, u32[]{:S(2)}) copy-start(bf16[2,8,240,128]{3,2,1,0:T(8,128)(2,1)} %get-tuple-element.109.p0) | copy-start | bytes 2949124
  274.0 2.0 copy-start
  276.0 0.7 copy-start.5
  323.1 0.8 copy-start.2
  323.9 0.8 copy-start.3
  324.7 0.7 copy-start.4

commit v3 on v2

--- a/solution.py
+++ b/solution.py
@@ -54,16 +54,70 @@
 MSO, MCQ, MCO, MPO, MGV, MGG, MGO = 0, 1, 2, 3, 4, 8, 12
 
 
-def kcall(body, outs, ins, scratch=()):
-    vm = pl.BlockSpec(memory_space=pltpu.VMEM)
-    return pl.pallas_call(
-        body,
+class Flow:
+    def __init__(self, ins, outs, sems):
+        self.ins = {i: pltpu.make_async_copy(src, dst, sems.at[j]) for j, (i, src, dst) in enumerate(ins)}
+        n = len(ins)
+        self.outs = {i: pltpu.make_async_copy(src, dst, sems.at[n + j]) for j, (i, dst, src) in enumerate(outs)}
+        self.waiting = set(self.ins)
+        self.going = []
+        for copy in self.ins.values():
+            copy.start()
+
+    def need(self, *which):
+        for i in which:
+            self.ins[i].wait()
+            self.waiting.discard(i)
+
+    def ready(self, *which):
+        for i in which:
+            self.outs[i].start()
+            self.going.append(i)
+
+    def end(self):
+        self.need(*sorted(self.waiting))
+        self.ready(*(i for i in self.outs if i not in self.going))
+        for copy in self.outs.values():
+            copy.wait()
+
+
+def kcall(body, outs, ins, scratch=(), late=(), early=()):
+    vm, hbm = pl.BlockSpec(memory_space=pltpu.VMEM), pl.BlockSpec(memory_space=pl.ANY)
+    single = not isinstance(outs, tuple)
+    outs = (outs,) if single else outs
+    n, m = len(ins), len(outs)
+    late, early = tuple(late), tuple(early)
+    scratch = list(scratch)
+    count = len(scratch)
+    if late or early:
+        scratch += [pltpu.VMEM(ins[i].shape, ins[i].dtype) for i in late]
+        scratch += [pltpu.VMEM(outs[i].shape, outs[i].dtype) for i in early]
+        scratch.append(pltpu.SemaphoreType.DMA((len(late) + len(early),)))
+
+    def whole(*refs):
+        if not (late or early):
+            return body(*refs)
+        given, made, rest = list(refs[:n]), list(refs[n : n + m]), refs[n + m :]
+        kept = rest[count:-1]
+        inward = [(i, given[i], kept[j]) for j, i in enumerate(late)]
+        outward = [(i, made[i], kept[len(late) + j]) for j, i in enumerate(early)]
+        for i, _, ref in inward:
+            given[i] = ref
+        for i, _, ref in outward:
+            made[i] = ref
+        flow = Flow(inward, outward, rest[-1])
+        body(flow, *given, *made, *rest[:count])
+        flow.end()
+
+    done = pl.pallas_call(
+        whole,
         out_shape=outs,
-        in_specs=[vm] * len(ins),
-        out_specs=jax.tree.map(lambda _: vm, outs),
-        scratch_shapes=list(scratch),
+        in_specs=[hbm if i in late else vm for i in range(n)],
+        out_specs=tuple(hbm if i in early else vm for i in range(m)),
+        scratch_shapes=scratch,
         compiler_params=pltpu.CompilerParams(vmem_limit_bytes=63 * 2**20),
     )(*ins)
+    return done[0] if single else done
 
 
 def sds(shape, dtype=F32):
@@ -91,13 +145,16 @@
     return jnp.sum(v, axis=0, keepdims=True)
 
 
-def unroll_rows(a_ref, flat, s_ref, chunks, rows):
-    q = 80
+def flatten(a_ref, flat, rows):
     for b in range(2):
         for t in range(a_ref.shape[1]):
             flat[b, t * rows : (t + 1) * rows, :] = a_ref[b, t, :rows, :].astype(F32)
 
-    @pl.loop(0, chunks)
+
+def unroll(flat, s_ref, lo_chunk, hi_chunk):
+    q = 80
+
+    @pl.loop(lo_chunk, hi_chunk)
     def _(c):
         f = [[flat[b, pl.ds(c * 5 * q + j, q, stride=5), :] for j in range(5)] for b in range(2)]
         for i in range(4):
@@ -136,15 +193,20 @@
     ]
 
 
-def unpack0_kernel(rows, a_ref, e, win, w1, w1b, vec, tw2, tw3, tv, p1, p2, flat, s_ref):
-    unroll_rows(a_ref, flat, s_ref, R1 // 400, rows)
+def take_front(s_ref, win, w1, w1b, vec):
     win[...] = get_rows(s_ref, 0, 36).astype(BF)
     put_taps(s_ref, 39, w1, w1b)
     for i, r in enumerate(VEC0):
         vec[i : i + 1, :] = get_rows(s_ref, r, 1)
+
+
+def take_time(s_ref, tw2, tw3):
     for i in range(4):
         tw2[i] = get_rows(s_ref, U2 + i, 4 * D, 4).astype(BF)
     tw3[...] = get_rows(s_ref, U3, 4 * D).astype(BF)
+
+
+def time_forward(s_ref, e, tw2, tw3, tv, p1, p2):
     u = e[...].astype(BF)
     p1[...] = unit_row(
         [nn(u, get_rows(s_ref, U1 + i, D, 4).astype(BF))[:1] + get_rows(s_ref, U1 + 4 * D + i, 1) for i in range(4)]
@@ -153,6 +215,14 @@
     p2[...] = unit_row([nn(u, tw2[i])[:1] + get_rows(s_ref, U2 + 16 * D + i, 1) for i in range(4)])
     u = silu(p2[...]).astype(BF)
     tv[...] = nn(u, tw3[...])[:1] + get_rows(s_ref, U3 + 4 * D, 1)
+
+
+def unpack0_kernel(rows, a_ref, e, win, w1, w1b, vec, tw2, tw3, tv, p1, p2, flat, s_ref):
+    flatten(a_ref, flat, rows)
+    unroll(flat, s_ref, 0, R1 // 400)
+    take_front(s_ref, win, w1, w1b, vec)
+    take_time(s_ref, tw2, tw3)
+    time_forward(s_ref, e, tw2, tw3, tv, p1, p2)
 
 
 FE, FU1, FU2, FD1, FD2, FD3, FL = 0, 3, 13, 23, 28, 33, 35
@@ -185,7 +255,8 @@
 
 
 def unpack1_kernel(rows, a_ref, c2, c2b, tr, mats, kv, vec, gib, wout, outb, flat, s_ref, o_ref):
-    unroll_rows(a_ref, flat, s_ref, R1 // 400, rows)
+    flatten(a_ref, flat, rows)
+    unroll(flat, s_ref, 0, R1 // 400)
     put_taps(s_ref, C2, c2, c2b)
     tr[MPI] = get_rows(s_ref, PI, D).astype(BF)
     for m, r in ((MSO, SO), (MCQ, CQ), (MCO, CO), (MPO, PO)):
@@ -303,38 +374,66 @@
     return v[:, HD * h : HD * (h + 1)]
 
 
-def front_kernel(noisy, tv, win, w1, vec0, c2, tr, vec1, h0, h1, h2, z0, a1, a2, ntr, x1, q, k, v, stats, sh, acc):
-    cols = jnp.concatenate([shift_lanes(noisy[...], t) for t in range(9)], axis=0).astype(BF)
+def group_norm(src, acc, total, stats, at):
+    mean, inv = group_stats(src, acc, total)
+    stats[at : at + 1, :], stats[at + 1 : at + 2, :] = mean, inv
+    return (src[...] - mean) * inv
+
+
+def start_steps(noisy, tv, win, w1, vec0, h0, h1, a1, stats, sh, acc):
+    def first():
+        cols = jnp.concatenate([shift_lanes(noisy[...], t) for t in range(9)], axis=0).astype(BF)
+        clear_margins(sh)
+        stats[...] = jnp.zeros_like(stats)
+        h = tn(cols, win[...]) + vec0[0:1, :]
+        h0[...] = h
+        y = silu(group_norm(h0, acc, colsum(h), stats, 0) * vec0[1:2, :] + vec0[2:3, :])
+        put_shifts(sh, y)
+        a1[...] = y.astype(BF)
+
+    def taps(r):
+        def one():
+            part = nn(sh[SIDE * r : SIDE * r + N, :], w1[r])
+            h1[...] = (h1[...] if r else vec0[3:4, :] + tv[...]) + part
+
+        return one
+
+    return [first, taps(0), taps(1), taps(2)]
+
+
+def start_kernel(noisy, tv, win, w1, vec0, h0, h1, a1, stats, sh, acc):
+    for step in start_steps(noisy, tv, win, w1, vec0, h0, h1, a1, stats, sh, acc):
+        step()
+
+
+def front_kernel(flow, h0, h1, stats_in, c2, tr, vec1, h2, z0, a2, ntr, x1, q, k, v, stats, sh, acc):
     clear_margins(sh)
-
-    def norm(src, total, at):
-        mean, inv = group_stats(src, acc, total)
-        stats[at : at + 1, :], stats[at + 1 : at + 2, :] = mean, inv
-        return (src[...] - mean) * inv
-
-    h = tn(cols, win[...]) + vec0[0:1, :]
-    h0[...] = h
-    y = silu(norm(h0, colsum(h), 0) * vec0[1:2, :] + vec0[2:3, :])
-    put_shifts(sh, y)
-    a1[...] = y.astype(BF)
-    h = conv_rows(sh, w1) + (vec0[3:4, :] + tv[...])
-    h1[...] = h
-    y = silu(norm(h1, colsum(h), 2) * vec1[N2G : N2G + 1, :] + vec1[N2B : N2B + 1, :])
+    stats[...] = stats_in[...]
+    y = silu(group_norm(h1, acc, colsum(h1[...]), stats, 2) * vec1[N2G : N2G + 1, :] + vec1[N2B : N2B + 1, :])
     put_shifts(sh, y)
     a2[...] = y.astype(BF)
+    flow.ready(2)
+    flow.need(0, 3)
     h = h0[...] + conv_rows(sh, c2) + vec1[C2B : C2B + 1, :]
     h2[...] = h
-    n = (norm(h2, colsum(h), 4) * vec1[NTG : NTG + 1, :] + vec1[NTB : NTB + 1, :]).astype(BF)
+    flow.ready(0)
+    n = group_norm(h2, acc, colsum(h), stats, 4)
+    n = (n * vec1[NTG : NTG + 1, :] + vec1[NTB : NTB + 1, :]).astype(BF)
     ntr[...] = n
+    flow.ready(3)
+    flow.need(4)
     z = nn(n, tr[MPI]) + vec1[PIB : PIB + 1, :]
     z0[...] = z
+    flow.ready(1)
     normed, _ = layer(z)
     x = (normed * vec1[L1G : L1G + 1, :] + vec1[L1B : L1B + 1, :]).astype(BF)
     x1[...] = x
-    for at, dst in ((MQ, q), (MK, k), (MV, v)):
+    flow.ready(4)
+    for i, (at, dst) in enumerate(((MQ, q), (MK, k), (MV, v))):
         y = nn(x, tr[at]).astype(BF)
         for hd in range(HEADS):
             dst[hd] = head(y, hd)
+        flow.ready(5 + i)
 
 
 AT = 512
@@ -361,10 +460,21 @@
     o[...] = ot[...].T.astype(BF)
 
 
-def cross_head(qh, kh):
-    s = nt(kh, qh) * (SCALE * LOG2E)
-    e = jnp.exp2(s - jnp.max(s, axis=0, keepdims=True))
-    return e * (1.0 / jnp.sum(e, axis=0, keepdims=True))
+KEYS = 128
+
+
+def by_head(v):
+    wide = jnp.concatenate([v, jnp.zeros((KEYS - TXT, D), v.dtype)], axis=0)
+    col = lax.broadcasted_iota(jnp.int32, (KEYS, D), 1) // HD
+    return jnp.concatenate([jnp.where(col == h, wide, 0.0) for h in range(HEADS)], axis=0)
+
+
+def from_heads(vt):
+    row = lax.broadcasted_iota(jnp.int32, (D, KEYS), 0) // HD
+    total = jnp.zeros((D, KEYS), F32)
+    for h in range(HEADS):
+        total += jnp.where(row == h, vt[:, KEYS * h : KEYS * (h + 1)], 0.0)
+    return total.T[:TXT]
 
 
 def transposed(v):
@@ -372,9 +482,9 @@
 
 
 def middle_kernel(
-    o, z0, h2, ctx, noise, mask, mats, kvw, vec, gib, wout, outb,
+    flow, o, z0, h2, ctx, noise, mask, mats, kvw, vec, gib, wout, outb,
     dz1, dh3, dos, loss, gd, ggi, ggo, gkv, dvec, dgib, dwout, dbout,
-    z1, z2, h3, x2, x3, oc, z3b, gl, a3, qc, kc, vc, derr, acc, ot, pt,
+    z1, z2, h3, x2, x3, oc, z3b, gl, by_a, by_g, a3, qc, kb, vb, prob, dsc, acc, pt,
 ):
     def row(i):
         return vec[i : i + 1, :]
@@ -382,24 +492,25 @@
     def put(i, v):
         dvec[i : i + 1, :] = v
 
-    kk = nn(ctx[...], kvw[0]).astype(BF)
-    vv = nn(ctx[...], kvw[1])
-    for h in range(HEADS):
-        kc[h] = head(kk, h)
-        vc[h] = head(vv, h).astype(BF)
-    vt = vv.T
+    flow.need(7)
+    kb[...] = by_head(nn(ctx[...], kvw[0])).astype(BF)
+    vb[...] = by_head(nn(ctx[...], kvw[1])).astype(BF)
+    flow.need(6, 1)
     z = z0[...] + nn(o[...], mats[MSO]) + row(SOB)
     z1[...] = z
     normed, _ = layer(z)
     x = (normed * row(L2G) + row(L2B)).astype(BF)
     x2[...] = x
     qq = nn(x, mats[MCQ]).astype(BF)
+    qc[...] = qq
+    s = nt(qq, kb[...]) * (SCALE * LOG2E)
+    there = lax.broadcasted_iota(jnp.int32, (1, KEYS), 1) < TXT
     for h in range(HEADS):
-        qh = head(qq, h)
-        qc[h] = qh
-        p = cross_head(qh, kc[h]).astype(BF)
-        ot[HD * h : HD * (h + 1), :] = nn(vt[HD * h : HD * (h + 1), :].astype(BF), p)
-    c = ot[...].T.astype(BF)
+        at = slice(KEYS * h, KEYS * (h + 1))
+        sh = jnp.where(there, s[:, at], -jnp.inf)
+        e = jnp.exp2(sh - jnp.max(sh, axis=1, keepdims=True))
+        prob[:, at] = e * (1.0 / jnp.sum(e, axis=1, keepdims=True))
+    c = nn(prob[...].astype(BF), vb[...]).astype(BF)
     oc[...] = c
     z = z1[...] + nn(c, mats[MCO]) + row(COB)
     z2[...] = z
@@ -409,11 +520,16 @@
     for j in range(4):
         a = nn(x, mats[MGV + j]) + gib[j : j + 1, :]
         g = nn(x, mats[MGG + j]) + gib[4 + j : 5 + j, :]
-        y = (a * (0.5 * g * (1.0 + lax.erf(g * math.sqrt(0.5))))).astype(BF)
+        cdf = 0.5 * (1.0 + lax.erf(g * math.sqrt(0.5)))
+        gelu = g * cdf
+        by_a[j] = gelu
+        by_g[j] = a * (cdf + g * jnp.exp(-0.5 * g * g) * (1.0 / math.sqrt(2.0 * math.pi)))
+        y = (a * gelu).astype(BF)
         gl[j] = y
         z = z + nn(y, mats[MGO + j])
     zb = (z + row(GOB)).astype(BF)
     z3b[...] = zb
+    flow.need(2)
     h = h2[...] + nn(zb, mats[MPO]) + row(POB)
     h3[...] = h
     mean, inv = group_stats(h3, acc, colsum(h))
@@ -444,28 +560,26 @@
     put(NOB, dbias)
     g = inv * (g * gain - group_mean(gain * dbias) - n * group_mean(gain * dgain))
     dh3[...] = g
+    flow.ready(1)
     put(POB, colsum(g))
     gd[0] = nn(transposed(z3b[...]), own(g).astype(BF)).astype(BF)
     dz3 = nt(g.astype(BF), mats[MPO])
     z1b = dz3.astype(BF)
     put(GOB, colsum(dz3))
     mine = own(dz3).astype(BF)
-    x = x3[...]
-    xt = transposed(x)
+    xt = transposed(x3[...])
     dx = jnp.zeros((N, D), F32)
     for j in range(4):
-        a = nn(x, mats[MGV + j]) + gib[j : j + 1, :]
-        g = nn(x, mats[MGG + j]) + gib[4 + j : 5 + j, :]
         dgl = nt(z1b, mats[MGO + j])
         ggo[j] = tn(gl[j], mine).astype(BF)
-        cdf = 0.5 * (1.0 + lax.erf(g * math.sqrt(0.5)))
-        da = dgl * (g * cdf)
-        dg = dgl * a * (cdf + g * jnp.exp(-0.5 * g * g) * (1.0 / math.sqrt(2.0 * math.pi)))
+        da = dgl * by_a[j]
+        dg = dgl * by_g[j]
         dgib[j : j + 1, :] = colsum(da)
         dgib[4 + j : 5 + j, :] = colsum(dg)
         ggi[j] = nn(xt, own(da).astype(BF)).astype(BF)
         ggi[4 + j] = nn(xt, own(dg).astype(BF)).astype(BF)
         dx += nt(da.astype(BF), mats[MGV + j]) + nt(dg.astype(BF), mats[MGG + j])
+    flow.ready(5, 6)
     normed, li = layer(z2[...])
     put(L3G, colsum(dx * normed))
     put(L3B, colsum(dx))
@@ -474,18 +588,17 @@
     put(COB, colsum(dz))
     gd[1] = tn(oc[...], own(dz).astype(BF)).astype(BF)
     do = nt(dz.astype(BF), mats[MCO]).astype(BF)
-    dks, dvs = [], []
+    dp = nt(do, vb[...])
+    dot = transposed(do)
+    qt = transposed(qc[...])
+    gkv[1] = tn(ctx[...], own(from_heads(nn(dot, prob[...].astype(BF)))).astype(BF)).astype(BF)
     for h in range(HEADS):
-        qh, kh, vh, doh = qc[h], kc[h], vc[h], head(do, h)
-        p = cross_head(qh, kh)
-        dp = nt(vh, doh)
-        ds = (p * (dp - jnp.sum(p * dp, axis=0, keepdims=True)) * SCALE).astype(BF)
-        dks.append(nn(ds, qh))
-        dvs.append(nn(p.astype(BF), doh))
-        ot[HD * h : HD * (h + 1), :] = tn(kh, ds)
-    for j, g in enumerate((dks, dvs)):
-        gkv[j] = tn(ctx[...], own(jnp.concatenate(g, axis=1)).astype(BF)).astype(BF)
-    dq = ot[...].T
+        at = slice(KEYS * h, KEYS * (h + 1))
+        p, d = prob[:, at], dp[:, at]
+        dsc[:, at] = (p * (d - jnp.sum(p * d, axis=1, keepdims=True)) * SCALE).astype(BF)
+    gkv[0] = tn(ctx[...], own(from_heads(nn(qt, dsc[...]))).astype(BF)).astype(BF)
+    flow.ready(7)
+    dq = nn(dsc[...], kb[...])
     gd[2] = tn(x2[...], own(dq).astype(BF)).astype(BF)
     dx = nt(dq.astype(BF), mats[MCQ])
     normed, li = layer(z1[...])
@@ -493,6 +606,7 @@
     put(L2B, colsum(dx))
     dz = z2[...] + layer_back(dx, normed, li, row(L2G))
     dz1[...] = dz
+    flow.ready(0)
     put(SOB, colsum(dz))
     gd[3] = tn(o[...], own(dz).astype(BF)).astype(BF)
     do = nt(dz.astype(BF), mats[MSO]).astype(BF)
@@ -588,7 +702,7 @@
 
 
 def back_kernel(
-    dq, dk, dv, dz1, dh3, z0, h2, h1, h0, stats, w1, c2, tr, vec0, vec1, a1, a2, ntr, x1, noisy,
+    flow, dq, dk, dv, dz1, dh3, z0, h2, h1, h0, stats, w1, c2, tr, vec0, vec1, a1, a2, ntr, x1, noisy,
     gd, ggi, ggo, gkv, dvec_in, dgib, dwout, dbout,
     out1, out0, dtv,
     dh, g_ref, go_ref, dvec, s_ref, flat, o_ref,
@@ -608,11 +722,13 @@
     xt = transposed(x1[...])
     for j, g in enumerate((dq, dk, dv)):
         put_rows(s_ref, QKV + j, nn(xt, own(g[...].astype(F32)).astype(BF)), 3)
+    flow.need(5, 3)
     normed, li = layer(z0[...])
     put(L1G, colsum(dx * normed))
     put(L1B, colsum(dx))
     dz = dz1[...] + layer_back(dx, normed, li, row(L1G))
     put(PIB, colsum(dz))
+    flow.need(17)
     put_rows(s_ref, PI, tn(ntr[...], own(dz).astype(BF)))
     g = nt(dz.astype(BF), tr[MPI])
 
@@ -624,6 +740,7 @@
     def normed_of(src, at):
         return (src[...] - stats[at : at + 1, :]) * stats[at + 1 : at + 2, :]
 
+    flow.need(6, 4)
     g, dgain, dbias = norm_back(g, normed_of(h2, 4), 4, row(NTG))
     put(NTG, dgain)
     put(NTB, dbias)
@@ -632,7 +749,9 @@
     put(C2B, colsum(g))
     put_shifts(g_ref, g)
     put_shifts(go_ref, own(g))
+    flow.need(16)
     conv_grads(a2, go_ref, s_ref, C2)
+    flow.need(7, 11)
     n = normed_of(h1, 2)
     g = conv_back_rows(g_ref, c2) * silu_slope(n * row(N2G) + row(N2B))
     g, dgain, dbias = norm_back(g, n, 2, row(N2G))
@@ -643,6 +762,7 @@
     put_shifts(g_ref, g)
     put_shifts(go_ref, own(g))
 
+    flow.need(20, 21, 22, 23)
     for i, r in enumerate((PO, CO, CQ, SO)):
         put_rows(s_ref, r, gd[i].astype(F32))
     for j in range(8):
@@ -673,7 +793,9 @@
     put_rows(s_ref, OUTB, jnp.where(at == 0, b0, jnp.where(at == 1, b1, 0.0)))
     s_ref[:, OUTB + 1 :, :] = jnp.zeros((2, 4 * R1 // 5 - OUTB - 1, 128), F32)
     by_owner(s_ref, flat, out1, R1)
-
+    flow.ready(0)
+
+    flow.need(15, 8, 10)
     conv_grads(a1, go_ref, s_ref, 39)
     n = normed_of(h0, 0)
     g = conv_back_rows(g_ref, w1) * silu_slope(n * vec0[1:2, :] + vec0[2:3, :])
@@ -770,7 +892,11 @@
 PIECES = tuple(slice(16 * a, 16 * b) for a, b in ((0, 7), (7, 14), (14, 21), (21, 28), (28, 35), (35, 42), (42, 48), (48, 54)))
 
 
-def gather_kernel(params, g0, g1, low, send_sem, recv_sem, keep_sem):
+def gather_kernel(
+    params, e, noisy, g0, g1, vec, p1, p2, stats, w1b_out, tw2_out, tw3_out, h0_out, h1_out, a1_out,
+    low, slabs, flat, s_ref, w1b, tw2, tw3, h0, h1, a1, w1, win, tv, sh, acc,
+    send_sem, recv_sem, keep_sem, slab_sem, out_sem,
+):
     low[:, :ROWS, :] = params[...].astype(BF)
     low[:, ROWS:, :] = jnp.zeros((2, SLAB - ROWS, 128), BF)
     me, y = lax.axis_index(DP), lax.axis_index(CH)
@@ -844,6 +970,55 @@
         arrive(third[i])
         last.extend(push(g.at[:, :, 1 - x, k, rows] if turn else g.at[1 - y, :, :, k, rows], core))
 
+    outs = [
+        pltpu.make_async_copy(src, dst, out_sem.at[i])
+        for i, (src, dst) in enumerate(
+            ((w1b, w1b_out), (tw2, tw2_out), (tw3, tw3_out), (h0, h0_out), (h1, h1_out), (a1, a1_out))
+        )
+    ]
+    fetches = [
+        pltpu.make_async_copy(g0.at[a, b], slabs.at[a, b], slab_sem.at[4 * a + b]) for a in range(2) for b in range(4)
+    ]
+
+    def fetch():
+        arrive(last)
+        last.clear()
+        for copy in fetches:
+            copy.start()
+
+    def flat_half(a):
+        for copy in fetches[4 * a : 4 * a + 4]:
+            copy.wait()
+        for t in range(16):
+            flat[a, t * ROWS : (t + 1) * ROWS, :] = slabs[a, t // 4, t // 2 % 2, t % 2, :ROWS, :].astype(F32)
+
+    def front():
+        take_front(s_ref, win, w1, w1b, vec)
+        outs[0].start()
+
+    def times():
+        take_time(s_ref, tw2, tw3)
+        outs[1].start()
+        outs[2].start()
+
+    def both(*steps):
+        def one():
+            for step in steps:
+                step()
+
+        return one
+
+    opening, *rows_of_taps = start_steps(noisy, tv, win, w1, vec, h0, h1, a1, stats, sh, acc)
+    todo = [
+        fetch,
+        both(lambda: flat_half(0), lambda: flat_half(1)),
+        lambda: unroll(flat, s_ref, 0, 17),
+        lambda: unroll(flat, s_ref, 17, R1 // 400),
+        both(front, times),
+        both(lambda: time_forward(s_ref, e, tw2, tw3, tv, p1, p2), opening),
+        both(outs[3].start, outs[5].start, *rows_of_taps[:2]),
+        both(rows_of_taps[2], outs[4].start),
+    ]
     ahead = 4
     for i in range(ahead):
         begin(i)
@@ -856,24 +1031,49 @@
             finish(i - 1)
         if 0 <= i - 3 < len(work):
             pass_on(i - 3)
+        if i - 3 >= len(PIECES) - 1:
+            todo.pop(0)()
     pass_on(len(work) - 1)
+    for step in todo:
+        step()
+    for copy in outs:
+        copy.wait()
     arrive(last)
     for copy in started:
         copy.wait_send()
 
 
-def gather_weights(params):
-    hbm = pl.BlockSpec(memory_space=pl.ANY)
-    whole = sds((2, 4, 2, 2, SLAB, 128), BF)
+def gather_weights(params, e, noisy):
+    hbm, vm = pl.BlockSpec(memory_space=pl.ANY), pl.BlockSpec(memory_space=pltpu.VMEM)
+    gathered = sds((2, 4, 2, 2, SLAB, 128), BF)
+    large = (sds((3, D, 3 * D), BF), sds((4, 4 * D, D), BF), sds((4 * D, D), BF))
+    large += (sds((N, D)), sds((N, D)), sds((N, D), BF))
+    small = (sds((8, D)), sds((8, 4 * D)), sds((8, 4 * D)), sds((8, D)))
     dma = pltpu.SemaphoreType.DMA
     return pl.pallas_call(
         gather_kernel,
-        out_shape=(whole, whole),
-        in_specs=[pl.BlockSpec(memory_space=pltpu.VMEM)],
-        out_specs=(hbm, hbm),
-        scratch_shapes=[pltpu.VMEM((2, SLAB, 128), BF), dma((128,)), dma((128,)), dma((2,))],
-        compiler_params=pltpu.CompilerParams(collective_id=2, has_side_effects=True),
-    )(params)
+        out_shape=(gathered, gathered) + small + large,
+        in_specs=[vm, vm, vm],
+        out_specs=(hbm, hbm) + (vm,) * len(small) + (hbm,) * len(large),
+        scratch_shapes=[
+            pltpu.VMEM((2, SLAB, 128), BF),
+            pltpu.VMEM(gathered.shape, BF),
+            pltpu.VMEM((2, 16 * ROWS, 128), F32),
+            pltpu.VMEM((3, 4 * R1 // 5, 128), F32),
+            *(pltpu.VMEM(v.shape, v.dtype) for v in large),
+            pltpu.VMEM((3, 3 * D, D), BF),
+            pltpu.VMEM((36, D), BF),
+            pltpu.VMEM((1, D), F32),
+            pltpu.VMEM((N + 2 * SIDE, 3 * D), BF),
+            pltpu.VMEM((8, D), F32),
+            dma((128,)),
+            dma((128,)),
+            dma((2,)),
+            dma((8,)),
+            dma((6,)),
+        ],
+        compiler_params=pltpu.CompilerParams(collective_id=2, has_side_effects=True, vmem_limit_bytes=63 * 2**20),
+    )(params, e, noisy)
 
 
 def add_up(*terms):
@@ -885,7 +1085,7 @@
 
 def reduce_kernel(
     p1, p0, facts, sum1, sum0, all_facts,
-    r1, sa, rx, ta, rz, r1b, sb, rbz, tb, rbx, some, land, fx, send_sem, recv_sem, fsend, frecv, gsend, grecv,
+    r1, sa, rx, ta, rz, r1b, sb, rbz, tb, rbx, some, land, fx, timed, send_sem, recv_sem, fsend, frecv, gsend, grecv,
 ):
     me = lax.axis_index(DP)
     k, x, z = me % 2, (me // 2) % 2, me // 4
@@ -935,8 +1135,12 @@
             copy.wait_recv()
         return add_up(ta[i, z], rz[i, 0], rz[i, 1], rz[i, 2])
 
+    fx[me] = facts[...]
+    for copy in fact_copies:
+        copy.wait_recv()
+    all_facts[...] = fx[...]
+    timed[...] = time_rows(fx, ROWS)
     some[...] = done(0)
-    fx[me] = facts[...]
 
     @pl.when(me > 0)
     def _():
@@ -950,9 +1154,6 @@
                 send_sem=gsend, recv_sem=grecv, device_id={DP: owner}, device_id_type=pl.DeviceIdType.MESH,
             ).start()
 
-    for copy in fact_copies:
-        copy.wait_recv()
-    all_facts[...] = fx[...]
     for i in range(3):
         sum1[SOME * i : SOME * (i + 1), :] = done(i + 1)
     over_x_b.wait_recv()
@@ -964,12 +1165,12 @@
             src_ref=part, dst_ref=part, send_sem=gsend, recv_sem=grecv,
             device_id={DP: me}, device_id_type=pl.DeviceIdType.MESH,
         ).wait_recv()
-        sum0[lo:hi, :] = land[lo:hi, :]
+        sum0[lo:hi, :] = land[lo:hi, :] + timed[lo:hi, :]
 
     @pl.when(me == 0)
     def _():
         landed(SOME, ROWS)
-        sum0[:SOME, :] = some[...]
+        sum0[:SOME, :] = some[...] + timed[:SOME, :]
 
     @pl.when((me > 0) & (me < 4))
     def _():
@@ -978,11 +1179,11 @@
     @pl.when(me == 4)
     def _():
         landed(0, 16 * SOME - 4 * ROWS)
-        sum0[16 * SOME - 4 * ROWS :, :] = jnp.zeros((5 * ROWS - 16 * SOME, 128), F32)
+        sum0[16 * SOME - 4 * ROWS :, :] = timed[16 * SOME - 4 * ROWS :, :]
 
     @pl.when(me > 4)
     def _():
-        sum0[...] = jnp.zeros_like(sum0)
+        sum0[...] = timed[...]
 
     @pl.when(me > 0)
     def _():
@@ -1017,6 +1218,7 @@
             pltpu.VMEM((SOME, 128), F32),
             pltpu.VMEM((ROWS, 128), F32),
             pltpu.VMEM((16, FACTS, 128), F32),
+            pltpu.VMEM((ROWS, 128), F32),
             dma((25,)),
             dma((25,)),
             dma((15,)),
@@ -1053,32 +1255,39 @@
     rows_dev = params.shape[2]
     rows_all = rows_dev * n_dp
     quick = n_dp == 16 and rows_dev == ROWS
+    e = jnp.broadcast_to(time_features(timesteps), (8, D))
+    alpha = alpha_bar(timesteps)[:, None]
+    noise = noise_eps[0]
+    noisy = jnp.sqrt(alpha) * latents[0] + jnp.sqrt(1.0 - alpha) * noise
+
     if quick:
-        part0, part1 = gather_weights(params[0])
-        part0, part1 = part0.reshape(2, 16, SLAB, 128), part1.reshape(2, 16, SLAB, 128)
+        _, part1, vec0, p1, p2, stats, w1b, tw2, tw3, h0, h1, a1 = gather_weights(params[0], e, noisy)
+        part1 = part1.reshape(2, 16, SLAB, 128)
     else:
         low = params[0].astype(BF)
         part0, part1 = (lax.all_gather(lax.all_gather(low[i], CH, axis=0), DP, axis=1) for i in range(2))
-
-    alpha = alpha_bar(timesteps)[:, None]
-    noise = noise_eps[0]
-    noisy = jnp.sqrt(alpha) * latents[0] + jnp.sqrt(1.0 - alpha) * noise
 
     px = (N, D)
     hx = (HEADS, N, HD)
     sh = (N + 2 * SIDE, 3 * D)
     taps, back = sds((3, 3 * D, D), BF), sds((3, D, 3 * D), BF)
-    e = time_features(timesteps)
     flat = pltpu.VMEM((2, rows_all, 128), F32)
     unrolled = pltpu.VMEM((3, 4 * R1 // 5, 128), F32)
     units = sds((8, 4 * D))
-    win, w1, w1b, vec0, tw2, tw3, tv, p1, p2 = kcall(
-        partial(unpack0_kernel, rows_dev),
-        (sds((36, D), BF), taps, back, sds((8, D)), sds((4, 4 * D, D), BF), sds((4 * D, D), BF), sds((1, D)))
-        + (units, units),
-        (part0, jnp.broadcast_to(e, (8, D))),
-        (flat, unrolled),
-    )
+    if not quick:
+        win, w1, w1b, vec0, tw2, tw3, tv, p1, p2 = kcall(
+            partial(unpack0_kernel, rows_dev),
+            (sds((36, D), BF), taps, back, sds((8, D)), sds((4, 4 * D, D), BF), sds((4 * D, D), BF), sds((1, D)))
+            + (units, units),
+            (part0, e),
+            (flat, unrolled),
+        )
+        h0, h1, a1, stats = kcall(
+            start_kernel,
+            (sds(px), sds(px), sds(px, BF), sds((8, D))),
+            (noisy, tv, win, w1, vec0),
+            (pltpu.VMEM(sh, BF), pltpu.VMEM((8, D), F32)),
+        )
     c2, c2b, tr, mats, kvw, vec1, gib, wout, outb = kcall(
         partial(unpack1_kernel, rows_dev),
         (taps, back, sds((4, D, D), BF), sds((16, D, D), BF), sds((2, CTX, D), BF))
@@ -1086,11 +1295,13 @@
         (part1,),
         (flat, unrolled, pltpu.VMEM((2, 40, 128), F32)),
     )
-    h0, h1, h2, z0, a1, a2, ntr, x1, q, k, v, stats = kcall(
+    h2, z0, a2, ntr, x1, q, k, v, stats = kcall(
         front_kernel,
-        (sds(px),) * 4 + (sds(px, BF),) * 4 + (sds(hx, BF),) * 3 + (sds((8, D)),),
-        (noisy, tv, win, w1, vec0, c2, tr, vec1),
+        (sds(px),) * 2 + (sds(px, BF),) * 3 + (sds(hx, BF),) * 3 + (sds((8, D)),),
+        (h0, h1, stats, c2, tr, vec1),
         (pltpu.VMEM(sh, BF), pltpu.VMEM((8, D), F32)),
+        late=(0, 3, 4),
+        early=range(8),
     )
     o, lse = kcall(
         attend_kernel, (sds(px, BF), sds((HEADS, 1, N))), (q, k, v), (pltpu.VMEM((D, N), F32),)
@@ -1106,15 +1317,19 @@
         + [pltpu.VMEM(px, BF)] * 4
         + [
             pltpu.VMEM((4, N, D), BF),
+            pltpu.VMEM((4, N, D), F32),
+            pltpu.VMEM((4, N, D), F32),
             pltpu.VMEM(px, BF),
-            pltpu.VMEM(hx, BF),
-            pltpu.VMEM((HEADS, TXT, HD), BF),
-            pltpu.VMEM((HEADS, TXT, HD), BF),
-            pltpu.VMEM((LAT, N), F32),
+            pltpu.VMEM(px, BF),
+            pltpu.VMEM((HEADS * KEYS, D), BF),
+            pltpu.VMEM((HEADS * KEYS, D), BF),
+            pltpu.VMEM((N, HEADS * KEYS), F32),
+            pltpu.VMEM((N, HEADS * KEYS), BF),
             pltpu.VMEM((8, D), F32),
-            pltpu.VMEM((D, N), F32),
             pltpu.VMEM((36, N), F32),
         ],
+        late=(7, 6, 1, 2),
+        early=(0, 1, 2, 4, 5, 6, 7),
     )
     dq, dk, dv = kcall(
         attend_back_kernel,
@@ -1143,9 +1358,11 @@
             pltpu.VMEM((7600, 128), F32),
             pltpu.VMEM((2, 40, 128), F32),
         ),
+        late=(5, 3, 17, 6, 4, 16, 7, 11, 20, 21, 22, 23, 15, 8, 10),
+        early=(0,),
     )
     facts = kcall(
-        time_back_kernel, sds((FACTS, 128)), (dtv, tw2, tw3, p1, p2, jnp.broadcast_to(e, (8, D)), pixel_mask, loss)
+        time_back_kernel, sds((FACTS, 128)), (dtv, tw2, tw3, p1, p2, e, pixel_mask, loss)
     )
     if quick:
         sum1, sum0, all_facts = sum_over_samples(own1, own0, facts)
@@ -1157,7 +1374,7 @@
         all_facts = lax.all_gather(facts, DP, axis=0)
     state = sds((2, rows_dev, 128))
     new_params, new_momentum, new_ema, sums = kcall(
-        partial(update_kernel, True),
+        partial(update_kernel, not quick),
         (state, state, state, sds((1, 128))),
         (params[0], momentum[0], ema_params[0], sum1, sum0, all_facts),
     )

time: 342 us -> 309 us (0.904)
  the two profiles are of different devices: /device:TPU:3 before, /device:TPU:1 now
where the time goes in v3:
time: 309 us; the launch traced here: 306 us
  Pallas kernels  293 us (95%)
  local copies, waits for them, and re-layouts  7.11 us (2%)
    pallas_call x8, Pallas kernels, kcall(): pl.pallas_call(whole, out_shape=outs, in_specs=[hbm if i in late else vm...  163 us
    pallas_call x1, Pallas kernels, gather_weights(): pl.pallas_call(gather_kernel, out_shape=(gathered, gathered) + small + la...  82.9 us
    pallas_call x1, Pallas kernels, sum_over_samples(): pl.pallas_call(reduce_kernel, out_shape=(sds((ROWS, 128)), sds((ROWS, 128...  47.1 us

profile of v3, /device:TPU:1, one launch (start us, length us, event | category | flops | bytes accessed | tf_op | source)
XLA Modules:
  0.0 306.0 jit_solution(13968991366909844737)
XLA Ops:
  1.3 0.1 maximum_reduce_fusion
  1.5 0.3 reduce-window.9
  1.7 0.1 slice.16
  1.8 0.1 slice_reduce_fusion
  2.0 0.1 multiply_bitcast_fusion
  2.0 0.6 select_reduce_fusion
  4.0 0.6 broadcast_in_dim.27.e.refs_5_
  4.6 1.3 bitcast_add_fusion.noisy.refs_19_
  6.0 82.9 %shard_map.119 = (bf16[2,4,2,2,864,128]{5,4,3,2,1,0:T(8,128)(2,1)}, bf16[2,4,2,2,864,128]{5,4,3,2,1,0:T(8,128)(2,1)}, f32[8,320]{1,0:T(8,128)}, f32[8,1280]{1,0:...) custom-call(f32[2,856,128]{2,1,0:T(8,128)} %bitcast.20, ...), custom_call_target="tpu_custom_call" | custom-call | tf_op jit(solution)/shard_map/pallas_call | solution.py:1053
  88.9 15.2 %shard_map.120 = (bf16[3,960,320]{2,1,0:T(8,128)(2,1)}, bf16[3,320,960]{2,1,0:T(8,128)(2,1)}, bf16[4,320,320]{2,1,0:T(8,128)(2,1)}, bf16[16,320,320]{2,1,0:T(8,1...) custom-call(bf16[2,16,864,128]{3,2,1,0:T(8,128)(2,1)} %bitcast.19), custom_call_target="tpu_custom_call" | custom-call | tf_op jit(solution)/shard_map/pallas_call | solution.py:112
  104.1 14.6 %shard_map.121 = (f32[1024,320]{1,0:T(8,128)}, f32[1024,320]{1,0:T(8,128)}, bf16[1024,320]{1,0:T(8,128)(2,1)}, bf16[1024,320]{1,0:T(8,128)(2,1)}, bf16[1024,320]...) custom-call(f32[1024,320]{1,0:T(8,128)} %get-tuple-element.61.refs_0, ...), custom_call_target="tpu_custom_call" | custom-call | tf_op jit(solution)/shard_map/pallas_call | solution.py:112
  118.7 16.3 %shard_map.122 = (bf16[1024,320]{1,0:T(8,128)(2,1)}, f32[8,1,1024]{2,1,0:T(1,128)}) custom-call(bf16[8,1024,40]{2,1,0:T(8,128)(2,1)} %get-tuple-element.68.refs_0_, bf16[8,1024,40]{2,1,0:T(8,128)(2,1)} %get-tuple-element.69.refs_1_, bf16[8,1024,40]{2,1,0:T(8,128)(2,1)} %get-tuple-element.70.refs_2_), custom_call_target="tpu_custom_call" | custom-call | tf_op jit(solution)/shard_map/pallas_call | solution.py:112
  135.0 45.1 %shard_map.123 = (f32[1024,320]{1,0:T(8,128)}, f32[1024,320]{1,0:T(8,128)}, bf16[8,1024,40]{2,1,0:T(8,128)(2,1)}, f32[1,1]{1,0:T(1,128)}, bf16[4,320,160]{2,1,0:...) custom-call(bf16[1024,320]{1,0:T(8,128)(2,1)} %get-tuple-element.71., ...), custom_call_target="tpu_custom_call" | custom-call | tf_op jit(solution)/shard_map/pallas_call | solution.py:112
  180.1 29.7 %shard_map.124 = (bf16[1024,320]{1,0:T(8,128)(2,1)}, bf16[1024,320]{1,0:T(8,128)(2,1)}, bf16[1024,320]{1,0:T(8,128)(2,1)}) custom-call(bf16[8,1024,40]{2,1,0:T(8,128)(2,1)} %get-tuple-element.68.refs_0_, bf16[8,1024,40]{2,1,0:T(8,128)(2,1)} %get-tuple-element.69.refs_1_, bf16[8,1024,40]{2,1,0:T(8,128)(2,1)} %get-tuple-element.70.refs_2_, ...), custom_call_target="tpu_custom_call" | custom-call | tf_op jit(solution)/shard_map/pallas_call | solution.py:112
  209.8 33.2 %shard_map.125 = (bf16[2,8,864,128]{3,2,1,0:T(8,128)(2,1)}, bf16[2,8,240,128]{3,2,1,0:T(8,128)(2,1)}, f32[1,320]{1,0:T(1,128)}) custom-call(bf16[1024,320]{1,0:T(8,128)(2,1)} %get-tuple-element.81.refs_0_, bf16[1024,320]{1,0:T(8,128)(2,1)} %get-tuple-element.82.refs_1_, bf16[1024,320]{1,0:T(8,128)(2,1)} %get-tuple-element.83.refs_2_, ...), custom_call_target="tpu_custom_call" | custom-call | tf_op jit(solution)/shard_map/pallas_call | solution.py:112
  243.0 5.5 %shard_map.126.facts = f32[40,128]{1,0:T(8,128)} custom-call(f32[1,320]{1,0:T(1,128)} %get-tuple-element.104.refs_0_, bf16[4,1280,320]{2,1,0:T(8,128)(2,1)} %get-tuple-element.105.refs_1_, bf16[1280,320]{1,0:T(8,128)(2,1)} %get-tuple-element.106.refs_2_, f32[8,1280]{1,0:T(8,128)} %get-tuple-element.107.refs_3_, f32[8,1280]{1,0:T(8,128)} %get-tuple-element.108.refs_4_, ...), custom_call_target="tpu_custom_call" | custom-call | tf_op jit(solution)/shard_map/pallas_call | solution.py:112
  248.5 2.0 copy-done
  250.5 0.7 copy-done.5
  251.3 47.1 %shard_map.127 = (f32[856,128]{1,0:T(8,128)S(1)}, f32[856,128]{1,0:T(8,128)S(1)}, f32[16,40,128]{2,1,0:T(8,128)S(1)}) custom-call(bf16[2,8,864,128]{3,2,1,0:T(8,128)(2,1)S(1)} %copy-done, bf16[2,8,240,128]{3,2,1,0:T(8,128)(2,1)S(1)} %copy-done.1, f32[40,128]{1,0:T(8,128)S(1)} %copy-done.5), custom_call_target="tpu_custom_call" | custom-call | tf_op jit(solution)/shard_map/pallas_call | solution.py:1202
  298.4 0.7 copy-done.2
  299.1 0.8 copy-done.3
  299.9 0.7 copy-done.4
  300.6 3.8 %shard_map.128 = (f32[2,856,128]{2,1,0:T(8,128)}, f32[2,856,128]{2,1,0:T(8,128)}, f32[2,856,128]{2,1,0:T(8,128)}, f32[1,128]{1,0:T(1,128)}) custom-call(f32[2,856,128]{2,1,0:T(8,128)} %bitcast.21, f32[2,856,128]{2,1,0:T(8,128)} %bitcast.22, f32[2,856,128]{2,1,0:T(8,128)} %bitcast.23, f32[856,128]{1,0:T(8,128)} %copy-done.2, f32[856,128]{1,0:T(8,128)} %copy-done.3, ...), custom_call_target="tpu_custom_call" | custom-call | tf_op jit(solution)/shard_map/pallas_call | solution.py:112
  304.5 1.3 fusion.2
  (11 shorter events, 0.1 us)
Async XLA Ops:
  243.0 5.5 %copy-start.1 = (bf16[2,8,240,128]{3,2,1,0:T(8,128)(2,1)S(1)}, bf16[2,8,240,128]{3,2,1,0:T(8,128)(2,1)}, u32[]{:S(2)}) copy-start(bf16[2,8,240,128]{3,2,1,0:T(8,128)(2,1)} %get-tuple-element.103.p0) | copy-start | bytes 2949124
  248.5 2.0 copy-start
  250.5 0.7 copy-start.5
  298.4 0.8 copy-start.2
  299.1 0.8 copy-start.3
  299.9 0.7 copy-start.4
